TPU v7x, 512 devices: a whole 4x4x16 slice. The times are simulated.
512 devices in a mesh: row: 32 (over x_lo, z), col: 16 (over x_hi, y, core).
Axes of the slice: x: 4 (x_hi: 2, x_lo: 2; x = x_hi * 2 + x_lo), y: 4, z: 16, core: 2. Of those that a mesh axis runs over, the one named last changes fastest.
Arguments:
- features: bfloat16 [16, 8192, 128], P('col', 'row'), may hold values from -6 to 6
- tile_rows: int32 [32, 16, 32], P('row', 'col'), may hold values from 0 to 31, as said below
- tile_cols: int32 [32, 16, 32], P('row', 'col'), may hold values from 0 to 63
- tile_count: int32 [32, 16], P('row', 'col'), may hold values from 1 to 32, as said below
- tile_values: bfloat16 [32, 16, 32, 128, 128], P('row', 'col'), may hold values from -0.125 to 0.125
- weight: bfloat16 [128, 128], replicated, may hold values from -0.5 to 0.5
- exit_weight: bfloat16 [128, 172], replicated, may hold values from -0.5 to 0.5
- exit_bias: float32 [172], replicated, may hold values from -8 to 8
- labels: int32 [32, 4096], P('row', 'col'), may hold values from 0 to 171
- label_mask: int32 [32, 4096], P('row', 'col'), may hold values 0 or 1
- upstream: bfloat16 [32, 4096, 128], P('row', 'col'), may hold values from -4 to 4
Outputs:
- grad_input: bfloat16 [16, 8192, 128], P('col', 'row')
- grad_weight: float32 [128, 128], replicated
- grad_exit_weight: float32 [128, 172], replicated
- grad_exit_bias: float32 [172], replicated
Inputs may be any that keep to these rules, and one draw needn't show every extreme that they name: tile_rows[r, c, s] * 64 + tile_cols[r, c, s] are distinct over the slots s of one device. `tile_count`: some device has all 32 slots nonempty.
All inputs are finite; a program needn't handle non-finite values. No bound on the sum of `label_mask` on one device may be relied on, other than what follows from the above.
Results may differ from a plain program's by a relative error of at most 0.023.
Values may be sent and summed in bfloat16 or wider, within the bound.
No kernel may reach another device: no remote copies, remote signals or barrier semaphores. Data moves between devices by JAX's collectives and lax.ppermute only.
A program may use at most 64 MiB of HBM per device.

v0:
```python
import jax
import jax.numpy as jnp
from jax import lax
from jax.sharding import PartitionSpec as P


def tile_products(values, rows_index, cols_index, count, source, out_count, flipped):
    take_index = rows_index if flipped else cols_index
    put_index = cols_index if flipped else rows_index
    slots = values.shape[0]
    operands = jnp.take(source, take_index, axis=0)
    form = "mkt,mkh->mth" if flipped else "mtk,mkh->mth"
    products = jnp.einsum(form, values, operands, preferred_element_type=jnp.float32)
    targets = jnp.where(jnp.arange(slots) < count, put_index, out_count)
    total = jax.ops.segment_sum(products, targets, num_segments=out_count + 1)
    return total[:out_count]


def local(
    features,
    tile_rows,
    tile_cols,
    tile_count,
    tile_values,
    weight,
    exit_weight,
    exit_bias,
    labels,
    label_mask,
    upstream,
):
    tile = tile_values.shape[-1]
    hidden = features.shape[-1]
    classes = exit_weight.shape[1]
    node_here = features.shape[1]
    row_devices = lax.axis_size("row")
    col_devices = lax.axis_size("col")
    row_tiles = node_here * col_devices // tile
    col_tiles = node_here * row_devices // tile
    nodes_total = node_here * row_devices * col_devices
    values = tile_values[0, 0]
    rows_index = tile_rows[0, 0]
    cols_index = tile_cols[0, 0]
    count = tile_count[0, 0]
    gathered = lax.all_gather(features, "row", axis=1, tiled=True)
    col_blocks = gathered.reshape(col_tiles, tile, hidden)
    partial_value = tile_products(
        values, rows_index, cols_index, count, col_blocks, row_tiles, False
    )
    partial_value = partial_value.astype(jnp.bfloat16).reshape(1, row_tiles * tile, hidden)
    summed = lax.psum_scatter(partial_value, "col", scatter_dimension=1, tiled=True).astype(
        jnp.float32
    )
    aggregated = summed[0].astype(jnp.bfloat16)
    pre = jnp.dot(aggregated, weight, preferred_element_type=jnp.float32)
    activated = jax.nn.silu(pre).astype(jnp.bfloat16)
    logits = jnp.dot(activated, exit_weight, preferred_element_type=jnp.float32) + exit_bias
    expd = jnp.exp(logits)
    probs = expd / jnp.sum(expd, axis=1, keepdims=True)
    onehot = (labels[0][:, None] == jnp.arange(classes)[None, :]).astype(jnp.float32)
    dlogits = (label_mask[0].astype(jnp.float32)[:, None] * (probs - onehot)).astype(jnp.bfloat16)
    dact = upstream[0].astype(jnp.float32) + jnp.dot(
        dlogits, exit_weight.T, preferred_element_type=jnp.float32
    )
    sig = jax.nn.sigmoid(pre)
    dpre = (dact * sig * (1.0 + pre * (1.0 - sig))).astype(jnp.bfloat16)
    scale = float(nodes_total) ** (-0.5)
    exit_term = jnp.dot(activated.T, dlogits, preferred_element_type=jnp.float32)
    bias_term = jnp.sum(dlogits.astype(jnp.float32), axis=0)
    layer_term = jnp.dot(aggregated.T, dpre, preferred_element_type=jnp.float32)
    dagg = jnp.dot(dpre, weight.T, preferred_element_type=jnp.float32).astype(jnp.bfloat16)
    grad_rows = lax.all_gather(dagg[None], "col", axis=1, tiled=True)
    row_blocks = grad_rows.reshape(row_tiles, tile, hidden)
    back = tile_products(values, rows_index, cols_index, count, row_blocks, col_tiles, True)
    back = back.astype(jnp.bfloat16).reshape(1, col_tiles * tile, hidden)
    grad_input = (
        lax.psum_scatter(back, "row", scatter_dimension=1, tiled=True)
        .astype(jnp.float32)
        .astype(jnp.bfloat16)
    )
    layer_total, exit_total, bias_total = lax.psum(
        (layer_term, exit_term, bias_term), ("row", "col")
    )
    return (grad_input, layer_total * scale, exit_total * scale, bias_total * scale)


def solution(mesh):
    in_specs = (
        P("col", "row", None),
        P("row", "col", None),
        P("row", "col", None),
        P("row", "col"),
        P("row", "col", None, None, None),
        P(),
        P(),
        P(),
        P("row", "col"),
        P("row", "col"),
        P("row", "col", None),
    )
    out_specs = (P("col", "row", None), P(), P(), P())
    return jax.shard_map(local, mesh=mesh, in_specs=in_specs, out_specs=out_specs, check_vma=False)
```

profile of v0, /device:TPU:8, one launch (start us, length us, event | category | flops | bytes accessed | tf_op | source)
XLA Modules:
  0.0 905.0 jit_solution(11178786422886067488)
XLA Ops:
  7.2 0.7 all-gather.4.cloned.1.call-update
  8.6 0.7 fusion.18
  9.3 0.7 compare_and_fusion
  10.0 138.1 %all-gather.4.cloned.1.call-done = bf16[1,8192,128]{2,1,0:T(8,128)(2,1)} async-done(((bf16[1,256,128]{2,1,0:T(8,128)(2,1)}), bf16[1,8192,128]{2,1,0:T(8,128)(2,1)}) %all-gather.4.cloned.1.call-update) | async-done | bytes 2097168 | tf_op jit(solution)/shard_map/all_gather | solution.py:45
  148.1 3.3 gather_fusion
  151.4 2.2 convolution_bitcast_fusion.1
  153.6 1.9 copy.18
  155.4 0.2 broadcast_in_dim.43
  155.7 4.7 scatter_fusion
  160.4 1.1 slice.19
  161.6 0.0 all-gather.6.cloned.1.call-start
  161.7 83.1 %reduce-scatter.3.cloned.1.call-done = bf16[1,256,128]{2,1,0:T(8,128)(2,1)} async-done(((bf16[1,4096,128]{2,1,0:T(8,128)(2,1)}), bf16[1,256,128]{2,1,0:T(8,128)(2,1)}) %reduce-scatter.3.cloned.1.call-update) | async-done | bytes 65552 | tf_op jit(solution)/shard_map/reduce_scatter | solution.py:51
  244.8 1.0 fusion.14
  245.9 0.2 fusion.23
  246.1 0.1 convert_reduce_fusion
  246.3 0.2 fusion.3
  246.5 0.8 convolution_convert_fusion
  247.4 0.8 fusion.12
  248.3 0.8 fusion.22
  249.2 59.3 %all-gather.6.cloned.1.call-done = bf16[4096,128]{1,0:T(8,128)(2,1)} async-done(((bf16[256,128]{1,0:T(8,128)(2,1)}), bf16[4096,128]{1,0:T(8,128)(2,1)}) %all-gather.6.cloned.1.call-update) | async-done | bytes 1048592 | tf_op jit(solution)/shard_map/all_gather | solution.py:72
  308.5 2.0 gather_fusion.1
  310.5 1.9 convolution_bitcast_fusion
  312.4 1.9 copy.20
  314.3 2.5 broadcast_in_dim.40
  316.8 6.1 scatter_fusion.1
  322.9 3.9 slice.18
  326.8 105.3 %psum.23 = f32[172]{0:T(256)S(1)} all-reduce(f32[172]{0:T(256)S(1)} %get-tuple-element.6), channel_id=1, replica_groups=mesh['row'=32,'col'=16] {'row','col'}, use_global_device_ids=true, to_apply=%region_8.9 | all-reduce | flops 172 | bytes 1376 | tf_op jit(solution)/shard_map/psum | solution.py:81
  432.1 0.6 broadcast_multiply_fusion.2
  432.7 332.9 %all-reduce.3.cloned.1.call-done = (f32[128,128]{1,0:T(8,128)}, f32[128,172]{0,1:T(8,128)}) async-done(((f32[128,128]{1,0:T(8,128)}, f32[128,172]{0,1:T(8,128)}), (f32[128,128]{1,0:T(8,128)}, f32[128,172]{0,1:T(8,128)})) %all-reduce.3.cloned.1.call-update) | async-done | bytes 153616 | tf_op jit(solution)/shard_map/psum | solution.py:81
  765.6 1.5 broadcast_multiply_fusion.1
  767.1 1.5 broadcast_multiply_fusion
  768.6 129.9 %reduce-scatter.5.cloned.1.call-done = bf16[1,256,128]{2,1,0:T(8,128)(2,1)} async-done(((bf16[1,8192,128]{2,1,0:T(8,128)(2,1)}), bf16[1,256,128]{2,1,0:T(8,128)(2,1)}) %reduce-scatter.5.cloned.1.call-update) | async-done | bytes 65552 | tf_op jit(solution)/shard_map/reduce_scatter | solution.py:77
  (30 shorter events, 0.3 us)
Async XLA Ops:
  7.2 144.2 %copy-start = (bf16[1,1,32,128,128]{4,3,2,1,0:T(8,128)(2,1)S(1)}, bf16[1,1,32,128,128]{4,3,2,1,0:T(8,128)(2,1)}, u32[]{:S(2)}) copy-start(bf16[1,1,32,128,128]{4,3,2,1,0:T(8,128)(2,1)} %param.15) | copy-start | bytes 3145732
  7.2 140.9 %all-gather.4.cloned.1.call-start = ((), (), s32[]{:S(2)}) async-start(), calls=%async_computation.2 | async-start | bytes 2162688 | tf_op jit(solution)/shard_map/all_gather | solution.py:45
  7.9 236.9 %reduce-scatter.3.cloned.1.call-start = ((), (), s32[]{:S(2)}) async-start(), calls=%async_computation.3 | async-start | bytes 1114112 | tf_op jit(solution)/shard_map/reduce_scatter | solution.py:51
  160.4 1.3 copy-start.4
  160.4 84.4 %copy-start.2 = (bf16[128,128]{1,0:T(8,128)(2,1)S(1)}, bf16[128,128]{1,0:T(8,128)(2,1)}, u32[]{:S(2)}) copy-start(bf16[128,128]{1,0:T(8,128)(2,1)} %param.16) | copy-start | bytes 98308
  160.4 85.5 %copy-start.7 = (bf16[128,172]{0,1:T(8,128)(2,1)S(1)}, bf16[128,172]{0,1:T(8,128)(2,1)}, u32[]{:S(2)}) copy-start(bf16[128,172]{0,1:T(8,128)(2,1)} %param.17) | copy-start | bytes 132100
  160.4 85.5 %copy-start.8 = (f32[172]{0:T(256)S(1)}, f32[172]{0:T(256)}, u32[]{:S(2)}) copy-start(f32[172]{0:T(256)} %param.18) | copy-start | bytes 2068
  160.4 85.7 %copy-start.3 = (s32[1,256]{1,0:T(1,128)S(1)}, s32[1,256]{1,0:T(1,128)}, u32[]{:S(2)}) copy-start(s32[1,256]{1,0:T(1,128)} %param.19) | copy-start | bytes 3076
  160.4 85.8 %copy-start.6 = (bf16[1,256,128]{2,1,0:T(8,128)(2,1)S(1)}, bf16[1,256,128]{2,1,0:T(8,128)(2,1)}, u32[]{:S(2)}) copy-start(bf16[1,256,128]{2,1,0:T(8,128)(2,1)} %param.21) | copy-start | bytes 196612
  161.6 85.8 %copy-start.5 = (s32[1,1,32]{2,1,0:T(1,128)S(1)}, s32[1,1,32]{2,1,0:T(1,128)}, u32[]{:S(2)}) copy-start(s32[1,1,32]{2,1,0:T(1,128)} %param.12) | copy-start | bytes 388
  161.6 146.9 %all-gather.6.cloned.1.call-start = ((), (), s32[]{:S(2)}) async-start(), calls=%async_computation.5 | async-start | bytes 1114112 | tf_op jit(solution)/shard_map/all_gather | solution.py:72
  244.8 2.6 copy-start.1
  247.3 518.2 %all-reduce.3.cloned.1.call-start = ((), (), s32[]{:S(2)}) async-start(), calls=%async_computation.6 | async-start | bytes 311296 | tf_op jit(solution)/shard_map/psum | solution.py:81
  249.1 649.4 %reduce-scatter.5.cloned.1.call-start = ((), (), s32[]{:S(2)}) async-start(), calls=%async_computation.4 | async-start | bytes 2162688 | tf_op jit(solution)/shard_map/reduce_scatter | solution.py:77
Sparse Core Ops, SparseCore 0:
  10.1 137.9 all-gather.3
  161.7 83.0 reduce-scatter.2
  249.3 59.1 all-gather.5
  315.4 450.1 all-reduce.2
  768.8 129.6 reduce-scatter.4
where the time goes:
time: 906 us; the launch traced here: 905 us
  waiting for transfers between devices  744 us (82%)
  blocking collectives  105 us (12%)
  local copies, waits for them, and re-layouts  16.8 us (2%)
  other arithmetic  15.8 us (2%)
  between operations  14.6 us (2%)
    psum x1, waiting for transfers between devices, local(): lax.psum((layer_term, exit_term, bias_term), ('row', 'col'))  333 us
    all_gather x1, waiting for transfers between devices, local(): gathered = lax.all_gather(features, 'row', axis=1, tiled=True)  138 us
    reduce_scatter x1, waiting for transfers between devices, local(): lax.psum_scatter(back, 'row', scatter_dimension=1, tiled=True)  130 us
    psum x1, blocking collectives, local(): lax.psum((layer_term, exit_term, bias_term), ('row', 'col'))  105 us
    reduce_scatter x1, waiting for transfers between devices, local(): lax.psum_scatter(partial_value, 'col', scatter_dimension=1, tiled=True)  83.1 us
    all_gather x1, waiting for transfers between devices, local(): grad_rows = lax.all_gather(dagg[None], 'col', axis=1, tiled=True)  59.3 us
  transfers between devices with their start and end apart: 5, of which 5 were waited for; matrix products, arithmetic and copies ran while one was open for 3% of the time, Pallas kernels for 0%

commit v1 on v0

v1 whole, which is shorter than its diff:
```python
import functools

import jax
import jax.numpy as jnp
from jax import lax
from jax.experimental import pallas as pl
from jax.experimental.pallas import tpu as pltpu
from jax.sharding import PartitionSpec as P

TILE = 128
Z = 16
NEAR = 4
FAR = 8
WROWS = 32
BIAS_AT = 304

VMEM_LIMIT = 48 * 1024 * 1024


def far_groups():
    return [
        [x * Z + NEAR * q + k for x in range(2) for q in range(Z // NEAR)]
        for k in range(NEAR)
    ]


def shift(d):
    return [(x * Z + z, x * Z + (z + d) % Z) for x in range(2) for z in range(Z)]


def vmem():
    return pl.BlockSpec(memory_space=pltpu.VMEM)


def smem():
    return pl.BlockSpec(memory_space=pltpu.SMEM)


def params():
    return pltpu.CompilerParams(vmem_limit_bytes=VMEM_LIMIT)


def place(col, mine):
    x = col // 32
    q = (col // 8) % 4
    rel = (((col // 2) % 4) - mine + 4) % 4
    return rel * 16 + x * 8 + q * 2 + col % 2


def forward_kernel(rows, cols, count, mine, a, own, nxt, prv, ha, hb, out, xs, acc):
    xs[0:16] = own[...]
    xs[16:32] = nxt[...]
    xs[32:40] = ha[...]
    xs[40:48] = hb[...]
    xs[48:64] = prv[...]
    acc[...] = jnp.zeros_like(acc)
    k = mine[0]
    n = count[0]
    slots = a.shape[0]
    group = 4
    for base in range(0, slots, group):
        prods = []
        for s in range(base, base + group):
            prods.append(
                jnp.dot(a[s], xs[place(cols[s], k)], preferred_element_type=jnp.float32)
            )
        for s, p in zip(range(base, base + group), prods):
            t = jnp.where(s < n, rows[s], out.shape[0])
            acc[t] += p
    out[...] = acc[0 : out.shape[0]].astype(jnp.bfloat16)


def forward_products(rows, cols, count, mine, a, own, nxt, prv, ha, hb, row_tiles):
    return pl.pallas_call(
        forward_kernel,
        out_shape=jax.ShapeDtypeStruct((row_tiles, TILE, TILE), jnp.bfloat16),
        in_specs=[smem()] * 4 + [vmem()] * 6,
        out_specs=vmem(),
        scratch_shapes=[
            pltpu.VMEM((64, TILE, TILE), jnp.bfloat16),
            pltpu.VMEM((row_tiles + 1, TILE, TILE), jnp.float32),
        ],
        compiler_params=params(),
        name="forward_products",
    )(rows, cols, count, mine, a, own, nxt, prv, ha, hb)


def dense_kernel(parts, weight, exit_weight, bias, labels, mask, up, out, wb):
    total = parts[0].astype(jnp.float32)
    for j in range(1, parts.shape[0]):
        total += parts[j].astype(jnp.float32)
    agg = total.astype(jnp.bfloat16)
    w = weight[...]
    ew = exit_weight[...]
    pre = jnp.dot(agg, w, preferred_element_type=jnp.float32)
    sig = 1.0 / (1.0 + jnp.exp(-pre))
    act = (pre * sig).astype(jnp.bfloat16)
    logits = jnp.dot(act, ew, preferred_element_type=jnp.float32) + bias[...]
    expd = jnp.exp(logits)
    probs = expd / jnp.sum(expd, axis=1, keepdims=True)
    ids = lax.broadcasted_iota(jnp.int32, logits.shape, 1)
    onehot = (labels[...] == ids).astype(jnp.float32)
    dlogits = (mask[...].astype(jnp.float32) * (probs - onehot)).astype(jnp.bfloat16)
    nt = (((1,), (1,)), ((), ()))
    tn = (((0,), (0,)), ((), ()))
    dact = up[...].astype(jnp.float32) + lax.dot_general(
        dlogits, ew, nt, preferred_element_type=jnp.float32
    )
    dpre = (dact * sig * (1.0 + pre * (1.0 - sig))).astype(jnp.bfloat16)
    dagg = lax.dot_general(dpre, w, nt, preferred_element_type=jnp.float32).astype(
        jnp.bfloat16
    )
    classes = ew.shape[1]
    wb[...] = jnp.zeros_like(wb)
    wb[0:TILE] = lax.dot_general(agg, dpre, tn, preferred_element_type=jnp.float32)
    wb[TILE : TILE + classes] = lax.dot_general(
        dlogits, act, tn, preferred_element_type=jnp.float32
    )
    bsum = jnp.sum(dlogits.astype(jnp.float32), axis=0, keepdims=True)
    wb[BIAS_AT : BIAS_AT + 1] = bsum[:, 0:TILE]
    wb[BIAS_AT + 1 : BIAS_AT + 2, 0 : classes - TILE] = bsum[:, TILE:]
    nodes = dagg.shape[0]
    for j in range(out.shape[0]):
        out[j, 0:nodes] = dagg
        out[j, nodes : nodes + WROWS] = wb[j * WROWS : (j + 1) * WROWS].astype(jnp.bfloat16)


def dense(parts, weight, exit_weight, bias, labels, mask, up):
    n, nodes, hidden = parts.shape
    return pl.pallas_call(
        dense_kernel,
        out_shape=jax.ShapeDtypeStruct((n, nodes + WROWS, hidden), jnp.bfloat16),
        in_specs=[vmem()] * 7,
        out_specs=vmem(),
        scratch_shapes=[pltpu.VMEM((n * WROWS, hidden), jnp.float32)],
        compiler_params=params(),
        name="dense",
    )(parts, weight, exit_weight, bias, labels, mask, up)


def backward_kernel(rows, cols, count, mine, a, g, own, nxt, prv, ha, hb, w, acc):
    acc[...] = jnp.zeros_like(acc)
    k = mine[0]
    n = count[0]
    slots = a.shape[0]
    group = 4
    tn = (((0,), (0,)), ((), ()))
    for base in range(0, slots, group):
        prods = []
        for s in range(base, base + group):
            t = rows[s]
            start = pl.multiple_of((t % 2) * TILE, TILE)
            gb = g[t // 2, pl.ds(start, TILE), :]
            prods.append(lax.dot_general(a[s], gb, tn, preferred_element_type=jnp.float32))
        for s, p in zip(range(base, base + group), prods):
            c = jnp.where(s < n, place(cols[s], k), 64)
            acc[c] += p
    own[...] = acc[0:16].astype(jnp.bfloat16)
    nxt[...] = acc[16:32].astype(jnp.bfloat16)
    prv[...] = acc[48:64].astype(jnp.bfloat16)
    nodes = 2 * TILE
    ws = g[0, nodes : nodes + WROWS].astype(jnp.float32)
    for j in range(1, g.shape[0]):
        ws += g[j, nodes : nodes + WROWS].astype(jnp.float32)
    ws = ws.astype(jnp.bfloat16)
    for i in range(8):
        ha[i * TILE : (i + 1) * TILE] = acc[32 + i].astype(jnp.bfloat16)
        hb[i * TILE : (i + 1) * TILE] = acc[40 + i].astype(jnp.bfloat16)
    ha[8 * TILE : 8 * TILE + WROWS] = ws
    hb[8 * TILE : 8 * TILE + WROWS] = ws
    w[...] = ws


def backward_products(rows, cols, count, mine, a, g):
    full = jax.ShapeDtypeStruct((16, TILE, TILE), jnp.bfloat16)
    half = jax.ShapeDtypeStruct((8 * TILE + WROWS, TILE), jnp.bfloat16)
    return pl.pallas_call(
        backward_kernel,
        out_shape=(full, full, full, half, half, jax.ShapeDtypeStruct((WROWS, TILE), jnp.bfloat16)),
        in_specs=[smem()] * 4 + [vmem()] * 2,
        out_specs=(vmem(),) * 6,
        scratch_shapes=[pltpu.VMEM((65, TILE, TILE), jnp.float32)],
        compiler_params=params(),
        name="backward_products",
    )(rows, cols, count, mine, a, g)


def add(a, b):
    return (a.astype(jnp.float32) + b.astype(jnp.float32)).astype(jnp.bfloat16)


def fold_kernel(odd, nxt, prv, ra, rb, w, onxt, oprv, ow):
    half = 8 * TILE
    for i in range(8):
        rows = slice(i * TILE, (i + 1) * TILE)
        onxt[i] = add(nxt[i], ra[rows])
        oprv[8 + i] = add(prv[8 + i], rb[rows])
    onxt[8:16] = nxt[8:16]
    oprv[0:8] = prv[0:8]
    other = jnp.where(
        odd[0] == 1,
        ra[half : half + WROWS].astype(jnp.float32),
        rb[half : half + WROWS].astype(jnp.float32),
    )
    ow[...] = w[...].astype(jnp.float32) + other


def fold(odd, nxt, prv, ra, rb, w):
    full = jax.ShapeDtypeStruct((16, TILE, TILE), jnp.bfloat16)
    return pl.pallas_call(
        fold_kernel,
        out_shape=(full, full, jax.ShapeDtypeStruct((WROWS, TILE), jnp.float32)),
        in_specs=[smem()] + [vmem()] * 5,
        out_specs=(vmem(),) * 3,
        compiler_params=params(),
        name="fold",
    )(odd, nxt, prv, ra, rb, w)


def join_kernel(own, rn, rp, w, rw, out):
    ws = (w[...] + rw[...]).astype(jnp.bfloat16)
    for j in range(FAR):
        for h in range(2):
            s = (
                own[2 * j + h].astype(jnp.float32)
                + rn[2 * j + h].astype(jnp.float32)
                + rp[2 * j + h].astype(jnp.float32)
            )
            out[j, h * TILE : (h + 1) * TILE] = s.astype(jnp.bfloat16)
        out[j, 2 * TILE : 2 * TILE + WROWS] = ws


def join(own, rn, rp, w, rw):
    return pl.pallas_call(
        join_kernel,
        out_shape=jax.ShapeDtypeStruct((FAR, 2 * TILE + WROWS, TILE), jnp.bfloat16),
        in_specs=[vmem()] * 5,
        out_specs=vmem(),
        compiler_params=params(),
        name="join",
    )(own, rn, rp, w, rw)


def finish_kernel(parts, out, w):
    total = parts[0].astype(jnp.float32)
    for j in range(1, parts.shape[0]):
        total += parts[j].astype(jnp.float32)
    nodes = out.shape[0]
    out[...] = total[0:nodes].astype(jnp.bfloat16)
    for j in range(w.shape[0]):
        w[j] = total[nodes : nodes + WROWS]


def finish(parts, copies):
    n, rows, hidden = parts.shape
    return pl.pallas_call(
        finish_kernel,
        out_shape=(
            jax.ShapeDtypeStruct((rows - WROWS, hidden), jnp.bfloat16),
            jax.ShapeDtypeStruct((copies, WROWS, hidden), jnp.float32),
        ),
        in_specs=[vmem()],
        out_specs=(vmem(),) * 2,
        compiler_params=params(),
        name="finish",
    )(parts)


def local(
    features,
    tile_rows,
    tile_cols,
    tile_count,
    tile_values,
    weight,
    exit_weight,
    exit_bias,
    labels,
    label_mask,
    upstream,
):
    hidden = features.shape[-1]
    classes = exit_weight.shape[1]
    node_here = features.shape[1]
    row_devices = lax.axis_size("row")
    col_devices = lax.axis_size("col")
    row_tiles = node_here * col_devices // TILE
    nodes_total = node_here * row_devices * col_devices
    scale = float(nodes_total) ** (-0.5)
    values = tile_values[0, 0]
    rows = tile_rows[0, 0]
    cols = tile_cols[0, 0]
    count = tile_count.reshape(1)
    z = lax.axis_index("row") % Z
    mine = (z % NEAR).astype(jnp.int32).reshape(1)
    odd = (z % 2).astype(jnp.int32).reshape(1)

    far = lax.all_to_all(
        jnp.broadcast_to(features, (FAR, node_here, hidden)),
        "row",
        0,
        0,
        axis_index_groups=far_groups(),
        tiled=True,
    )
    prv = lax.ppermute(far, "row", shift(1))
    nxt = lax.ppermute(far, "row", shift(-1))
    ha = lax.ppermute(nxt[: FAR // 2], "row", shift(-1))
    hb = lax.ppermute(prv[FAR // 2 :], "row", shift(1))

    def blocks(v):
        return v.reshape(-1, TILE, hidden)

    partial_value = forward_products(
        rows,
        cols,
        count,
        mine,
        values,
        blocks(far),
        blocks(nxt),
        blocks(prv),
        blocks(ha),
        blocks(hb),
        row_tiles,
    )
    parts = lax.all_to_all(
        partial_value.reshape(col_devices, node_here, hidden), "col", 0, 0, tiled=True
    )
    sent = dense(
        parts,
        weight,
        exit_weight,
        exit_bias.reshape(1, classes),
        labels.reshape(node_here, 1),
        label_mask.reshape(node_here, 1),
        upstream[0],
    )
    got = lax.all_to_all(sent, "col", 0, 0, tiled=True)
    own, nxt, prv, ha, hb, w = backward_products(rows, cols, count, mine, values, got)

    ra = lax.ppermute(ha, "row", shift(1))
    rb = lax.ppermute(hb, "row", shift(-1))
    nxt, prv, w = fold(odd, nxt, prv, ra, rb, w)
    rn = lax.ppermute(nxt, "row", shift(1))
    rp = lax.ppermute(prv, "row", shift(-1))
    rw = lax.ppermute(w, "row", [(i, i ^ 2) for i in range(2 * Z)])
    joined = join(own, rn, rp, w, rw)
    last = lax.all_to_all(
        joined, "row", 0, 0, axis_index_groups=far_groups(), tiled=True
    )
    grad_input, wsum = finish(last, col_devices)
    wall = lax.all_to_all(wsum, "col", 0, 0, tiled=True).reshape(-1, hidden) * scale
    layer_total = wall[0:TILE]
    exit_total = wall[TILE : TILE + classes].T
    bias_total = wall[BIAS_AT : BIAS_AT + 2].reshape(-1)[:classes]
    return (grad_input[None], layer_total, exit_total, bias_total)


def solution(mesh):
    in_specs = (
        P("col", "row", None),
        P("row", "col", None),
        P("row", "col", None),
        P("row", "col"),
        P("row", "col", None, None, None),
        P(),
        P(),
        P(),
        P("row", "col"),
        P("row", "col"),
        P("row", "col", None),
    )
    out_specs = (P("col", "row", None), P(), P(), P())
    return jax.shard_map(local, mesh=mesh, in_specs=in_specs, out_specs=out_specs, check_vma=False)
```

time: 906 us -> 216 us (0.24)
  the two profiles are of different devices: /device:TPU:8 before, /device:TPU:32 now
where the time goes in v1:
time: 216 us; the launch traced here: 215 us
  blocking collectives  122 us (56%)
  waiting for transfers between devices  47.1 us (22%)
  starting transfers between devices  34.8 us (16%)
  Pallas kernels  6.38 us (3%)
  local copies, waits for them, and re-layouts  3.9 us (2%)
    all_to_all x1, blocking collectives, local(): lax.all_to_all(jnp.broadcast_to(features, (FAR, node_here, hidden)), 'row...  48.1 us
    all_to_all x1, blocking collectives, local(): lax.all_to_all(joined, 'row', 0, 0, axis_index_groups=far_groups(), tiled...  38 us
    all_to_all x1, blocking collectives, local(): got = lax.all_to_all(sent, 'col', 0, 0, tiled=True)  22 us
    all_to_all x1, waiting for transfers between devices, local(): lax.all_to_all(partial_value.reshape(col_devices, node_here, hidden), 'co...  17.6 us
    all_to_all x1, blocking collectives, local(): lax.all_to_all(wsum, 'col', 0, 0, tiled=True).reshape(-1, hidden) * scale  13.5 us
    ppermute x1, waiting for transfers between devices, local(): rw = lax.ppermute(w, 'row', [(i, i ^ 2) for i in range(2 * Z)])  8.91 us
    ppermute x1, waiting for transfers between devices, local(): prv = lax.ppermute(far, 'row', shift(1))  7.83 us
    all_to_all x1, starting transfers between devices, local(): lax.all_to_all(partial_value.reshape(col_devices, node_here, hidden), 'co...  6.88 us
  transfers between devices with their start and end apart: 10, of which 7 were waited for; matrix products, arithmetic and copies ran while one was open for 1% of the time, Pallas kernels for 0%

profile of v1, /device:TPU:32, one launch (start us, length us, event | category | flops | bytes accessed | tf_op | source)
XLA Modules:
  0.0 215.5 jit_solution(9982893160596828726)
XLA Ops:
  0.6 0.9 broadcast_in_dim.11
  1.6 48.1 %all_to_all.25 = bf16[8,256,128]{2,1,0:T(8,128)(2,1)S(1)} all-to-all(bf16[8,256,128]{2,1,0:T(8,128)(2,1)S(1)} %broadcast_in_dim.11), channel_id=1, replica_groups={{0,64,128,192,256,320,384,448},{16,80,144,208,272,336,400,464},{32,96,1..., dimensions={0} | all-to-all | bytes 1048576 | tf_op jit(solution)/shard_map/all_to_all | solution.py:298
  49.7 3.0 %collective-permute-start.1 = (bf16[8,256,128]{2,1,0:T(8,128)(2,1)S(1)}, bf16[8,256,128]{2,1,0:T(8,128)(2,1)S(1)}, u32[]{:S(2)}, u32[]{:S(2)}) collective-permute-start(bf16[8,256,128]{2,1,0:T(8,128)(2,1)S(1)} %all_to_all.25), channel_id=1, source_target_pairs={{0,16},{16,32},{32,48},{48,64},{64,80},{80,96},{96,112},{112,128},... | collective-permute-start | bytes 1572872 | tf_op jit(solution)/shard_map/ppermute | solution.py:306
  52.7 2.8 %collective-permute-start = (bf16[8,256,128]{2,1,0:T(8,128)(2,1)S(1)}, bf16[8,256,128]{2,1,0:T(8,128)(2,1)S(1)}, u32[]{:S(2)}, u32[]{:S(2)}) collective-permute-start(bf16[8,256,128]{2,1,0:T(8,128)(2,1)S(1)} %all_to_all.25), channel_id=1, source_target_pairs={{0,240},{16,0},{32,16},{48,32},{64,48},{80,64},{96,80},{112,96},{1... | collective-permute-start | bytes 1572872 | tf_op jit(solution)/shard_map/ppermute | solution.py:307
  55.6 7.8 %collective-permute-done.1 = bf16[8,256,128]{2,1,0:T(8,128)(2,1)S(1)} collective-permute-done((bf16[8,256,128]{2,1,0:T(8,128)(2,1)S(1)}, bf16[8,256,128]{2,1,0:T(8,128)(2,1)S(1)}, u32[]{:S(2)}, u32[]{:S(2)}) %collective-permute-start.1) | collective-permute-done | bytes 524320 | tf_op jit(solution)/shard_map/ppermute | solution.py:306
  63.4 2.2 %collective-permute-start.3 = (bf16[4,256,128]{2,1,0:T(8,128)(2,1)S(1)}, bf16[4,256,128]{2,1,0:T(8,128)(2,1)S(1)}, u32[]{:S(2)}, u32[]{:S(2)}) collective-permute-start(bf16[4,256,128]{2,1,0:T(8,128)(2,1)S(1)} %slice.29), channel_id=1, source_target_pairs={{0,16},{16,32},{32,48},{48,64},{64,80},{80,96},{96,112},{112,128},... | collective-permute-start | bytes 786440 | tf_op jit(solution)/shard_map/ppermute | solution.py:309
  65.6 0.7 slice.28
  66.4 3.6 %collective-permute-start.2 = (bf16[4,256,128]{2,1,0:T(8,128)(2,1)}, bf16[4,256,128]{2,1,0:T(8,128)(2,1)S(1)}, u32[]{:S(2)}, u32[]{:S(2)}) collective-permute-start(bf16[4,256,128]{2,1,0:T(8,128)(2,1)} %slice.28), channel_id=1, source_target_pairs={{0,240},{16,0},{32,16},{48,32},{64,48},{80,64},{96,80},{112,96},{1... | collective-permute-start | bytes 786440 | tf_op jit(solution)/shard_map/ppermute | solution.py:308
  70.7 1.0 collective-permute-done.3
  71.7 3.1 %collective-permute-done.2 = bf16[4,256,128]{2,1,0:T(8,128)(2,1)S(1)} collective-permute-done((bf16[4,256,128]{2,1,0:T(8,128)(2,1)}, bf16[4,256,128]{2,1,0:T(8,128)(2,1)S(1)}, u32[]{:S(2)}, u32[]{:S(2)}) %collective-permute-start.2) | collective-permute-done | bytes 262176 | tf_op jit(solution)/shard_map/ppermute | solution.py:308
  74.8 2.6 %forward_products.1 = bf16[32,128,128]{2,1,0:T(8,128)(2,1)} custom-call(s32[32]{0:T(128)S(1)} %bitcast.35, s32[32]{0:T(128)S(1)} %bitcast.37, s32[1]{0:T(128)} %bitcast.25.count, s32[1]{0:T(128)} %bitcast.3.mine, bf16[32,128,128]{2,1,0:T(8,128)(2,1)S(1)} %bitcast.27, bf16[16,128,128]{2,1,0:T(8,128)(2,1)S(1)} %bitcast.29, bf16[16,128,128]{2,1,0:T(8,128)(2,1)S(1)} %bitcast.31, ...), custom_call_target="tpu_custom_call" | custom-call | tf_op jit(solution)/shard_map/forward_products/pallas_call | solution.py:74
  77.5 6.9 %all-to-all-start.1 = ((bf16[16,256,128]{2,1,0:T(8,128)(2,1)}), bf16[16,256,128]{2,1,0:T(8,128)(2,1)S(1)}, u32[]{:S(2)}, u32[]{:S(2)}) async-start(bf16[16,256,128]{2,1,0:T(8,128)(2,1)} %bitcast.11), calls=%async_computation.1 | async-start | bytes 2097152 | tf_op jit(solution)/shard_map/all_to_all | solution.py:327
  84.8 17.6 %all-to-all-done.1.parts = bf16[16,256,128]{2,1,0:T(8,128)(2,1)S(1)} async-done(((bf16[16,256,128]{2,1,0:T(8,128)(2,1)}), bf16[16,256,128]{2,1,0:T(8,128)(2,1)S(1)}, u32[]{:S(2)}, u32[]{:S(2)}) %all-to-all-start.1) | async-done | bytes 1048608 | tf_op jit(solution)/shard_map/all_to_all | solution.py:327
  102.4 0.8 dense.1
  103.2 22.0 %all_to_all.26.g = bf16[16,288,128]{2,1,0:T(8,128)(2,1)S(1)} all-to-all(bf16[16,288,128]{2,1,0:T(8,128)(2,1)S(1)} %dense.1), channel_id=1, replica_groups=mesh['row'=32,'col'=16] {'col'}, dimensions={0} | all-to-all | bytes 2359296 | tf_op jit(solution)/shard_map/all_to_all | solution.py:339
  125.3 1.9 backward_products.1
  127.2 3.1 %collective-permute-start.4 = (bf16[1056,128]{1,0:T(8,128)(2,1)S(1)}, bf16[1056,128]{1,0:T(8,128)(2,1)S(1)}, u32[]{:S(2)}, u32[]{:S(2)}) collective-permute-start(bf16[1056,128]{1,0:T(8,128)(2,1)S(1)} %get-tuple-element.18), channel_id=1, source_target_pairs={{0,16},{16,32},{32,48},{48,64},{64,80},{80,96},{96,112},{112,128},... | collective-permute-start | bytes 811016 | tf_op jit(solution)/shard_map/ppermute | solution.py:342
  130.3 2.8 %collective-permute-start.5 = (bf16[1056,128]{1,0:T(8,128)(2,1)S(1)}, bf16[1056,128]{1,0:T(8,128)(2,1)S(1)}, u32[]{:S(2)}, u32[]{:S(2)}) collective-permute-start(bf16[1056,128]{1,0:T(8,128)(2,1)S(1)} %get-tuple-element.19), channel_id=1, source_target_pairs={{0,240},{16,0},{32,16},{48,32},{64,48},{80,64},{96,80},{112,96},{1... | collective-permute-start | bytes 811016 | tf_op jit(solution)/shard_map/ppermute | solution.py:343
  133.1 4.3 %collective-permute-done.4.ra = bf16[1056,128]{1,0:T(8,128)(2,1)S(1)} collective-permute-done((bf16[1056,128]{1,0:T(8,128)(2,1)S(1)}, bf16[1056,128]{1,0:T(8,128)(2,1)S(1)}, u32[]{:S(2)}, u32[]{:S(2)}) %collective-permute-start.4) | collective-permute-done | bytes 270368 | tf_op jit(solution)/shard_map/ppermute | solution.py:342
  137.3 4.3 %collective-permute-done.5.rb = bf16[1056,128]{1,0:T(8,128)(2,1)S(1)} collective-permute-done((bf16[1056,128]{1,0:T(8,128)(2,1)S(1)}, bf16[1056,128]{1,0:T(8,128)(2,1)S(1)}, u32[]{:S(2)}, u32[]{:S(2)}) %collective-permute-start.5) | collective-permute-done | bytes 270368 | tf_op jit(solution)/shard_map/ppermute | solution.py:343
  141.6 0.1 fold.1
  141.8 3.6 %collective-permute-start.6 = (bf16[16,128,128]{2,1,0:T(8,128)(2,1)S(1)}, bf16[16,128,128]{2,1,0:T(8,128)(2,1)S(1)}, u32[]{:S(2)}, u32[]{:S(2)}) collective-permute-start(bf16[16,128,128]{2,1,0:T(8,128)(2,1)S(1)} %get-tuple-element.21), channel_id=1, source_target_pairs={{0,16},{16,32},{32,48},{48,64},{64,80},{80,96},{96,112},{112,128},... | collective-permute-start | bytes 1572872 | tf_op jit(solution)/shard_map/ppermute | solution.py:345
  145.4 2.2 %collective-permute-start.7 = (bf16[16,128,128]{2,1,0:T(8,128)(2,1)S(1)}, bf16[16,128,128]{2,1,0:T(8,128)(2,1)S(1)}, u32[]{:S(2)}, u32[]{:S(2)}) collective-permute-start(bf16[16,128,128]{2,1,0:T(8,128)(2,1)S(1)} %get-tuple-element.22), channel_id=1, source_target_pairs={{0,240},{16,0},{32,16},{48,32},{64,48},{80,64},{96,80},{112,96},{1... | collective-permute-start | bytes 1572872 | tf_op jit(solution)/shard_map/ppermute | solution.py:346
  147.6 4.6 %collective-permute-start.8 = (f32[32,128]{1,0:T(8,128)S(1)}, f32[32,128]{1,0:T(8,128)S(1)}, u32[]{:S(2)}, u32[]{:S(2)}) collective-permute-start(f32[32,128]{1,0:T(8,128)S(1)} %get-tuple-element.23.w), channel_id=1, source_target_pairs={{0,32},{16,48},{32,0},{48,16},{64,96},{80,112},{96,64},{112,80},{1... | collective-permute-start | bytes 49160 | tf_op jit(solution)/shard_map/ppermute | solution.py:347
  152.2 8.9 %collective-permute-done.8.rw = f32[32,128]{1,0:T(8,128)S(1)} collective-permute-done((f32[32,128]{1,0:T(8,128)S(1)}, f32[32,128]{1,0:T(8,128)S(1)}, u32[]{:S(2)}, u32[]{:S(2)}) %collective-permute-start.8) | collective-permute-done | bytes 16416 | tf_op jit(solution)/shard_map/ppermute | solution.py:347
  161.2 0.2 join.1
  161.3 38.0 %all_to_all.27.parts = bf16[8,288,128]{2,1,0:T(8,128)(2,1)S(1)} all-to-all(bf16[8,288,128]{2,1,0:T(8,128)(2,1)S(1)} %join.1), channel_id=1, replica_groups={{0,64,128,192,256,320,384,448},{16,80,144,208,272,336,400,464},{32,96,1..., dimensions={0} | all-to-all | bytes 1179648 | tf_op jit(solution)/shard_map/all_to_all | solution.py:349
  199.4 0.7 finish.1
  200.1 13.5 %all_to_all.28 = f32[16,32,128]{2,1,0:T(8,128)S(1)} all-to-all(f32[16,32,128]{2,1,0:T(8,128)S(1)} %get-tuple-element.25), channel_id=1, replica_groups=mesh['row'=32,'col'=16] {'col'}, dimensions={0} | all-to-all | bytes 524288 | tf_op jit(solution)/shard_map/all_to_all | solution.py:353
  213.6 0.6 slice.30
  214.3 0.6 slice_bitcast_fusion
  214.9 0.6 slice_bitcast_fusion.1
  (26 shorter events, 0.5 us)
Async XLA Ops:
  1.5 73.3 %copy-start = (bf16[1,1,32,128,128]{4,3,2,1,0:T(8,128)(2,1)S(1)}, bf16[1,1,32,128,128]{4,3,2,1,0:T(8,128)(2,1)}, u32[]{:S(2)}) copy-start(bf16[1,1,32,128,128]{4,3,2,1,0:T(8,128)(2,1)} %param.15) | copy-start | bytes 3145732
  1.6 73.3 %copy-start.3 = (s32[1,1,32]{2,1,0:T(1,128)S(1)}, s32[1,1,32]{2,1,0:T(1,128)}, u32[]{:S(2)}) copy-start(s32[1,1,32]{2,1,0:T(1,128)} %param.12) | copy-start | bytes 388
  1.6 73.3 %copy-start.4 = (s32[1,1,32]{2,1,0:T(1,128)S(1)}, s32[1,1,32]{2,1,0:T(1,128)}, u32[]{:S(2)}) copy-start(s32[1,1,32]{2,1,0:T(1,128)} %param.13) | copy-start | bytes 388
  49.7 13.7 %collective-permute-start.1 = (bf16[8,256,128]{2,1,0:T(8,128)(2,1)S(1)}, bf16[8,256,128]{2,1,0:T(8,128)(2,1)S(1)}, u32[]{:S(2)}, u32[]{:S(2)}) collective-permute-start(bf16[8,256,128]{2,1,0:T(8,128)(2,1)S(1)} %all_to_all.25), channel_id=1, source_target_pairs={{0,16},{16,32},{32,48},{48,64},{64,80},{80,96},{96,112},{112,128},... | collective-permute-start | bytes 1572872 | tf_op jit(solution)/shard_map/ppermute | solution.py:306
  52.7 12.9 %collective-permute-start = (bf16[8,256,128]{2,1,0:T(8,128)(2,1)S(1)}, bf16[8,256,128]{2,1,0:T(8,128)(2,1)S(1)}, u32[]{:S(2)}, u32[]{:S(2)}) collective-permute-start(bf16[8,256,128]{2,1,0:T(8,128)(2,1)S(1)} %all_to_all.25), channel_id=1, source_target_pairs={{0,240},{16,0},{32,16},{48,32},{64,48},{80,64},{96,80},{112,96},{1... | collective-permute-start | bytes 1572872 | tf_op jit(solution)/shard_map/ppermute | solution.py:307
  63.4 8.3 %collective-permute-start.3 = (bf16[4,256,128]{2,1,0:T(8,128)(2,1)S(1)}, bf16[4,256,128]{2,1,0:T(8,128)(2,1)S(1)}, u32[]{:S(2)}, u32[]{:S(2)}) collective-permute-start(bf16[4,256,128]{2,1,0:T(8,128)(2,1)S(1)} %slice.29), channel_id=1, source_target_pairs={{0,16},{16,32},{32,48},{48,64},{64,80},{80,96},{96,112},{112,128},... | collective-permute-start | bytes 786440 | tf_op jit(solution)/shard_map/ppermute | solution.py:309
  66.4 8.5 %collective-permute-start.2 = (bf16[4,256,128]{2,1,0:T(8,128)(2,1)}, bf16[4,256,128]{2,1,0:T(8,128)(2,1)S(1)}, u32[]{:S(2)}, u32[]{:S(2)}) collective-permute-start(bf16[4,256,128]{2,1,0:T(8,128)(2,1)} %slice.28), channel_id=1, source_target_pairs={{0,240},{16,0},{32,16},{48,32},{64,48},{80,64},{96,80},{112,96},{1... | collective-permute-start | bytes 786440 | tf_op jit(solution)/shard_map/ppermute | solution.py:308
  77.4 6.9 %copy-start.7 = (s32[1,256]{1,0:T(1,128)S(1)}, s32[1,256]{1,0:T(1,128)}, u32[]{:S(2)}) copy-start(s32[1,256]{1,0:T(1,128)} %param.19) | copy-start | bytes 3076
  77.4 7.1 %copy-start.8 = (s32[1,256]{1,0:T(1,128)S(1)}, s32[1,256]{1,0:T(1,128)}, u32[]{:S(2)}) copy-start(s32[1,256]{1,0:T(1,128)} %param.20) | copy-start | bytes 3076
  77.4 7.2 %copy-start.6 = (bf16[128,172]{0,1:T(8,128)(2,1)S(1)}, bf16[128,172]{0,1:T(8,128)(2,1)}, u32[]{:S(2)}) copy-start(bf16[128,172]{0,1:T(8,128)(2,1)} %param.17) | copy-start | bytes 132100
  77.4 24.9 %copy-start.1 = (bf16[1,256,128]{2,1,0:T(8,128)(2,1)S(1)}, bf16[1,256,128]{2,1,0:T(8,128)(2,1)}, u32[]{:S(2)}) copy-start(bf16[1,256,128]{2,1,0:T(8,128)(2,1)} %param.21) | copy-start | bytes 196612
  77.4 24.9 %copy-start.2 = (bf16[128,128]{1,0:T(8,128)(2,1)S(1)}, bf16[128,128]{1,0:T(8,128)(2,1)}, u32[]{:S(2)}) copy-start(bf16[128,128]{1,0:T(8,128)(2,1)} %weight.1) | copy-start | bytes 98308
  77.5 24.9 %copy-start.5 = (f32[172]{0:T(256)S(1)}, f32[172]{0:T(256)}, u32[]{:S(2)}) copy-start(f32[172]{0:T(256)} %param.18) | copy-start | bytes 2068
  77.5 24.9 %all-to-all-start.1 = ((bf16[16,256,128]{2,1,0:T(8,128)(2,1)}), bf16[16,256,128]{2,1,0:T(8,128)(2,1)S(1)}, u32[]{:S(2)}, u32[]{:S(2)}) async-start(bf16[16,256,128]{2,1,0:T(8,128)(2,1)} %bitcast.11), calls=%async_computation.1 | async-start | bytes 2097152 | tf_op jit(solution)/shard_map/all_to_all | solution.py:327
  127.2 10.1 %collective-permute-start.4 = (bf16[1056,128]{1,0:T(8,128)(2,1)S(1)}, bf16[1056,128]{1,0:T(8,128)(2,1)S(1)}, u32[]{:S(2)}, u32[]{:S(2)}) collective-permute-start(bf16[1056,128]{1,0:T(8,128)(2,1)S(1)} %get-tuple-element.18), channel_id=1, source_target_pairs={{0,16},{16,32},{32,48},{48,64},{64,80},{80,96},{96,112},{112,128},... | collective-permute-start | bytes 811016 | tf_op jit(solution)/shard_map/ppermute | solution.py:342
  130.3 11.3 %collective-permute-start.5 = (bf16[1056,128]{1,0:T(8,128)(2,1)S(1)}, bf16[1056,128]{1,0:T(8,128)(2,1)S(1)}, u32[]{:S(2)}, u32[]{:S(2)}) collective-permute-start(bf16[1056,128]{1,0:T(8,128)(2,1)S(1)} %get-tuple-element.19), channel_id=1, source_target_pairs={{0,240},{16,0},{32,16},{48,32},{64,48},{80,64},{96,80},{112,96},{1... | collective-permute-start | bytes 811016 | tf_op jit(solution)/shard_map/ppermute | solution.py:343
  141.8 19.4 %collective-permute-start.6 = (bf16[16,128,128]{2,1,0:T(8,128)(2,1)S(1)}, bf16[16,128,128]{2,1,0:T(8,128)(2,1)S(1)}, u32[]{:S(2)}, u32[]{:S(2)}) collective-permute-start(bf16[16,128,128]{2,1,0:T(8,128)(2,1)S(1)} %get-tuple-element.21), channel_id=1, source_target_pairs={{0,16},{16,32},{32,48},{48,64},{64,80},{80,96},{96,112},{112,128},... | collective-permute-start | bytes 1572872 | tf_op jit(solution)/shard_map/ppermute | solution.py:345
  145.4 15.7 %collective-permute-start.7 = (bf16[16,128,128]{2,1,0:T(8,128)(2,1)S(1)}, bf16[16,128,128]{2,1,0:T(8,128)(2,1)S(1)}, u32[]{:S(2)}, u32[]{:S(2)}) collective-permute-start(bf16[16,128,128]{2,1,0:T(8,128)(2,1)S(1)} %get-tuple-element.22), channel_id=1, source_target_pairs={{0,240},{16,0},{32,16},{48,32},{64,48},{80,64},{96,80},{112,96},{1... | collective-permute-start | bytes 1572872 | tf_op jit(solution)/shard_map/ppermute | solution.py:346
  147.6 13.5 %collective-permute-start.8 = (f32[32,128]{1,0:T(8,128)S(1)}, f32[32,128]{1,0:T(8,128)S(1)}, u32[]{:S(2)}, u32[]{:S(2)}) collective-permute-start(f32[32,128]{1,0:T(8,128)S(1)} %get-tuple-element.23.w), channel_id=1, source_target_pairs={{0,32},{16,48},{32,0},{48,16},{64,96},{80,112},{96,64},{112,80},{1... | collective-permute-start | bytes 49160 | tf_op jit(solution)/shard_map/ppermute | solution.py:347

commit v2 on v0

v2 whole, which is shorter than its diff:
```python
import jax
import jax.numpy as jnp
from jax import lax
from jax.experimental import pallas as pl
from jax.experimental.pallas import tpu as pltpu
from jax.sharding import PartitionSpec as P

TILE = 128
Z = 16
NEAR = 4
FAR = Z // NEAR
WROWS = 48
BIAS_AT = 304
NT = (((1,), (1,)), ((), ()))
TN = (((0,), (0,)), ((), ()))

VMEM_LIMIT = 48 * 1024 * 1024


def far_groups():
    return [
        [x * Z + NEAR * q + k for q in range(FAR)] for x in range(2) for k in range(NEAR)
    ]


def pair_groups():
    return [[z, z + Z] for z in range(Z)]


def chip_groups():
    return [[2 * i + core for i in range(8)] for core in range(2)]


def shift(d):
    return [(x * Z + z, x * Z + (z + d) % Z) for x in range(2) for z in range(Z)]


def flip(n, bit):
    return [(i, i ^ bit) for i in range(n)]


def vmem():
    return pl.BlockSpec(memory_space=pltpu.VMEM)


def smem():
    return pl.BlockSpec(memory_space=pltpu.SMEM)


def params():
    return pltpu.CompilerParams(vmem_limit_bytes=VMEM_LIMIT)


def bf(v):
    return v.astype(jnp.bfloat16)


def f32(v):
    return v.astype(jnp.float32)


def out(shape, dtype=jnp.bfloat16):
    return jax.ShapeDtypeStruct(shape, dtype)


def call(kernel, name, outs, scalars, arrays, scratch=()):
    return pl.pallas_call(
        kernel,
        out_shape=outs,
        in_specs=[smem()] * len(scalars) + [vmem()] * len(arrays),
        out_specs=jax.tree.map(lambda _: vmem(), outs),
        scratch_shapes=list(scratch),
        compiler_params=params(),
        name=name,
    )(*scalars, *arrays)


def split_col(col):
    return col // 32, (col // 8) % 4, (col // 2) % 4, col % 2


def forward_kernel(rows, cols, count, here, a, own, nxt, prv, ha, hb, keep, send, xs, acc):
    xs[0:16] = own[...]
    xs[16:32] = nxt[...]
    xs[32:40] = ha[...]
    xs[40:48] = hb[...]
    xs[48:64] = prv[...]
    acc[...] = jnp.zeros_like(acc)
    mine, core = here[1], here[2]
    n = count[0]
    group = 4
    for base in range(0, a.shape[0], group):
        prods = []
        for s in range(base, base + group):
            x, q, k, half = split_col(cols[s])
            at = ((k - mine + 4) % 4) * 16 + q * 4 + x * 2 + half
            prods.append(jnp.dot(a[s], xs[at], preferred_element_type=jnp.float32))
        for s, p in zip(range(base, base + group), prods):
            t = rows[s]
            at = (((t // 2) % 2 + core) % 2) * 16 + (t // 4) * 2 + t % 2
            acc[jnp.where(s < n, at, 32)] += p
    keep[...] = bf(acc[0:16])
    send[...] = bf(acc[16:32])


def dense_kernel(parts, weight, exit_weight, bias, labels, mask, up, sent, wb):
    total = f32(parts[0])
    for j in range(1, parts.shape[0]):
        total += f32(parts[j])
    agg = bf(total)
    w = weight[...]
    ew = exit_weight[...]
    pre = jnp.dot(agg, w, preferred_element_type=jnp.float32)
    sig = 1.0 / (1.0 + jnp.exp(-pre))
    act = bf(pre * sig)
    logits = jnp.dot(act, ew, preferred_element_type=jnp.float32) + bias[...]
    expd = jnp.exp(logits)
    probs = expd / jnp.sum(expd, axis=1, keepdims=True)
    ids = lax.broadcasted_iota(jnp.int32, logits.shape, 1)
    onehot = f32(labels[...] == ids)
    dlogits = bf(f32(mask[...]) * (probs - onehot))
    dact = f32(up[...]) + lax.dot_general(
        dlogits, ew, NT, preferred_element_type=jnp.float32
    )
    dpre = bf(dact * sig * (1.0 + pre * (1.0 - sig)))
    dagg = bf(lax.dot_general(dpre, w, NT, preferred_element_type=jnp.float32))
    classes = ew.shape[1]
    wb[...] = jnp.zeros_like(wb)
    wb[0:TILE] = lax.dot_general(agg, dpre, TN, preferred_element_type=jnp.float32)
    wb[TILE : TILE + classes] = lax.dot_general(
        dlogits, act, TN, preferred_element_type=jnp.float32
    )
    bsum = jnp.sum(f32(dlogits), axis=0, keepdims=True)
    wb[BIAS_AT : BIAS_AT + 1] = bsum[:, 0:TILE]
    wb[BIAS_AT + 1 : BIAS_AT + 2, 0 : classes - TILE] = bsum[:, TILE:]
    nodes = dagg.shape[0]
    for j in range(sent.shape[0]):
        sent[j, 0:nodes] = dagg
        sent[j, nodes : nodes + WROWS] = bf(wb[j * WROWS : (j + 1) * WROWS])


def backward_kernel(
    rows, cols, count, here, a, got, oth, hu, ru, lu, ou, hv, rv, lv, ov, w, g, acc
):
    nodes = 2 * TILE
    for i in range(8):
        g[0, i] = got[i, 0:nodes]
        g[1, i] = oth[i, 0:nodes]
    acc[...] = jnp.zeros_like(acc)
    mx, mine, core = here[0], here[1], here[2]
    n = count[0]
    group = 4
    for base in range(0, a.shape[0], group):
        prods = []
        for s in range(base, base + group):
            t = rows[s]
            start = pl.multiple_of((t % 2) * TILE, TILE)
            gb = g[((t // 2) % 2 + core) % 2, t // 4, pl.ds(start, TILE), :]
            prods.append(lax.dot_general(a[s], gb, TN, preferred_element_type=jnp.float32))
        for s, p in zip(range(base, base + group), prods):
            x, q, k, half = split_col(cols[s])
            at = ((x + mx) % 2) * 32 + ((k - mine + 4) % 4) * 8 + q * 2 + half
            acc[jnp.where(s < n, at, 64)] += p
    ov[...] = bf(acc[0:8])
    rv[...] = bf(acc[8:16])
    hv[...] = bf(acc[16:24])
    lv[...] = bf(acc[24:32])
    ou[...] = bf(acc[32:40])
    ru[...] = bf(acc[40:48])
    lu[...] = bf(acc[56:64])
    mine_sum = f32(got[0, nodes : nodes + WROWS])
    other_sum = f32(oth[0, nodes : nodes + WROWS])
    for j in range(1, 8):
        mine_sum += f32(got[j, nodes : nodes + WROWS])
        other_sum += f32(oth[j, nodes : nodes + WROWS])
    ws = bf(mine_sum + other_sum)
    for i in range(8):
        hu[i * TILE : (i + 1) * TILE] = bf(acc[48 + i])
    hu[8 * TILE : 8 * TILE + WROWS] = ws
    w[...] = ws


def fold1_kernel(hv, xh, w, a, b, ow):
    for i in range(4):
        rows = slice(i * TILE, (i + 1) * TILE)
        a[rows] = bf(f32(hv[i]) + f32(xh[rows]))
        b[rows] = bf(f32(hv[4 + i]) + f32(xh[(4 + i) * TILE : (5 + i) * TILE]))
    ws = bf(f32(w[...]) + f32(xh[8 * TILE : 8 * TILE + WROWS]))
    a[4 * TILE : 4 * TILE + WROWS] = ws
    b[4 * TILE : 4 * TILE + WROWS] = ws
    ow[...] = ws


def fold2_kernel(here, rv, xr, lv, xl, ra, rb, w, r, l, ow):
    for i in range(4):
        rows = slice(i * TILE, (i + 1) * TILE)
        r[i] = bf(f32(rv[i]) + f32(xr[i]) + f32(ra[rows]))
        l[4 + i] = bf(f32(lv[4 + i]) + f32(xl[4 + i]) + f32(rb[rows]))
        r[4 + i] = bf(f32(rv[4 + i]) + f32(xr[4 + i]))
        l[i] = bf(f32(lv[i]) + f32(xl[i]))
    tail = slice(4 * TILE, 4 * TILE + WROWS)
    partner = jnp.where(here[1] % 2 == 1, f32(ra[tail]), f32(rb[tail]))
    ow[...] = f32(w[...]) + partner


def join_kernel(ov, xo, rn, rp, w, rw, o):
    ws = bf(w[...] + rw[...])
    for j in range(FAR):
        for h in range(2):
            i = 2 * j + h
            s = f32(ov[i]) + f32(xo[i]) + f32(rn[i]) + f32(rp[i])
            o[j, h * TILE : (h + 1) * TILE] = bf(s)
        o[j, 2 * TILE : 2 * TILE + WROWS] = ws


def finish_kernel(parts, o, w):
    total = f32(parts[0])
    for j in range(1, parts.shape[0]):
        total += f32(parts[j])
    nodes = o.shape[0]
    o[...] = bf(total[0:nodes])
    for j in range(w.shape[0]):
        w[j] = total[nodes : nodes + WROWS]


def unpack_kernel(scale, wall, layer, exit_t, bias, wb):
    for j in range(wall.shape[0]):
        wb[j * WROWS : (j + 1) * WROWS] = wall[j] * scale[0]
    classes = exit_t.shape[0]
    layer[...] = wb[0:TILE]
    exit_t[...] = wb[TILE : TILE + classes]
    bias[:, 0:TILE] = wb[BIAS_AT : BIAS_AT + 1]
    bias[:, TILE:classes] = wb[BIAS_AT + 1 : BIAS_AT + 2, 0 : classes - TILE]


def local(
    features,
    tile_rows,
    tile_cols,
    tile_count,
    tile_values,
    weight,
    exit_weight,
    exit_bias,
    labels,
    label_mask,
    upstream,
):
    hidden = features.shape[-1]
    classes = exit_weight.shape[1]
    nodes = features.shape[1]
    nodes_total = nodes * lax.axis_size("row") * lax.axis_size("col")
    scale = jnp.full((1,), float(nodes_total) ** (-0.5), jnp.float32)
    values = tile_values[0, 0]
    r = lax.axis_index("row")
    here = jnp.stack([r // Z, r % NEAR, lax.axis_index("col") % 2]).astype(jnp.int32)
    scalars = (tile_rows[0, 0], tile_cols[0, 0], tile_count.reshape(1), here)

    def blocks(v):
        return v.reshape(-1, TILE, hidden)

    def acc(n):
        return pltpu.VMEM((n, TILE, hidden), jnp.float32)

    x_pair, core_pair = flip(2 * Z, Z), flip(16, 1)

    pair = lax.all_gather(
        features, "row", axis=0, axis_index_groups=pair_groups(), tiled=True
    )
    far = lax.all_gather(pair, "row", axis=0, axis_index_groups=far_groups(), tiled=True)
    nxt = lax.ppermute(far, "row", shift(-1))
    prv = lax.ppermute(far, "row", shift(1))
    ha = lax.ppermute(nxt[:FAR], "row", shift(-1))
    hb = lax.ppermute(prv[FAR:], "row", shift(1))

    full, half = out((16, TILE, hidden)), out((8, TILE, hidden))
    keep, send = call(
        forward_kernel,
        "forward_products",
        (full, full),
        scalars,
        (values, blocks(far), blocks(nxt), blocks(prv), blocks(ha), blocks(hb)),
        (pltpu.VMEM((64, TILE, hidden), jnp.bfloat16), acc(33)),
    )
    came = lax.ppermute(send, "col", core_pair)
    paired = bf(f32(keep) + f32(came)).reshape(8, nodes, hidden)
    parts = lax.all_to_all(
        paired, "col", 0, 0, axis_index_groups=chip_groups(), tiled=True
    )
    sent = call(
        dense_kernel,
        "dense",
        out((8, nodes + WROWS, hidden)),
        (),
        (
            parts,
            weight,
            exit_weight,
            exit_bias.reshape(1, classes),
            labels.reshape(nodes, 1),
            label_mask.reshape(nodes, 1),
            upstream[0],
        ),
        (pltpu.VMEM((8 * WROWS, hidden), jnp.float32),),
    )
    got = lax.all_to_all(sent, "col", 0, 0, axis_index_groups=chip_groups(), tiled=True)
    oth = lax.ppermute(got, "col", core_pair)
    hu, ru, lu, ou, hv, rv, lv, ov, w = call(
        backward_kernel,
        "backward_products",
        (out((8 * TILE + WROWS, hidden)),) + (half,) * 7 + (out((WROWS, hidden)),),
        scalars,
        (values, got, oth),
        (pltpu.VMEM((2, 8, nodes, hidden), jnp.bfloat16), acc(65)),
    )

    xh = lax.ppermute(hu, "row", x_pair)
    xr = lax.ppermute(ru, "row", x_pair)
    xl = lax.ppermute(lu, "row", x_pair)
    xo = lax.ppermute(ou, "row", x_pair)
    side = out((4 * TILE + WROWS, hidden))
    a, b, w = call(
        fold1_kernel, "fold1", (side, side, out((WROWS, hidden))), (), (hv, xh, w)
    )
    ra = lax.ppermute(a, "row", shift(1))
    rb = lax.ppermute(b, "row", shift(-1))
    rr, ll, w = call(
        fold2_kernel,
        "fold2",
        (half, half, out((WROWS, hidden), jnp.float32)),
        (here,),
        (rv, xr, lv, xl, ra, rb, w),
    )
    rn = lax.ppermute(rr, "row", shift(1))
    rp = lax.ppermute(ll, "row", shift(-1))
    rw = lax.ppermute(w, "row", flip(2 * Z, 2))
    joined = call(
        join_kernel,
        "join",
        out((FAR, nodes + WROWS, hidden)),
        (),
        (ov, xo, rn, rp, w, rw),
    )
    last = lax.all_to_all(
        joined, "row", 0, 0, axis_index_groups=far_groups(), tiled=True
    )
    grad_input, wsum = call(
        finish_kernel,
        "finish",
        (out((nodes, hidden)), out((8, WROWS, hidden), jnp.float32)),
        (),
        (last,),
    )
    wall = lax.all_to_all(wsum, "col", 0, 0, axis_index_groups=chip_groups(), tiled=True)
    layer_total, exit_t, bias_total = call(
        unpack_kernel,
        "unpack",
        (
            out((TILE, hidden), jnp.float32),
            out((classes, hidden), jnp.float32),
            out((1, classes), jnp.float32),
        ),
        (scale,),
        (wall,),
        (pltpu.VMEM((8 * WROWS, hidden), jnp.float32),),
    )
    return (grad_input[None], layer_total, exit_t.T, bias_total.reshape(classes))


def solution(mesh):
    in_specs = (
        P("col", "row", None),
        P("row", "col", None),
        P("row", "col", None),
        P("row", "col"),
        P("row", "col", None, None, None),
        P(),
        P(),
        P(),
        P("row", "col"),
        P("row", "col"),
        P("row", "col", None),
    )
    out_specs = (P("col", "row", None), P(), P(), P())
    return jax.shard_map(local, mesh=mesh, in_specs=in_specs, out_specs=out_specs, check_vma=False)
```

time: 906 us -> 190 us (0.21)
  the two profiles are of different devices: /device:TPU:8 before, /device:TPU:2 now
where the time goes in v2:
time: 190 us; the launch traced here: 189 us
  blocking collectives  89.1 us (47%)
  starting transfers between devices  52.8 us (28%)
  waiting for transfers between devices  32.7 us (17%)
  Pallas kernels  7.29 us (4%)
  local copies, waits for them, and re-layouts  4.46 us (2%)
    all_gather x1, blocking collectives, local(): lax.all_gather(pair, 'row', axis=0, axis_index_groups=far_groups(), tiled...  27.7 us
    all_to_all x1, blocking collectives, local(): lax.all_to_all(joined, 'row', 0, 0, axis_index_groups=far_groups(), tiled...  25.1 us
    all_to_all x1, blocking collectives, local(): lax.all_to_all(sent, 'col', 0, 0, axis_index_groups=chip_groups(), tiled=...  16.1 us
    all_to_all x1, blocking collectives, local(): lax.all_to_all(wsum, 'col', 0, 0, axis_index_groups=chip_groups(), tiled=...  10.9 us
    all_gather x1, blocking collectives, local(): lax.all_gather(features, 'row', axis=0, axis_index_groups=pair_groups(),...  9.21 us
    all_to_all x1, waiting for transfers between devices, local(): lax.all_to_all(paired, 'col', 0, 0, axis_index_groups=chip_groups(), tile...  8.82 us
    pallas_call x8, Pallas kernels, call(): pl.pallas_call(kernel, out_shape=outs, in_specs=[smem()] * len(scalars) +...  7.29 us
    ppermute x1, waiting for transfers between devices, local(): hb = lax.ppermute(prv[FAR:], 'row', shift(1))  6.54 us
  transfers between devices with their start and end apart: 16, of which 9 were waited for; matrix products, arithmetic and copies ran while one was open for 1% of the time, Pallas kernels for 0%

profile of v2, /device:TPU:2, one launch (start us, length us, event | category | flops | bytes accessed | tf_op | source)
XLA Modules:
  0.0 188.9 jit_solution(12251893760908154164)
XLA Ops:
  0.6 9.2 %all_gather.6 = bf16[2,256,128]{2,1,0:T(8,128)(2,1)S(1)} all-gather(bf16[1,256,128]{2,1,0:T(8,128)(2,1)} %param.11), channel_id=1, replica_groups={{0,256},{16,272},{32,288},{48,304},{64,320},{80,336},{96,352},{112,368}..., dimensions={0}, use_global_device_ids=true | all-gather | bytes 196608 | tf_op jit(solution)/shard_map/all_gather | solution.py:267
  9.9 27.7 %all_gather.7 = bf16[8,256,128]{2,1,0:T(8,128)(2,1)S(1)} all-gather(bf16[2,256,128]{2,1,0:T(8,128)(2,1)S(1)} %all_gather.6), channel_id=1, replica_groups={{0,64,128,192},{16,80,144,208},{32,96,160,224},{48,112,176,240},{256,32..., dimensions={0}, use_global_device_ids=true | all-gather | bytes 655360 | tf_op jit(solution)/shard_map/all_gather | solution.py:270
  37.6 4.9 %collective-permute-start = (bf16[8,256,128]{2,1,0:T(8,128)(2,1)S(1)}, bf16[8,256,128]{2,1,0:T(8,128)(2,1)S(1)}, u32[]{:S(2)}, u32[]{:S(2)}) collective-permute-start(bf16[8,256,128]{2,1,0:T(8,128)(2,1)S(1)} %all_gather.7), channel_id=1, source_target_pairs={{0,240},{16,0},{32,16},{48,32},{64,48},{80,64},{96,80},{112,96},{1... | collective-permute-start | bytes 1572872 | tf_op jit(solution)/shard_map/ppermute | solution.py:271
  42.5 1.9 %collective-permute-start.1 = (bf16[8,256,128]{2,1,0:T(8,128)(2,1)S(1)}, bf16[8,256,128]{2,1,0:T(8,128)(2,1)S(1)}, u32[]{:S(2)}, u32[]{:S(2)}) collective-permute-start(bf16[8,256,128]{2,1,0:T(8,128)(2,1)S(1)} %all_gather.7), channel_id=1, source_target_pairs={{0,16},{16,32},{32,48},{48,64},{64,80},{80,96},{96,112},{112,128},... | collective-permute-start | bytes 1572872 | tf_op jit(solution)/shard_map/ppermute | solution.py:272
  44.5 5.5 %collective-permute-done = bf16[8,256,128]{2,1,0:T(8,128)(2,1)S(1)} collective-permute-done((bf16[8,256,128]{2,1,0:T(8,128)(2,1)S(1)}, bf16[8,256,128]{2,1,0:T(8,128)(2,1)S(1)}, u32[]{:S(2)}, u32[]{:S(2)}) %collective-permute-start) | collective-permute-done | bytes 524320 | tf_op jit(solution)/shard_map/ppermute | solution.py:271
  50.0 5.6 %collective-permute-start.2 = (bf16[4,256,128]{2,1,0:T(8,128)(2,1)S(1)}, bf16[4,256,128]{2,1,0:T(8,128)(2,1)S(1)}, u32[]{:S(2)}, u32[]{:S(2)}) collective-permute-start(bf16[4,256,128]{2,1,0:T(8,128)(2,1)S(1)} %slice.8), channel_id=1, source_target_pairs={{0,240},{16,0},{32,16},{48,32},{64,48},{80,64},{96,80},{112,96},{1... | collective-permute-start | bytes 786440 | tf_op jit(solution)/shard_map/ppermute | solution.py:273
  56.3 1.9 %collective-permute-start.3 = (bf16[4,256,128]{2,1,0:T(8,128)(2,1)}, bf16[4,256,128]{2,1,0:T(8,128)(2,1)S(1)}, u32[]{:S(2)}, u32[]{:S(2)}) collective-permute-start(bf16[4,256,128]{2,1,0:T(8,128)(2,1)} %slice.9), channel_id=1, source_target_pairs={{0,16},{16,32},{32,48},{48,64},{64,80},{80,96},{96,112},{112,128},... | collective-permute-start | bytes 786440 | tf_op jit(solution)/shard_map/ppermute | solution.py:274
  59.5 6.5 %collective-permute-done.3 = bf16[4,256,128]{2,1,0:T(8,128)(2,1)S(1)} collective-permute-done((bf16[4,256,128]{2,1,0:T(8,128)(2,1)}, bf16[4,256,128]{2,1,0:T(8,128)(2,1)S(1)}, u32[]{:S(2)}, u32[]{:S(2)}) %collective-permute-start.3) | collective-permute-done | bytes 262176 | tf_op jit(solution)/shard_map/ppermute | solution.py:274
  66.7 2.0 %forward_products.1 = (bf16[16,128,128]{2,1,0:T(8,128)(2,1)S(1)}, bf16[16,128,128]{2,1,0:T(8,128)(2,1)S(1)}) custom-call(s32[32]{0:T(128)S(1)} %bitcast.30, s32[32]{0:T(128)S(1)} %bitcast.32, s32[1]{0:T(128)} %bitcast.20.count, s32[3]{0:T(128)S(1)} %pad_add_fusion.here, bf16[32,128,128]{2,1,0:T(8,128)(2,1)S(1)} %bitcast.22, ...), custom_call_target="tpu_custom_call" | custom-call | tf_op jit(solution)/shard_map/forward_products/pallas_call | solution.py:67
  68.7 1.9 %collective-permute-start.4 = (bf16[16,128,128]{2,1,0:T(8,128)(2,1)S(1)}, bf16[16,128,128]{2,1,0:T(8,128)(2,1)S(1)}, u32[]{:S(2)}, u32[]{:S(2)}) collective-permute-start(bf16[16,128,128]{2,1,0:T(8,128)(2,1)S(1)} %get-tuple-element.27), channel_id=1, source_target_pairs={{0,1},{1,0},{2,3},{3,2},{4,5},{5,4},{6,7},{7,6},{8,9},{9,8},{10,11... | collective-permute-start | bytes 1572872 | tf_op jit(solution)/shard_map/ppermute | solution.py:285
  70.6 1.9 collective-permute-done.4
  72.5 1.0 add_convert_fusion
  73.4 6.0 %all-to-all-start = ((bf16[8,256,128]{2,1,0:T(8,128)(2,1)}), bf16[8,256,128]{2,1,0:T(8,128)(2,1)S(1)}, u32[]{:S(2)}, u32[]{:S(2)}) async-start(bf16[8,256,128]{2,1,0:T(8,128)(2,1)} %bitcast.12), calls=%async_computation | async-start | bytes 1048576 | tf_op jit(solution)/shard_map/all_to_all | solution.py:287
  81.9 8.8 %all-to-all-done.parts = bf16[8,256,128]{2,1,0:T(8,128)(2,1)S(1)} async-done(((bf16[8,256,128]{2,1,0:T(8,128)(2,1)}), bf16[8,256,128]{2,1,0:T(8,128)(2,1)S(1)}, u32[]{:S(2)}, u32[]{:S(2)}) %all-to-all-start) | async-done | bytes 524320 | tf_op jit(solution)/shard_map/all_to_all | solution.py:287
  91.4 0.8 dense.1
  92.1 16.1 %all_to_all.20.got = bf16[8,304,128]{2,1,0:T(8,128)(2,1)S(1)} all-to-all(bf16[8,304,128]{2,1,0:T(8,128)(2,1)S(1)} %dense.1), channel_id=1, replica_groups={{0,2,4,6,8,10,12,14},{1,3,5,7,9,11,13,15},{16,18,20,22,24,26,28,30},{17..., dimensions={0} | all-to-all | bytes 1245184 | tf_op jit(solution)/shard_map/all_to_all | solution.py:306
  108.2 1.9 %collective-permute-start.5 = (bf16[8,304,128]{2,1,0:T(8,128)(2,1)S(1)}, bf16[8,304,128]{2,1,0:T(8,128)(2,1)S(1)}, u32[]{:S(2)}, u32[]{:S(2)}) collective-permute-start(bf16[8,304,128]{2,1,0:T(8,128)(2,1)S(1)} %all_to_all.20.got), channel_id=1, source_target_pairs={{0,1},{1,0},{2,3},{3,2},{4,5},{5,4},{6,7},{7,6},{8,9},{9,8},{10,11... | collective-permute-start | bytes 1867784 | tf_op jit(solution)/shard_map/ppermute | solution.py:307
  110.1 2.0 %collective-permute-done.5.oth = bf16[8,304,128]{2,1,0:T(8,128)(2,1)S(1)} collective-permute-done((bf16[8,304,128]{2,1,0:T(8,128)(2,1)S(1)}, bf16[8,304,128]{2,1,0:T(8,128)(2,1)S(1)}, u32[]{:S(2)}, u32[]{:S(2)}) %collective-permute-start.5) | collective-permute-done | bytes 622624 | tf_op jit(solution)/shard_map/ppermute | solution.py:307
  112.1 2.3 %backward_products.1 = (bf16[1072,128]{1,0:T(8,128)(2,1)S(1)}, bf16[8,128,128]{2,1,0:T(8,128)(2,1)S(1)}, bf16[8,128,128]{2,1,0:T(8,128)(2,1)S(1)}, bf16[8,128,12...) custom-call(s32[32]{0:T(128)S(1)} %bitcast.31, ...), custom_call_target="tpu_custom_call" | custom-call | tf_op jit(solution)/shard_map/backward_products/pallas_call | solution.py:67
  114.4 3.3 %collective-permute-start.9 = (bf16[1072,128]{1,0:T(8,128)(2,1)S(1)}, bf16[1072,128]{1,0:T(8,128)(2,1)S(1)}, u32[]{:S(2)}, u32[]{:S(2)}) collective-permute-start(bf16[1072,128]{1,0:T(8,128)(2,1)S(1)} %get-tuple-element.35), channel_id=1, source_target_pairs={{0,256},{16,272},{32,288},{48,304},{64,320},{80,336},{96,352},{112... | collective-permute-start | bytes 823304 | tf_op jit(solution)/shard_map/ppermute | solution.py:317
  117.8 2.5 %collective-permute-start.7 = (bf16[8,128,128]{2,1,0:T(8,128)(2,1)S(1)}, bf16[8,128,128]{2,1,0:T(8,128)(2,1)S(1)}, u32[]{:S(2)}, u32[]{:S(2)}) collective-permute-start(bf16[8,128,128]{2,1,0:T(8,128)(2,1)S(1)} %get-tuple-element.31), channel_id=1, source_target_pairs={{0,256},{16,272},{32,288},{48,304},{64,320},{80,336},{96,352},{112... | collective-permute-start | bytes 786440 | tf_op jit(solution)/shard_map/ppermute | solution.py:318
  120.3 3.3 %collective-permute-start.8 = (bf16[8,128,128]{2,1,0:T(8,128)(2,1)S(1)}, bf16[8,128,128]{2,1,0:T(8,128)(2,1)S(1)}, u32[]{:S(2)}, u32[]{:S(2)}) collective-permute-start(bf16[8,128,128]{2,1,0:T(8,128)(2,1)S(1)} %get-tuple-element.33), channel_id=1, source_target_pairs={{0,256},{16,272},{32,288},{48,304},{64,320},{80,336},{96,352},{112... | collective-permute-start | bytes 786440 | tf_op jit(solution)/shard_map/ppermute | solution.py:319
  123.6 2.1 %collective-permute-done.9.xh = bf16[1072,128]{1,0:T(8,128)(2,1)S(1)} collective-permute-done((bf16[1072,128]{1,0:T(8,128)(2,1)S(1)}, bf16[1072,128]{1,0:T(8,128)(2,1)S(1)}, u32[]{:S(2)}, u32[]{:S(2)}) %collective-permute-start.9) | collective-permute-done | bytes 274464 | tf_op jit(solution)/shard_map/ppermute | solution.py:317
  125.8 1.9 %collective-permute-start.10 = (bf16[560,128]{1,0:T(8,128)(2,1)S(1)}, bf16[560,128]{1,0:T(8,128)(2,1)S(1)}, u32[]{:S(2)}, u32[]{:S(2)}) collective-permute-start(bf16[560,128]{1,0:T(8,128)(2,1)S(1)} %get-tuple-element.37), channel_id=1, source_target_pairs={{0,16},{16,32},{32,48},{48,64},{64,80},{80,96},{96,112},{112,128},... | collective-permute-start | bytes 430088 | tf_op jit(solution)/shard_map/ppermute | solution.py:325
  127.7 5.1 %collective-permute-start.11 = (bf16[560,128]{1,0:T(8,128)(2,1)S(1)}, bf16[560,128]{1,0:T(8,128)(2,1)S(1)}, u32[]{:S(2)}, u32[]{:S(2)}) collective-permute-start(bf16[560,128]{1,0:T(8,128)(2,1)S(1)} %get-tuple-element.38), channel_id=1, source_target_pairs={{0,240},{16,0},{32,16},{48,32},{64,48},{80,64},{96,80},{112,96},{1... | collective-permute-start | bytes 430088 | tf_op jit(solution)/shard_map/ppermute | solution.py:326
  132.9 3.3 %collective-permute-start.6 = (bf16[8,128,128]{2,1,0:T(8,128)(2,1)S(1)}, bf16[8,128,128]{2,1,0:T(8,128)(2,1)S(1)}, u32[]{:S(2)}, u32[]{:S(2)}) collective-permute-start(bf16[8,128,128]{2,1,0:T(8,128)(2,1)S(1)} %get-tuple-element.29), channel_id=1, source_target_pairs={{0,256},{16,272},{32,288},{48,304},{64,320},{80,336},{96,352},{112... | collective-permute-start | bytes 786440 | tf_op jit(solution)/shard_map/ppermute | solution.py:320
  137.7 1.9 %collective-permute-start.12 = (bf16[8,128,128]{2,1,0:T(8,128)(2,1)S(1)}, bf16[8,128,128]{2,1,0:T(8,128)(2,1)S(1)}, u32[]{:S(2)}, u32[]{:S(2)}) collective-permute-start(bf16[8,128,128]{2,1,0:T(8,128)(2,1)S(1)} %get-tuple-element.40), channel_id=1, source_target_pairs={{0,16},{16,32},{32,48},{48,64},{64,80},{80,96},{96,112},{112,128},... | collective-permute-start | bytes 786440 | tf_op jit(solution)/shard_map/ppermute | solution.py:334
  139.6 5.1 %collective-permute-start.13 = (bf16[8,128,128]{2,1,0:T(8,128)(2,1)S(1)}, bf16[8,128,128]{2,1,0:T(8,128)(2,1)S(1)}, u32[]{:S(2)}, u32[]{:S(2)}) collective-permute-start(bf16[8,128,128]{2,1,0:T(8,128)(2,1)S(1)} %get-tuple-element.41), channel_id=1, source_target_pairs={{0,240},{16,0},{32,16},{48,32},{64,48},{80,64},{96,80},{112,96},{1... | collective-permute-start | bytes 786440 | tf_op jit(solution)/shard_map/ppermute | solution.py:335
  144.7 2.0 %collective-permute-start.14 = (f32[48,128]{1,0:T(8,128)S(1)}, f32[48,128]{1,0:T(8,128)S(1)}, u32[]{:S(2)}, u32[]{:S(2)}) collective-permute-start(f32[48,128]{1,0:T(8,128)S(1)} %get-tuple-element.42.w), channel_id=1, source_target_pairs={{0,32},{16,48},{32,0},{48,16},{64,96},{80,112},{96,64},{112,80},{1... | collective-permute-start | bytes 73736 | tf_op jit(solution)/shard_map/ppermute | solution.py:336
  146.8 4.6 %collective-permute-done.14.rw = f32[48,128]{1,0:T(8,128)S(1)} collective-permute-done((f32[48,128]{1,0:T(8,128)S(1)}, f32[48,128]{1,0:T(8,128)S(1)}, u32[]{:S(2)}, u32[]{:S(2)}) %collective-permute-start.14) | collective-permute-done | bytes 24608 | tf_op jit(solution)/shard_map/ppermute | solution.py:336
  151.5 25.1 %all_to_all.21.parts = bf16[4,304,128]{2,1,0:T(8,128)(2,1)S(1)} all-to-all(bf16[4,304,128]{2,1,0:T(8,128)(2,1)S(1)} %join.1), channel_id=1, replica_groups={{0,64,128,192},{16,80,144,208},{32,96,160,224},{48,112,176,240},{256,32..., dimensions={0} | all-to-all | bytes 622592 | tf_op jit(solution)/shard_map/all_to_all | solution.py:344
  177.3 10.9 %all_to_all.22.wall = f32[8,48,128]{2,1,0:T(8,128)S(1)} all-to-all(f32[8,48,128]{2,1,0:T(8,128)S(1)} %get-tuple-element.44), channel_id=1, replica_groups={{0,2,4,6,8,10,12,14},{1,3,5,7,9,11,13,15},{16,18,20,22,24,26,28,30},{17..., dimensions={0} | all-to-all | bytes 393216 | tf_op jit(solution)/shard_map/all_to_all | solution.py:354
  (38 shorter events, 8.0 us)
Async XLA Ops:
  0.6 65.4 %copy-start = (bf16[1,1,32,128,128]{4,3,2,1,0:T(8,128)(2,1)S(1)}, bf16[1,1,32,128,128]{4,3,2,1,0:T(8,128)(2,1)}, u32[]{:S(2)}) copy-start(bf16[1,1,32,128,128]{4,3,2,1,0:T(8,128)(2,1)} %param.15) | copy-start | bytes 3145732
  37.6 12.4 %collective-permute-start = (bf16[8,256,128]{2,1,0:T(8,128)(2,1)S(1)}, bf16[8,256,128]{2,1,0:T(8,128)(2,1)S(1)}, u32[]{:S(2)}, u32[]{:S(2)}) collective-permute-start(bf16[8,256,128]{2,1,0:T(8,128)(2,1)S(1)} %all_gather.7), channel_id=1, source_target_pairs={{0,240},{16,0},{32,16},{48,32},{64,48},{80,64},{96,80},{112,96},{1... | collective-permute-start | bytes 1572872 | tf_op jit(solution)/shard_map/ppermute | solution.py:271
  42.5 13.1 %collective-permute-start.1 = (bf16[8,256,128]{2,1,0:T(8,128)(2,1)S(1)}, bf16[8,256,128]{2,1,0:T(8,128)(2,1)S(1)}, u32[]{:S(2)}, u32[]{:S(2)}) collective-permute-start(bf16[8,256,128]{2,1,0:T(8,128)(2,1)S(1)} %all_gather.7), channel_id=1, source_target_pairs={{0,16},{16,32},{32,48},{48,64},{64,80},{80,96},{96,112},{112,128},... | collective-permute-start | bytes 1572872 | tf_op jit(solution)/shard_map/ppermute | solution.py:272
  50.0 9.5 %collective-permute-start.2 = (bf16[4,256,128]{2,1,0:T(8,128)(2,1)S(1)}, bf16[4,256,128]{2,1,0:T(8,128)(2,1)S(1)}, u32[]{:S(2)}, u32[]{:S(2)}) collective-permute-start(bf16[4,256,128]{2,1,0:T(8,128)(2,1)S(1)} %slice.8), channel_id=1, source_target_pairs={{0,240},{16,0},{32,16},{48,32},{64,48},{80,64},{96,80},{112,96},{1... | collective-permute-start | bytes 786440 | tf_op jit(solution)/shard_map/ppermute | solution.py:273
  56.3 9.7 %collective-permute-start.3 = (bf16[4,256,128]{2,1,0:T(8,128)(2,1)}, bf16[4,256,128]{2,1,0:T(8,128)(2,1)S(1)}, u32[]{:S(2)}, u32[]{:S(2)}) collective-permute-start(bf16[4,256,128]{2,1,0:T(8,128)(2,1)} %slice.9), channel_id=1, source_target_pairs={{0,16},{16,32},{32,48},{48,64},{64,80},{80,96},{96,112},{112,128},... | collective-permute-start | bytes 786440 | tf_op jit(solution)/shard_map/ppermute | solution.py:274
  66.0 0.7 copy-start.3
  66.0 0.7 copy-start.4
  68.7 3.8 %collective-permute-start.4 = (bf16[16,128,128]{2,1,0:T(8,128)(2,1)S(1)}, bf16[16,128,128]{2,1,0:T(8,128)(2,1)S(1)}, u32[]{:S(2)}, u32[]{:S(2)}) collective-permute-start(bf16[16,128,128]{2,1,0:T(8,128)(2,1)S(1)} %get-tuple-element.27), channel_id=1, source_target_pairs={{0,1},{1,0},{2,3},{3,2},{4,5},{5,4},{6,7},{7,6},{8,9},{9,8},{10,11... | collective-permute-start | bytes 1572872 | tf_op jit(solution)/shard_map/ppermute | solution.py:285
  73.4 17.3 %all-to-all-start = ((bf16[8,256,128]{2,1,0:T(8,128)(2,1)}), bf16[8,256,128]{2,1,0:T(8,128)(2,1)S(1)}, u32[]{:S(2)}, u32[]{:S(2)}) async-start(bf16[8,256,128]{2,1,0:T(8,128)(2,1)} %bitcast.12), calls=%async_computation | async-start | bytes 1048576 | tf_op jit(solution)/shard_map/all_to_all | solution.py:287
  79.4 0.7 copy-start.7
  80.3 0.7 copy-start.8
  81.0 0.8 copy-start.6
  81.7 8.9 %copy-start.1 = (bf16[1,256,128]{2,1,0:T(8,128)(2,1)S(1)}, bf16[1,256,128]{2,1,0:T(8,128)(2,1)}, u32[]{:S(2)}) copy-start(bf16[1,256,128]{2,1,0:T(8,128)(2,1)} %param.21) | copy-start | bytes 196612
  81.7 8.9 %copy-start.2 = (bf16[128,128]{1,0:T(8,128)(2,1)S(1)}, bf16[128,128]{1,0:T(8,128)(2,1)}, u32[]{:S(2)}) copy-start(bf16[128,128]{1,0:T(8,128)(2,1)} %weight.1) | copy-start | bytes 98308
  90.7 0.7 copy-start.5
  108.2 3.9 %collective-permute-start.5 = (bf16[8,304,128]{2,1,0:T(8,128)(2,1)S(1)}, bf16[8,304,128]{2,1,0:T(8,128)(2,1)S(1)}, u32[]{:S(2)}, u32[]{:S(2)}) collective-permute-start(bf16[8,304,128]{2,1,0:T(8,128)(2,1)S(1)} %all_to_all.20.got), channel_id=1, source_target_pairs={{0,1},{1,0},{2,3},{3,2},{4,5},{5,4},{6,7},{7,6},{8,9},{9,8},{10,11... | collective-permute-start | bytes 1867784 | tf_op jit(solution)/shard_map/ppermute | solution.py:307
  114.4 11.3 %collective-permute-start.9 = (bf16[1072,128]{1,0:T(8,128)(2,1)S(1)}, bf16[1072,128]{1,0:T(8,128)(2,1)S(1)}, u32[]{:S(2)}, u32[]{:S(2)}) collective-permute-start(bf16[1072,128]{1,0:T(8,128)(2,1)S(1)} %get-tuple-element.35), channel_id=1, source_target_pairs={{0,256},{16,272},{32,288},{48,304},{64,320},{80,336},{96,352},{112... | collective-permute-start | bytes 823304 | tf_op jit(solution)/shard_map/ppermute | solution.py:317
  117.8 18.5 %collective-permute-start.7 = (bf16[8,128,128]{2,1,0:T(8,128)(2,1)S(1)}, bf16[8,128,128]{2,1,0:T(8,128)(2,1)S(1)}, u32[]{:S(2)}, u32[]{:S(2)}) collective-permute-start(bf16[8,128,128]{2,1,0:T(8,128)(2,1)S(1)} %get-tuple-element.31), channel_id=1, source_target_pairs={{0,256},{16,272},{32,288},{48,304},{64,320},{80,336},{96,352},{112... | collective-permute-start | bytes 786440 | tf_op jit(solution)/shard_map/ppermute | solution.py:318
  120.3 16.7 %collective-permute-start.8 = (bf16[8,128,128]{2,1,0:T(8,128)(2,1)S(1)}, bf16[8,128,128]{2,1,0:T(8,128)(2,1)S(1)}, u32[]{:S(2)}, u32[]{:S(2)}) collective-permute-start(bf16[8,128,128]{2,1,0:T(8,128)(2,1)S(1)} %get-tuple-element.33), channel_id=1, source_target_pairs={{0,256},{16,272},{32,288},{48,304},{64,320},{80,336},{96,352},{112... | collective-permute-start | bytes 786440 | tf_op jit(solution)/shard_map/ppermute | solution.py:319
  125.8 11.2 %collective-permute-start.10 = (bf16[560,128]{1,0:T(8,128)(2,1)S(1)}, bf16[560,128]{1,0:T(8,128)(2,1)S(1)}, u32[]{:S(2)}, u32[]{:S(2)}) collective-permute-start(bf16[560,128]{1,0:T(8,128)(2,1)S(1)} %get-tuple-element.37), channel_id=1, source_target_pairs={{0,16},{16,32},{32,48},{48,64},{64,80},{80,96},{96,112},{112,128},... | collective-permute-start | bytes 430088 | tf_op jit(solution)/shard_map/ppermute | solution.py:325
  127.7 9.2 %collective-permute-start.11 = (bf16[560,128]{1,0:T(8,128)(2,1)S(1)}, bf16[560,128]{1,0:T(8,128)(2,1)S(1)}, u32[]{:S(2)}, u32[]{:S(2)}) collective-permute-start(bf16[560,128]{1,0:T(8,128)(2,1)S(1)} %get-tuple-element.38), channel_id=1, source_target_pairs={{0,240},{16,0},{32,16},{48,32},{64,48},{80,64},{96,80},{112,96},{1... | collective-permute-start | bytes 430088 | tf_op jit(solution)/shard_map/ppermute | solution.py:326
  132.9 13.9 %collective-permute-start.6 = (bf16[8,128,128]{2,1,0:T(8,128)(2,1)S(1)}, bf16[8,128,128]{2,1,0:T(8,128)(2,1)S(1)}, u32[]{:S(2)}, u32[]{:S(2)}) collective-permute-start(bf16[8,128,128]{2,1,0:T(8,128)(2,1)S(1)} %get-tuple-element.29), channel_id=1, source_target_pairs={{0,256},{16,272},{32,288},{48,304},{64,320},{80,336},{96,352},{112... | collective-permute-start | bytes 786440 | tf_op jit(solution)/shard_map/ppermute | solution.py:320
  137.7 13.7 %collective-permute-start.12 = (bf16[8,128,128]{2,1,0:T(8,128)(2,1)S(1)}, bf16[8,128,128]{2,1,0:T(8,128)(2,1)S(1)}, u32[]{:S(2)}, u32[]{:S(2)}) collective-permute-start(bf16[8,128,128]{2,1,0:T(8,128)(2,1)S(1)} %get-tuple-element.40), channel_id=1, source_target_pairs={{0,16},{16,32},{32,48},{48,64},{64,80},{80,96},{96,112},{112,128},... | collective-permute-start | bytes 786440 | tf_op jit(solution)/shard_map/ppermute | solution.py:334
  139.6 11.8 %collective-permute-start.13 = (bf16[8,128,128]{2,1,0:T(8,128)(2,1)S(1)}, bf16[8,128,128]{2,1,0:T(8,128)(2,1)S(1)}, u32[]{:S(2)}, u32[]{:S(2)}) collective-permute-start(bf16[8,128,128]{2,1,0:T(8,128)(2,1)S(1)} %get-tuple-element.41), channel_id=1, source_target_pairs={{0,240},{16,0},{32,16},{48,32},{64,48},{80,64},{96,80},{112,96},{1... | collective-permute-start | bytes 786440 | tf_op jit(solution)/shard_map/ppermute | solution.py:335
  144.7 6.6 %collective-permute-start.14 = (f32[48,128]{1,0:T(8,128)S(1)}, f32[48,128]{1,0:T(8,128)S(1)}, u32[]{:S(2)}, u32[]{:S(2)}) collective-permute-start(f32[48,128]{1,0:T(8,128)S(1)} %get-tuple-element.42.w), channel_id=1, source_target_pairs={{0,32},{16,48},{32,0},{48,16},{64,96},{80,112},{96,64},{112,80},{1... | collective-permute-start | bytes 73736 | tf_op jit(solution)/shard_map/ppermute | solution.py:336

commit v3 on v2

v3 whole, which is shorter than its diff:
```python
import jax
import jax.numpy as jnp
from jax import lax
from jax.experimental import pallas as pl
from jax.experimental.pallas import tpu as pltpu
from jax.sharding import Mesh
from jax.sharding import PartitionSpec as P

TILE = 128
Z = 16
NEAR = 4
FAR = Z // NEAR
WROWS = 32
BIAS_AT = 304
RING = ("q", "k")
PLANE = ("h", "y", "x")
NT = (((1,), (1,)), ((), ()))
TN = (((0,), (0,)), ((), ()))

VMEM_LIMIT = 48 * 1024 * 1024


def shift(v, d):
    return lax.ppermute(v, RING, [(z, (z + d) % Z) for z in range(Z)])


def other_core(v):
    return lax.ppermute(v, "core", [(0, 1), (1, 0)])


def swap(v):
    return lax.ppermute(v, ("x", "core"), [(0, 0), (1, 2), (2, 1), (3, 3)])


def vmem():
    return pl.BlockSpec(memory_space=pltpu.VMEM)


def smem():
    return pl.BlockSpec(memory_space=pltpu.SMEM)


def params():
    return pltpu.CompilerParams(vmem_limit_bytes=VMEM_LIMIT)


def bf(v):
    return v.astype(jnp.bfloat16)


def f32(v):
    return v.astype(jnp.float32)


def out(shape, dtype=jnp.bfloat16):
    return jax.ShapeDtypeStruct(shape, dtype)


def call(kernel, name, outs, scalars, arrays, scratch=()):
    return pl.pallas_call(
        kernel,
        out_shape=outs,
        in_specs=[smem()] * len(scalars) + [vmem()] * len(arrays),
        out_specs=jax.tree.map(lambda _: vmem(), outs),
        scratch_shapes=list(scratch),
        compiler_params=params(),
        name=name,
    )(*scalars, *arrays)


def split_col(col):
    return col // 32, (col // 8) % 4, (col // 2) % 4, col % 2


def forward_kernel(ints, here, a, own, nxt, prv, ha, hb, far_core, o, xs, acc):
    xs[0:8] = own[...]
    xs[8:16] = nxt[...]
    xs[16:24] = prv[...]
    xs[24:28] = ha[...]
    xs[28:32] = hb[...]
    xs[32:64] = far_core[...]
    acc[...] = jnp.zeros_like(acc)
    core, mine = here[0], here[1]
    n = ints[0, 64]
    group = 4
    for base in range(0, a.shape[0], group):
        prods = []
        for s in range(base, base + group):
            c, q, k, half = split_col(ints[0, 32 + s])
            rel = (k - mine + 4) % 4
            cls = jnp.where(rel == 2, 3, jnp.where(rel == 3, 2, rel))
            at = ((c + core) % 2) * 32 + cls * 8 + q * 2 + half
            prods.append(jnp.dot(a[s], xs[at], preferred_element_type=jnp.float32))
        for s, p in zip(range(base, base + group), prods):
            acc[jnp.where(s < n, ints[0, s], o.shape[0])] += p
    o[...] = bf(acc[0 : o.shape[0]])


def dense_kernel(parts, weight, exit_weight, bias, ints, up, sent, wb):
    total = f32(parts[0])
    for j in range(1, parts.shape[0]):
        total += f32(parts[j])
    agg = bf(total)
    w = weight[...]
    ew = exit_weight[...]
    pre = jnp.dot(agg, w, preferred_element_type=jnp.float32)
    sig = 1.0 / (1.0 + jnp.exp(-pre))
    act = bf(pre * sig)
    logits = jnp.dot(act, ew, preferred_element_type=jnp.float32) + bias[...]
    expd = jnp.exp(logits)
    probs = expd / jnp.sum(expd, axis=1, keepdims=True)
    ids = f32(lax.broadcasted_iota(jnp.int32, logits.shape, 1))
    columns = jnp.transpose(f32(ints[...]))
    labels = jnp.concatenate([columns[:, 1:2], columns[:, 2:3]], axis=0)
    mask = jnp.concatenate([columns[:, 3:4], columns[:, 4:5]], axis=0)
    onehot = f32(labels == ids)
    dlogits = bf(mask * (probs - onehot))
    dact = f32(up[...]) + lax.dot_general(
        dlogits, ew, NT, preferred_element_type=jnp.float32
    )
    dpre = bf(dact * sig * (1.0 + pre * (1.0 - sig)))
    dagg = bf(lax.dot_general(dpre, w, NT, preferred_element_type=jnp.float32))
    classes = ew.shape[1]
    wb[...] = jnp.zeros_like(wb)
    wb[0:TILE] = lax.dot_general(agg, dpre, TN, preferred_element_type=jnp.float32)
    wb[TILE : TILE + classes] = lax.dot_general(
        dlogits, act, TN, preferred_element_type=jnp.float32
    )
    bsum = jnp.sum(f32(dlogits), axis=0, keepdims=True)
    wb[BIAS_AT : BIAS_AT + 1] = bsum[:, 0:TILE]
    wb[BIAS_AT + 1 : BIAS_AT + 2, 0 : classes - TILE] = bsum[:, TILE:]
    nodes = dagg.shape[0]
    for j in range(sent.shape[0]):
        sent[j, 0:nodes] = dagg
        sent[j, nodes : nodes + WROWS] = bf(wb[j * WROWS : (j + 1) * WROWS])


def backward_kernel(ints, here, a, g, hu, rest, hv, rv, lv, ov, w, acc):
    nodes = 2 * TILE
    acc[...] = jnp.zeros_like(acc)
    core, mine = here[0], here[1]
    n = ints[0, 64]
    group = 4
    for base in range(0, a.shape[0], group):
        prods = []
        for s in range(base, base + group):
            t = ints[0, s]
            start = pl.multiple_of((t % 2) * TILE, TILE)
            gb = g[t // 2, pl.ds(start, TILE), :]
            prods.append(lax.dot_general(a[s], gb, TN, preferred_element_type=jnp.float32))
        for s, p in zip(range(base, base + group), prods):
            c, q, k, half = split_col(ints[0, 32 + s])
            at = ((c + core) % 2) * 32 + ((k - mine + 4) % 4) * 8 + q * 2 + half
            acc[jnp.where(s < n, at, 64)] += p
    ov[...] = bf(acc[0:8])
    rv[...] = bf(acc[8:16])
    hv[...] = bf(acc[16:24])
    lv[...] = bf(acc[24:32])
    rest[0:16] = bf(acc[32:48])
    rest[16:24] = bf(acc[56:64])
    total = f32(g[0, nodes : nodes + WROWS])
    for j in range(1, g.shape[0]):
        total += f32(g[j, nodes : nodes + WROWS])
    ws = bf(total)
    for i in range(8):
        hu[i * TILE : (i + 1) * TILE] = bf(acc[48 + i])
    hu[8 * TILE : 8 * TILE + WROWS] = ws
    w[...] = ws


def fold1_kernel(hv, xh, w, a, b, ow):
    for i in range(4):
        rows = slice(i * TILE, (i + 1) * TILE)
        a[rows] = bf(f32(hv[i]) + f32(xh[rows]))
        b[rows] = bf(f32(hv[4 + i]) + f32(xh[(4 + i) * TILE : (5 + i) * TILE]))
    ws = bf(f32(w[...]) + f32(xh[8 * TILE : 8 * TILE + WROWS]))
    a[4 * TILE : 4 * TILE + WROWS] = ws
    b[4 * TILE : 4 * TILE + WROWS] = ws
    ow[...] = ws


def fold2_kernel(here, rv, lv, xs, ra, rb, w, r, l, ow):
    for i in range(4):
        rows = slice(i * TILE, (i + 1) * TILE)
        r[i] = bf(f32(rv[i]) + f32(xs[8 + i]) + f32(ra[rows]))
        l[4 + i] = bf(f32(lv[4 + i]) + f32(xs[20 + i]) + f32(rb[rows]))
        r[4 + i] = bf(f32(rv[4 + i]) + f32(xs[12 + i]))
        l[i] = bf(f32(lv[i]) + f32(xs[16 + i]))
    tail = slice(4 * TILE, 4 * TILE + WROWS)
    partner = jnp.where(here[1] % 2 == 1, f32(ra[tail]), f32(rb[tail]))
    ow[...] = f32(w[...]) + partner


def join_kernel(ov, xs, rn, rp, w, rw, o):
    ws = bf(w[...] + rw[...])
    for j in range(FAR):
        for h in range(2):
            i = 2 * j + h
            s = f32(ov[i]) + f32(xs[i]) + f32(rn[i]) + f32(rp[i])
            o[j, h * TILE : (h + 1) * TILE] = bf(s)
        o[j, 2 * TILE : 2 * TILE + WROWS] = ws


def finish_kernel(parts, o, w):
    total = f32(parts[0])
    for j in range(1, parts.shape[0]):
        total += f32(parts[j])
    nodes = o.shape[0]
    o[...] = bf(total[0:nodes])
    for j in range(w.shape[0]):
        w[j] = total[nodes : nodes + WROWS]


def unpack_kernel(scale, wall, layer, exit_t, bias, wb):
    for j in range(wall.shape[0]):
        wb[j * WROWS : (j + 1) * WROWS] = wall[j] * scale[0]
    classes = exit_t.shape[0]
    layer[...] = wb[0:TILE]
    exit_t[...] = wb[TILE : TILE + classes]
    bias[:, 0:TILE] = wb[BIAS_AT : BIAS_AT + 1]
    bias[:, TILE:classes] = wb[BIAS_AT + 1 : BIAS_AT + 2, 0 : classes - TILE]


def local(
    features,
    tile_rows,
    tile_cols,
    tile_count,
    tile_values,
    weight,
    exit_weight,
    exit_bias,
    labels,
    label_mask,
    upstream,
):
    hidden = features.shape[-1]
    classes = exit_weight.shape[1]
    nodes = features.shape[1]
    slots = tile_rows.shape[-1]
    plane = 16
    nodes_total = nodes * 2 * Z * plane
    scale = jnp.full((1,), float(nodes_total) ** (-0.5), jnp.float32)
    here = jnp.stack([lax.axis_index("core"), lax.axis_index("k")]).astype(jnp.int32)

    def blocks(v):
        return v.reshape(-1, TILE, hidden)

    def acc(n):
        return pltpu.VMEM((n, TILE, hidden), jnp.float32)

    feats = swap(features[0])
    ints = jnp.concatenate(
        [
            tile_rows.reshape(slots),
            tile_cols.reshape(slots),
            tile_count.reshape(1),
            jnp.zeros((TILE - 2 * slots - 1,), jnp.int32),
            labels.reshape(nodes),
            label_mask.reshape(nodes),
            jnp.zeros((3 * TILE,), jnp.int32),
        ]
    ).reshape(8, TILE)
    ints = swap(ints)
    values = swap(tile_values[0, 0])
    up = swap(upstream[0])

    far = lax.all_gather(feats, "q", axis=0)
    nxt = shift(far, -1)
    prv = shift(far, 1)
    ha = shift(far[: FAR // 2], -2)
    hb = shift(far[FAR // 2 :], 2)
    mine = [blocks(v) for v in (far, nxt, prv, ha, hb)]
    across = other_core(jnp.concatenate(mine, axis=0))

    partial_value = call(
        forward_kernel,
        "forward_products",
        out((2 * plane, TILE, hidden)),
        (ints, here),
        (values, *mine, across),
        (pltpu.VMEM((64, TILE, hidden), jnp.bfloat16), acc(2 * plane + 1)),
    )
    parts = lax.all_to_all(
        partial_value.reshape(plane, nodes, hidden), PLANE, 0, 0, tiled=True
    )
    sent = call(
        dense_kernel,
        "dense",
        out((plane, nodes + WROWS, hidden)),
        (),
        (parts, weight, exit_weight, exit_bias.reshape(1, classes), ints, up),
        (pltpu.VMEM((plane * WROWS, hidden), jnp.float32),),
    )
    got = lax.all_to_all(sent, PLANE, 0, 0, tiled=True)
    half = out((8, TILE, hidden))
    hu, rest, hv, rv, lv, ov, w = call(
        backward_kernel,
        "backward_products",
        (
            out((8 * TILE + WROWS, hidden)),
            out((24, TILE, hidden)),
            half,
            half,
            half,
            half,
            out((WROWS, hidden)),
        ),
        (ints, here),
        (values, got),
        (acc(65),),
    )

    xh = other_core(hu)
    xs = other_core(rest)
    side = out((4 * TILE + WROWS, hidden))
    a, b, w = call(
        fold1_kernel, "fold1", (side, side, out((WROWS, hidden))), (), (hv, xh, w)
    )
    ra = shift(a, 1)
    rb = shift(b, -1)
    rr, ll, w = call(
        fold2_kernel,
        "fold2",
        (half, half, out((WROWS, hidden), jnp.float32)),
        (here,),
        (rv, lv, xs, ra, rb, w),
    )
    rn = shift(rr, 1)
    rp = shift(ll, -1)
    rw = lax.ppermute(w, "k", [(k, k ^ 2) for k in range(NEAR)])
    joined = call(
        join_kernel,
        "join",
        out((FAR, nodes + WROWS, hidden)),
        (),
        (ov, xs, rn, rp, w, rw),
    )
    last = lax.all_to_all(joined, "q", 0, 0, tiled=True)
    grad_input, wsum = call(
        finish_kernel,
        "finish",
        (out((nodes, hidden)), out((plane, WROWS, hidden), jnp.float32)),
        (),
        (last,),
    )
    grad_input = swap(grad_input)
    wall = lax.all_to_all(wsum, PLANE, 0, 0, tiled=True)
    layer_total, exit_t, bias_total = call(
        unpack_kernel,
        "unpack",
        (
            out((TILE, hidden), jnp.float32),
            out((classes, hidden), jnp.float32),
            out((1, classes), jnp.float32),
        ),
        (scale,),
        (wall,),
        (pltpu.VMEM((plane * WROWS, hidden), jnp.float32),),
    )
    return (grad_input[None], layer_total, exit_t.T, bias_total.reshape(classes))


def solution(mesh):
    fine = Mesh(
        mesh.devices.reshape(2, FAR, NEAR, 2, 4, 2), ("x", "q", "k", "h", "y", "core")
    )
    row, col = ("x", "q", "k"), ("h", "y", "core")
    in_specs = (
        P(col, row, None),
        P(row, col, None),
        P(row, col, None),
        P(row, col),
        P(row, col, None, None, None),
        P(),
        P(),
        P(),
        P(row, col),
        P(row, col),
        P(row, col, None),
    )
    out_specs = (P(col, row, None), P(), P(), P())
    return jax.shard_map(local, mesh=fine, in_specs=in_specs, out_specs=out_specs, check_vma=False)
```

time: 190 us -> 189 us (level)
  the two profiles are of different devices: /device:TPU:2 before, /device:TPU:32 now
where the time goes in v3:
time: 189 us; the launch traced here: 188 us
  blocking collectives  75.1 us (40%)
  starting transfers between devices  56.8 us (30%)
  waiting for transfers between devices  42.2 us (22%)
  Pallas kernels  8.12 us (4%)
  local copies, waits for them, and re-layouts  4.36 us (2%)
    all_to_all x1, blocking collectives, local(): last = lax.all_to_all(joined, 'q', 0, 0, tiled=True)  27.1 us
    all_gather x1, blocking collectives, local(): far = lax.all_gather(feats, 'q', axis=0)  25.4 us
    ppermute x8, starting transfers between devices, shift(): return lax.ppermute(v, RING, [(z, (z + d) % Z) for z in range(Z)])  24.4 us
    all_to_all x1, blocking collectives, local(): got = lax.all_to_all(sent, PLANE, 0, 0, tiled=True)  22.6 us
    all_to_all x1, waiting for transfers between devices, local(): lax.all_to_all(partial_value.reshape(plane, nodes, hidden), PLANE, 0, 0,...  17.1 us
    ppermute x8, waiting for transfers between devices, shift(): return lax.ppermute(v, RING, [(z, (z + d) % Z) for z in range(Z)])  11.3 us
    all_to_all x1, starting transfers between devices, local(): lax.all_to_all(partial_value.reshape(plane, nodes, hidden), PLANE, 0, 0,...  10.8 us
    pallas_call x8, Pallas kernels, call(): pl.pallas_call(kernel, out_shape=outs, in_specs=[smem()] * len(scalars) +...  8.12 us
  transfers between devices with their start and end apart: 19, of which 9 were waited for; matrix products, arithmetic and copies ran while one was open for 2% of the time, Pallas kernels for 0%

profile of v3, /device:TPU:32, one launch (start us, length us, event | category | flops | bytes accessed | tf_op | source)
XLA Modules:
  0.0 188.2 jit_solution(2104654572980425840)
XLA Ops:
  0.6 1.5 collective-permute-start.2
  2.1 1.9 collective-permute-start.1
  4.0 25.4 %all-gather = bf16[1024,128]{1,0:T(8,128)(2,1)S(1)} all-gather(bf16[256,128]{1,0:T(8,128)(2,1)S(1)} %collective-permute-done.2), channel_id=2, replica_groups=mesh['x'=2,'q'=4,'k'=4,'h'=2,'y'=4,'core'=2] {'q'}, dimensions={0}, use_global_device_ids=true | all-gather | bytes 327680 | tf_op jit(solution)/shard_map/all_gather | solution.py:268
  29.4 3.0 %collective-permute-start.3 = (bf16[4,256,128]{2,1,0:T(8,128)(2,1)S(1)}, bf16[4,256,128]{2,1,0:T(8,128)(2,1)S(1)}, u32[]{:S(2)}, u32[]{:S(2)}) collective-permute-start(bf16[4,256,128]{2,1,0:T(8,128)(2,1)S(1)} %bitcast.25), channel_id=1, source_target_pairs={{0,240},{16,0},{32,16},{48,32},{64,48},{80,64},{96,80},{112,96},{1... | collective-permute-start | bytes 786440 | tf_op jit(solution)/shard_map/ppermute | solution.py:24
  32.4 2.9 %collective-permute-start.4 = (bf16[4,256,128]{2,1,0:T(8,128)(2,1)S(1)}, bf16[4,256,128]{2,1,0:T(8,128)(2,1)S(1)}, u32[]{:S(2)}, u32[]{:S(2)}) collective-permute-start(bf16[4,256,128]{2,1,0:T(8,128)(2,1)S(1)} %bitcast.26), channel_id=1, source_target_pairs={{0,16},{16,32},{32,48},{48,64},{64,80},{80,96},{96,112},{112,128},... | collective-permute-start | bytes 786440 | tf_op jit(solution)/shard_map/ppermute | solution.py:24
  35.4 4.8 %collective-permute-start.5 = (bf16[2,256,128]{2,1,0:T(8,128)(2,1)S(1)}, bf16[2,256,128]{2,1,0:T(8,128)(2,1)S(1)}, u32[]{:S(2)}, u32[]{:S(2)}) collective-permute-start(bf16[2,256,128]{2,1,0:T(8,128)(2,1)S(1)} %bitcast.39), channel_id=1, source_target_pairs={{0,224},{16,240},{32,0},{48,16},{64,32},{80,48},{96,64},{112,80},{... | collective-permute-start | bytes 393224 | tf_op jit(solution)/shard_map/ppermute | solution.py:24
  40.1 2.1 %collective-permute-start.6 = (bf16[2,256,128]{2,1,0:T(8,128)(2,1)S(1)}, bf16[2,256,128]{2,1,0:T(8,128)(2,1)S(1)}, u32[]{:S(2)}, u32[]{:S(2)}) collective-permute-start(bf16[2,256,128]{2,1,0:T(8,128)(2,1)S(1)} %bitcast.38), channel_id=1, source_target_pairs={{0,32},{16,48},{32,64},{48,80},{64,96},{80,112},{96,128},{112,144}... | collective-permute-start | bytes 393224 | tf_op jit(solution)/shard_map/ppermute | solution.py:24
  44.4 3.1 %collective-permute-done.5 = bf16[2,256,128]{2,1,0:T(8,128)(2,1)S(1)} collective-permute-done((bf16[2,256,128]{2,1,0:T(8,128)(2,1)S(1)}, bf16[2,256,128]{2,1,0:T(8,128)(2,1)S(1)}, u32[]{:S(2)}, u32[]{:S(2)}) %collective-permute-start.5) | collective-permute-done | bytes 131104 | tf_op jit(solution)/shard_map/ppermute | solution.py:24
  48.1 4.3 %collective-permute-done.6 = bf16[2,256,128]{2,1,0:T(8,128)(2,1)S(1)} collective-permute-done((bf16[2,256,128]{2,1,0:T(8,128)(2,1)S(1)}, bf16[2,256,128]{2,1,0:T(8,128)(2,1)S(1)}, u32[]{:S(2)}, u32[]{:S(2)}) %collective-permute-start.6) | collective-permute-done | bytes 131104 | tf_op jit(solution)/shard_map/ppermute | solution.py:24
  53.1 2.0 %collective-permute-start.7 = (bf16[32,128,128]{2,1,0:T(8,128)(2,1)}, bf16[32,128,128]{2,1,0:T(8,128)(2,1)S(1)}, u32[]{:S(2)}, u32[]{:S(2)}) collective-permute-start(bf16[32,128,128]{2,1,0:T(8,128)(2,1)} %constant_dynamic-update-slice_fusion), channel_id=1, source_target_pairs={{0,1},{1,0},{2,3},{3,2},{4,5},{5,4},{6,7},{7,6},{8,9},{9,8},{10,11... | collective-permute-start | bytes 3145736 | tf_op jit(solution)/shard_map/ppermute | solution.py:28
  56.7 1.2 collective-permute-done.7.far_core
  57.9 2.7 %forward_products.1 = bf16[32,128,128]{2,1,0:T(8,128)(2,1)} custom-call(s32[8,128]{1,0:T(8,128)S(1)} %collective-permute-done.ints, s32[2]{0:T(128)S(1)} %pad_add_fusion.here, bf16[32,128,128]{2,1,0:T(8,128)(2,1)S(1)} %collective-permute-done.1.a, bf16[8,128,128]{2,1,0:T(8,128)(2,1)S(1)} %bitcast.28, bf16[8,128,128]{2,1,0:T(8,128)(2,1)S(1)} %bitcast.30, ...), custom_call_target="tpu_custom_call" | custom-call | tf_op jit(solution)/shard_map/forward_products/pallas_call | solution.py:60
  60.6 10.8 %all-to-all-start = ((bf16[16,256,128]{2,1,0:T(8,128)(2,1)}), bf16[16,256,128]{2,1,0:T(8,128)(2,1)S(1)}, u32[]{:S(2)}, u32[]{:S(2)}) async-start(bf16[16,256,128]{2,1,0:T(8,128)(2,1)} %bitcast.18), calls=%async_computation | async-start | bytes 2097152 | tf_op jit(solution)/shard_map/all_to_all | solution.py:284
  72.2 17.1 %all-to-all-done.parts = bf16[16,256,128]{2,1,0:T(8,128)(2,1)S(1)} async-done(((bf16[16,256,128]{2,1,0:T(8,128)(2,1)}), bf16[16,256,128]{2,1,0:T(8,128)(2,1)S(1)}, u32[]{:S(2)}, u32[]{:S(2)}) %all-to-all-start) | async-done | bytes 1048608 | tf_op jit(solution)/shard_map/all_to_all | solution.py:284
  89.3 0.9 dense.1
  90.2 22.6 %all_to_all.20.g = bf16[16,288,128]{2,1,0:T(8,128)(2,1)S(1)} all-to-all(bf16[16,288,128]{2,1,0:T(8,128)(2,1)S(1)} %dense.1), channel_id=1, replica_groups=mesh['x'=2,'q'=4,'k'=4,'h'=2,'y'=4,'core'=2] {'h','y','x'}, dimensions={0} | all-to-all | bytes 2359296 | tf_op jit(solution)/shard_map/all_to_all | solution.py:295
  112.8 2.2 %backward_products.1 = (bf16[1056,128]{1,0:T(8,128)(2,1)S(1)}, bf16[24,128,128]{2,1,0:T(8,128)(2,1)S(1)}, bf16[8,128,128]{2,1,0:T(8,128)(2,1)S(1)}, bf16[8,128,1...) custom-call(s32[8,128]{1,0:T(8,128)S(1)} %collective-permute-done.in, ...), custom_call_target="tpu_custom_call" | custom-call | tf_op jit(solution)/shard_map/backward_products/pallas_call | solution.py:60
  115.0 1.9 %collective-permute-start.9 = (bf16[24,128,128]{2,1,0:T(8,128)(2,1)S(1)}, bf16[24,128,128]{2,1,0:T(8,128)(2,1)S(1)}, u32[]{:S(2)}, u32[]{:S(2)}) collective-permute-start(bf16[24,128,128]{2,1,0:T(8,128)(2,1)S(1)} %get-tuple-element.23), channel_id=1, source_target_pairs={{0,1},{1,0},{2,3},{3,2},{4,5},{5,4},{6,7},{7,6},{8,9},{9,8},{10,11... | collective-permute-start | bytes 2359304 | tf_op jit(solution)/shard_map/ppermute | solution.py:28
  116.9 2.4 %collective-permute-start.10 = (bf16[1056,128]{1,0:T(8,128)(2,1)S(1)}, bf16[1056,128]{1,0:T(8,128)(2,1)S(1)}, u32[]{:S(2)}, u32[]{:S(2)}) collective-permute-start(bf16[1056,128]{1,0:T(8,128)(2,1)S(1)} %get-tuple-element.27), channel_id=1, source_target_pairs={{0,1},{1,0},{2,3},{3,2},{4,5},{5,4},{6,7},{7,6},{8,9},{9,8},{10,11... | collective-permute-start | bytes 811016 | tf_op jit(solution)/shard_map/ppermute | solution.py:28
  119.3 1.2 collective-permute-done.10.xh
  120.6 1.9 %collective-permute-start.11 = (bf16[544,128]{1,0:T(8,128)(2,1)S(1)}, bf16[544,128]{1,0:T(8,128)(2,1)S(1)}, u32[]{:S(2)}, u32[]{:S(2)}) collective-permute-start(bf16[544,128]{1,0:T(8,128)(2,1)S(1)} %get-tuple-element.29), channel_id=1, source_target_pairs={{0,16},{16,32},{32,48},{48,64},{64,80},{80,96},{96,112},{112,128},... | collective-permute-start | bytes 417800 | tf_op jit(solution)/shard_map/ppermute | solution.py:24
  122.5 3.9 %collective-permute-start.12 = (bf16[544,128]{1,0:T(8,128)(2,1)S(1)}, bf16[544,128]{1,0:T(8,128)(2,1)S(1)}, u32[]{:S(2)}, u32[]{:S(2)}) collective-permute-start(bf16[544,128]{1,0:T(8,128)(2,1)S(1)} %get-tuple-element.30), channel_id=1, source_target_pairs={{0,240},{16,0},{32,16},{48,32},{64,48},{80,64},{96,80},{112,96},{1... | collective-permute-start | bytes 417800 | tf_op jit(solution)/shard_map/ppermute | solution.py:24
  126.4 2.0 %collective-permute-done.11.ra = bf16[544,128]{1,0:T(8,128)(2,1)S(1)} collective-permute-done((bf16[544,128]{1,0:T(8,128)(2,1)S(1)}, bf16[544,128]{1,0:T(8,128)(2,1)S(1)}, u32[]{:S(2)}, u32[]{:S(2)}) %collective-permute-start.11) | collective-permute-done | bytes 139296 | tf_op jit(solution)/shard_map/ppermute | solution.py:24
  128.4 1.9 %collective-permute-done.12.rb = bf16[544,128]{1,0:T(8,128)(2,1)S(1)} collective-permute-done((bf16[544,128]{1,0:T(8,128)(2,1)S(1)}, bf16[544,128]{1,0:T(8,128)(2,1)S(1)}, u32[]{:S(2)}, u32[]{:S(2)}) %collective-permute-start.12) | collective-permute-done | bytes 139296 | tf_op jit(solution)/shard_map/ppermute | solution.py:24
  131.1 3.9 %collective-permute-start.13 = (bf16[8,128,128]{2,1,0:T(8,128)(2,1)S(1)}, bf16[8,128,128]{2,1,0:T(8,128)(2,1)S(1)}, u32[]{:S(2)}, u32[]{:S(2)}) collective-permute-start(bf16[8,128,128]{2,1,0:T(8,128)(2,1)S(1)} %get-tuple-element.32), channel_id=1, source_target_pairs={{0,16},{16,32},{32,48},{48,64},{64,80},{80,96},{96,112},{112,128},... | collective-permute-start | bytes 786440 | tf_op jit(solution)/shard_map/ppermute | solution.py:24
  135.0 1.9 %collective-permute-start.14 = (bf16[8,128,128]{2,1,0:T(8,128)(2,1)S(1)}, bf16[8,128,128]{2,1,0:T(8,128)(2,1)S(1)}, u32[]{:S(2)}, u32[]{:S(2)}) collective-permute-start(bf16[8,128,128]{2,1,0:T(8,128)(2,1)S(1)} %get-tuple-element.33), channel_id=1, source_target_pairs={{0,240},{16,0},{32,16},{48,32},{64,48},{80,64},{96,80},{112,96},{1... | collective-permute-start | bytes 786440 | tf_op jit(solution)/shard_map/ppermute | solution.py:24
  136.9 6.3 %collective-permute-start.15 = (f32[32,128]{1,0:T(8,128)S(1)}, f32[32,128]{1,0:T(8,128)S(1)}, u32[]{:S(2)}, u32[]{:S(2)}) collective-permute-start(f32[32,128]{1,0:T(8,128)S(1)} %get-tuple-element.34.w), channel_id=1, source_target_pairs={{0,32},{16,48},{32,0},{48,16},{1,33},{17,49},{33,1},{49,17},{2,34}... | collective-permute-start | bytes 49160 | tf_op jit(solution)/shard_map/ppermute | solution.py:331
  143.2 3.6 %collective-permute-done.15.rw = f32[32,128]{1,0:T(8,128)S(1)} collective-permute-done((f32[32,128]{1,0:T(8,128)S(1)}, f32[32,128]{1,0:T(8,128)S(1)}, u32[]{:S(2)}, u32[]{:S(2)}) %collective-permute-start.15) | collective-permute-done | bytes 16416 | tf_op jit(solution)/shard_map/ppermute | solution.py:331
  146.9 27.1 %all_to_all.21.parts = bf16[4,288,128]{2,1,0:T(8,128)(2,1)S(1)} all-to-all(bf16[4,288,128]{2,1,0:T(8,128)(2,1)S(1)} %join.1), channel_id=1, replica_groups=mesh['x'=2,'q'=4,'k'=4,'h'=2,'y'=4,'core'=2] {'q'}, dimensions={0} | all-to-all | bytes 589824 | tf_op jit(solution)/shard_map/all_to_all | solution.py:339
  174.0 0.7 finish.1
  174.8 3.5 %all-to-all-start.3 = ((f32[16,32,128]{2,1,0:T(8,128)}), f32[16,32,128]{2,1,0:T(8,128)S(1)}, u32[]{:S(2)}, u32[]{:S(2)}) async-start(f32[16,32,128]{2,1,0:T(8,128)} %get-tuple-element.36), calls=%async_computation.3 | async-start | bytes 524288 | tf_op jit(solution)/shard_map/all_to_all | solution.py:348
  179.0 8.0 %all-to-all-done.3.wall = f32[16,32,128]{2,1,0:T(8,128)S(1)} async-done(((f32[16,32,128]{2,1,0:T(8,128)}), f32[16,32,128]{2,1,0:T(8,128)S(1)}, u32[]{:S(2)}, u32[]{:S(2)}) %all-to-all-start.3) | async-done | bytes 262176 | tf_op jit(solution)/shard_map/all_to_all | solution.py:348
  (45 shorter events, 8.0 us)
Async XLA Ops:
  0.6 3.4 %collective-permute-start.2 = (bf16[256,128]{1,0:T(8,128)(2,1)}, bf16[256,128]{1,0:T(8,128)(2,1)S(1)}, u32[]{:S(2)}, u32[]{:S(2)}) collective-permute-start(bf16[256,128]{1,0:T(8,128)(2,1)} %bitcast.48), channel_id=1, source_target_pairs={{0,0},{1,256},{256,1},{257,257},{2,2},{3,258},{258,3},{259,259},{4... | collective-permute-start | bytes 196616 | tf_op jit(solution)/shard_map/ppermute | solution.py:32
  2.1 54.5 %collective-permute-start.1 = (bf16[32,128,128]{2,1,0:T(8,128)(2,1)}, bf16[32,128,128]{2,1,0:T(8,128)(2,1)S(1)}, u32[]{:S(2)}, u32[]{:S(2)}) collective-permute-start(bf16[32,128,128]{2,1,0:T(8,128)(2,1)} %bitcast.46), channel_id=1, source_target_pairs={{0,0},{1,256},{256,1},{257,257},{2,2},{3,258},{258,3},{259,259},{4... | collective-permute-start | bytes 3145736 | tf_op jit(solution)/shard_map/ppermute | solution.py:32
  29.4 13.5 %collective-permute-start.3 = (bf16[4,256,128]{2,1,0:T(8,128)(2,1)S(1)}, bf16[4,256,128]{2,1,0:T(8,128)(2,1)S(1)}, u32[]{:S(2)}, u32[]{:S(2)}) collective-permute-start(bf16[4,256,128]{2,1,0:T(8,128)(2,1)S(1)} %bitcast.25), channel_id=1, source_target_pairs={{0,240},{16,0},{32,16},{48,32},{64,48},{80,64},{96,80},{112,96},{1... | collective-permute-start | bytes 786440 | tf_op jit(solution)/shard_map/ppermute | solution.py:24
  32.4 11.3 %collective-permute-start.4 = (bf16[4,256,128]{2,1,0:T(8,128)(2,1)S(1)}, bf16[4,256,128]{2,1,0:T(8,128)(2,1)S(1)}, u32[]{:S(2)}, u32[]{:S(2)}) collective-permute-start(bf16[4,256,128]{2,1,0:T(8,128)(2,1)S(1)} %bitcast.26), channel_id=1, source_target_pairs={{0,16},{16,32},{32,48},{48,64},{64,80},{80,96},{96,112},{112,128},... | collective-permute-start | bytes 786440 | tf_op jit(solution)/shard_map/ppermute | solution.py:24
  35.3 20.5 %copy-start.3 = (s32[1,256]{1,0:T(1,128)S(1)}, s32[1,256]{1,0:T(1,128)}, u32[]{:S(2)}) copy-start(s32[1,256]{1,0:T(1,128)} %param.19) | copy-start | bytes 3076
  35.3 20.5 %copy-start.4 = (s32[1,256]{1,0:T(1,128)S(1)}, s32[1,256]{1,0:T(1,128)}, u32[]{:S(2)}) copy-start(s32[1,256]{1,0:T(1,128)} %param.20) | copy-start | bytes 3076
  35.3 20.5 %copy-start.5 = (s32[1,1,32]{2,1,0:T(1,128)S(1)}, s32[1,1,32]{2,1,0:T(1,128)}, u32[]{:S(2)}) copy-start(s32[1,1,32]{2,1,0:T(1,128)} %param.12) | copy-start | bytes 388
  35.4 20.5 %copy-start.6 = (s32[1,1,32]{2,1,0:T(1,128)S(1)}, s32[1,1,32]{2,1,0:T(1,128)}, u32[]{:S(2)}) copy-start(s32[1,1,32]{2,1,0:T(1,128)} %param.13) | copy-start | bytes 388
  35.4 12.1 %collective-permute-start.5 = (bf16[2,256,128]{2,1,0:T(8,128)(2,1)S(1)}, bf16[2,256,128]{2,1,0:T(8,128)(2,1)S(1)}, u32[]{:S(2)}, u32[]{:S(2)}) collective-permute-start(bf16[2,256,128]{2,1,0:T(8,128)(2,1)S(1)} %bitcast.39), channel_id=1, source_target_pairs={{0,224},{16,240},{32,0},{48,16},{64,32},{80,48},{96,64},{112,80},{... | collective-permute-start | bytes 393224 | tf_op jit(solution)/shard_map/ppermute | solution.py:24
  40.1 12.3 %collective-permute-start.6 = (bf16[2,256,128]{2,1,0:T(8,128)(2,1)S(1)}, bf16[2,256,128]{2,1,0:T(8,128)(2,1)S(1)}, u32[]{:S(2)}, u32[]{:S(2)}) collective-permute-start(bf16[2,256,128]{2,1,0:T(8,128)(2,1)S(1)} %bitcast.38), channel_id=1, source_target_pairs={{0,32},{16,48},{32,64},{48,80},{64,96},{80,112},{96,128},{112,144}... | collective-permute-start | bytes 393224 | tf_op jit(solution)/shard_map/ppermute | solution.py:24
  53.1 4.8 %collective-permute-start.7 = (bf16[32,128,128]{2,1,0:T(8,128)(2,1)}, bf16[32,128,128]{2,1,0:T(8,128)(2,1)S(1)}, u32[]{:S(2)}, u32[]{:S(2)}) collective-permute-start(bf16[32,128,128]{2,1,0:T(8,128)(2,1)} %constant_dynamic-update-slice_fusion), channel_id=1, source_target_pairs={{0,1},{1,0},{2,3},{3,2},{4,5},{5,4},{6,7},{7,6},{8,9},{9,8},{10,11... | collective-permute-start | bytes 3145736 | tf_op jit(solution)/shard_map/ppermute | solution.py:28
  55.9 0.7 collective-permute-start
  60.6 10.9 %copy-start.7 = (bf16[1,256,128]{2,1,0:T(8,128)(2,1)S(1)}, bf16[1,256,128]{2,1,0:T(8,128)(2,1)}, u32[]{:S(2)}) copy-start(bf16[1,256,128]{2,1,0:T(8,128)(2,1)} %param.21) | copy-start | bytes 196612
  60.6 11.5 %copy-start.2 = (bf16[128,172]{0,1:T(8,128)(2,1)S(1)}, bf16[128,172]{0,1:T(8,128)(2,1)}, u32[]{:S(2)}) copy-start(bf16[128,172]{0,1:T(8,128)(2,1)} %param.17) | copy-start | bytes 132100
  60.6 28.7 %copy-start = (bf16[128,128]{1,0:T(8,128)(2,1)S(1)}, bf16[128,128]{1,0:T(8,128)(2,1)}, u32[]{:S(2)}) copy-start(bf16[128,128]{1,0:T(8,128)(2,1)} %weight.1) | copy-start | bytes 98308
  60.6 28.7 %copy-start.1 = (f32[172]{0:T(256)S(1)}, f32[172]{0:T(256)}, u32[]{:S(2)}) copy-start(f32[172]{0:T(256)} %param.18) | copy-start | bytes 2068
  60.6 28.7 %all-to-all-start = ((bf16[16,256,128]{2,1,0:T(8,128)(2,1)}), bf16[16,256,128]{2,1,0:T(8,128)(2,1)S(1)}, u32[]{:S(2)}, u32[]{:S(2)}) async-start(bf16[16,256,128]{2,1,0:T(8,128)(2,1)} %bitcast.18), calls=%async_computation | async-start | bytes 2097152 | tf_op jit(solution)/shard_map/all_to_all | solution.py:284
  71.4 0.8 collective-permute-start.8
  115.0 15.3 %collective-permute-start.9 = (bf16[24,128,128]{2,1,0:T(8,128)(2,1)S(1)}, bf16[24,128,128]{2,1,0:T(8,128)(2,1)S(1)}, u32[]{:S(2)}, u32[]{:S(2)}) collective-permute-start(bf16[24,128,128]{2,1,0:T(8,128)(2,1)S(1)} %get-tuple-element.23), channel_id=1, source_target_pairs={{0,1},{1,0},{2,3},{3,2},{4,5},{5,4},{6,7},{7,6},{8,9},{9,8},{10,11... | collective-permute-start | bytes 2359304 | tf_op jit(solution)/shard_map/ppermute | solution.py:28
  116.9 3.6 %collective-permute-start.10 = (bf16[1056,128]{1,0:T(8,128)(2,1)S(1)}, bf16[1056,128]{1,0:T(8,128)(2,1)S(1)}, u32[]{:S(2)}, u32[]{:S(2)}) collective-permute-start(bf16[1056,128]{1,0:T(8,128)(2,1)S(1)} %get-tuple-element.27), channel_id=1, source_target_pairs={{0,1},{1,0},{2,3},{3,2},{4,5},{5,4},{6,7},{7,6},{8,9},{9,8},{10,11... | collective-permute-start | bytes 811016 | tf_op jit(solution)/shard_map/ppermute | solution.py:28
  120.6 7.8 %collective-permute-start.11 = (bf16[544,128]{1,0:T(8,128)(2,1)S(1)}, bf16[544,128]{1,0:T(8,128)(2,1)S(1)}, u32[]{:S(2)}, u32[]{:S(2)}) collective-permute-start(bf16[544,128]{1,0:T(8,128)(2,1)S(1)} %get-tuple-element.29), channel_id=1, source_target_pairs={{0,16},{16,32},{32,48},{48,64},{64,80},{80,96},{96,112},{112,128},... | collective-permute-start | bytes 417800 | tf_op jit(solution)/shard_map/ppermute | solution.py:24
  122.5 7.8 %collective-permute-start.12 = (bf16[544,128]{1,0:T(8,128)(2,1)S(1)}, bf16[544,128]{1,0:T(8,128)(2,1)S(1)}, u32[]{:S(2)}, u32[]{:S(2)}) collective-permute-start(bf16[544,128]{1,0:T(8,128)(2,1)S(1)} %get-tuple-element.30), channel_id=1, source_target_pairs={{0,240},{16,0},{32,16},{48,32},{64,48},{80,64},{96,80},{112,96},{1... | collective-permute-start | bytes 417800 | tf_op jit(solution)/shard_map/ppermute | solution.py:24
  131.1 15.7 %collective-permute-start.13 = (bf16[8,128,128]{2,1,0:T(8,128)(2,1)S(1)}, bf16[8,128,128]{2,1,0:T(8,128)(2,1)S(1)}, u32[]{:S(2)}, u32[]{:S(2)}) collective-permute-start(bf16[8,128,128]{2,1,0:T(8,128)(2,1)S(1)} %get-tuple-element.32), channel_id=1, source_target_pairs={{0,16},{16,32},{32,48},{48,64},{64,80},{80,96},{96,112},{112,128},... | collective-permute-start | bytes 786440 | tf_op jit(solution)/shard_map/ppermute | solution.py:24
  135.0 11.8 %collective-permute-start.14 = (bf16[8,128,128]{2,1,0:T(8,128)(2,1)S(1)}, bf16[8,128,128]{2,1,0:T(8,128)(2,1)S(1)}, u32[]{:S(2)}, u32[]{:S(2)}) collective-permute-start(bf16[8,128,128]{2,1,0:T(8,128)(2,1)S(1)} %get-tuple-element.33), channel_id=1, source_target_pairs={{0,240},{16,0},{32,16},{48,32},{64,48},{80,64},{96,80},{112,96},{1... | collective-permute-start | bytes 786440 | tf_op jit(solution)/shard_map/ppermute | solution.py:24
  136.9 9.9 %collective-permute-start.15 = (f32[32,128]{1,0:T(8,128)S(1)}, f32[32,128]{1,0:T(8,128)S(1)}, u32[]{:S(2)}, u32[]{:S(2)}) collective-permute-start(f32[32,128]{1,0:T(8,128)S(1)} %get-tuple-element.34.w), channel_id=1, source_target_pairs={{0,32},{16,48},{32,0},{48,16},{1,33},{17,49},{33,1},{49,17},{2,34}... | collective-permute-start | bytes 49160 | tf_op jit(solution)/shard_map/ppermute | solution.py:331
  174.8 12.2 %all-to-all-start.3 = ((f32[16,32,128]{2,1,0:T(8,128)}), f32[16,32,128]{2,1,0:T(8,128)S(1)}, u32[]{:S(2)}, u32[]{:S(2)}) async-start(f32[16,32,128]{2,1,0:T(8,128)} %get-tuple-element.36), calls=%async_computation.3 | async-start | bytes 524288 | tf_op jit(solution)/shard_map/all_to_all | solution.py:348
  178.3 0.7 collective-permute-start.16

commit v4 on v3

--- a/solution.py
+++ b/solution.py
@@ -12,6 +12,7 @@
 FAR = Z // NEAR
 WROWS = 32
 BIAS_AT = 304
+PROWS = 16
 RING = ("q", "k")
 PLANE = ("h", "y", "x")
 NT = (((1,), (1,)), ((), ()))
@@ -50,6 +51,14 @@
 
 def f32(v):
     return v.astype(jnp.float32)
+
+
+def tile(v, i):
+    return v[i * TILE : (i + 1) * TILE]
+
+
+def block(v, i):
+    return f32(tile(v, i))
 
 
 def out(shape, dtype=jnp.bfloat16):
@@ -72,31 +81,100 @@
     return col // 32, (col // 8) % 4, (col // 2) % 4, col % 2
 
 
-def forward_kernel(ints, here, a, own, nxt, prv, ha, hb, far_core, o, xs, acc):
-    xs[0:8] = own[...]
-    xs[8:16] = nxt[...]
-    xs[16:24] = prv[...]
-    xs[24:28] = ha[...]
-    xs[28:32] = hb[...]
-    xs[32:64] = far_core[...]
+def window_kernel(own, nxt, prv, ha, hb, o):
+    o[0:8] = own[...]
+    o[8:16] = nxt[...]
+    o[16:24] = prv[...]
+    o[24:28] = ha[...]
+    o[28:32] = hb[...]
+
+
+def forward_kernel(here, packed, near, across, o, small, vi, ints, sem, xs, acc):
+    read_ints(packed, vi, ints, sem)
+    slots = (packed.shape[0] - small.shape[0]) // TILE
+    small[...] = packed[slots * TILE : slots * TILE + small.shape[0]]
+    xs[0:32] = near[...]
+    xs[32:64] = across[...]
     acc[...] = jnp.zeros_like(acc)
     core, mine = here[0], here[1]
-    n = ints[0, 64]
+    n = ints[2, 0]
     group = 4
-    for base in range(0, a.shape[0], group):
+    for base in range(0, slots, group):
         prods = []
         for s in range(base, base + group):
-            c, q, k, half = split_col(ints[0, 32 + s])
+            c, q, k, half = split_col(ints[1, s])
             rel = (k - mine + 4) % 4
             cls = jnp.where(rel == 2, 3, jnp.where(rel == 3, 2, rel))
             at = ((c + core) % 2) * 32 + cls * 8 + q * 2 + half
-            prods.append(jnp.dot(a[s], xs[at], preferred_element_type=jnp.float32))
+            prods.append(jnp.dot(tile(packed, s), xs[at], preferred_element_type=jnp.float32))
         for s, p in zip(range(base, base + group), prods):
             acc[jnp.where(s < n, ints[0, s], o.shape[0])] += p
     o[...] = bf(acc[0 : o.shape[0]])
 
 
-def dense_kernel(parts, weight, exit_weight, bias, ints, up, sent, wb):
+def pack_kernel(tiles, up, rows, cols, count, labels, mask, o, vr, vc, vn, vl, vm, b, sems):
+    top, nodes, slots = tiles.shape[0], up.shape[0], rows.shape[1]
+    large = [
+        pltpu.make_async_copy(tiles, o.at[0:top], sems.at[0]),
+        pltpu.make_async_copy(up, o.at[top : top + nodes], sems.at[1]),
+    ]
+    little = [
+        pltpu.make_async_copy(src, dst, sems.at[2 + i])
+        for i, (src, dst) in enumerate(
+            ((rows, vr), (cols, vc), (count, vn), (labels, vl), (mask, vm))
+        )
+    ]
+    for c in large + little:
+        c.start()
+    for c in little:
+        c.wait()
+    b[...] = jnp.zeros_like(b)
+    b[0:1, 0:slots] = f32(vr[...])
+    b[1:2, 0:slots] = f32(vc[...])
+    b[2:3, 0:1] = f32(vn[...])
+    for i in range(2):
+        b[3 + i : 4 + i] = f32(vl[:, i * TILE : (i + 1) * TILE])
+        b[5 + i : 6 + i] = f32(vm[:, i * TILE : (i + 1) * TILE])
+    o[top + nodes : top + nodes + PROWS] = bf(b[...])
+    for c in large:
+        c.wait()
+
+
+def pack(tiles, up, rows, cols, count, labels, mask):
+    def like(v):
+        return pltpu.VMEM(v.shape, v.dtype)
+
+    arrays = (tiles, up, rows, cols, count, labels, mask)
+    return pl.pallas_call(
+        pack_kernel,
+        out_shape=out((tiles.shape[0] + up.shape[0] + PROWS, TILE)),
+        in_specs=[pl.BlockSpec(memory_space=pl.ANY)] * len(arrays),
+        out_specs=vmem(),
+        scratch_shapes=[like(v) for v in arrays[2:]]
+        + [pltpu.VMEM((PROWS, TILE), jnp.float32), pltpu.SemaphoreType.DMA((7,))],
+        compiler_params=pltpu.CompilerParams(vmem_limit_bytes=60 * 1024 * 1024),
+        name="pack",
+    )(*arrays)
+
+
+def read_ints(packed, vi, ints, sem):
+    rows = packed.shape[0]
+    vi[...] = f32(packed[rows - PROWS : rows])[0:8].astype(jnp.int32)
+    c = pltpu.make_async_copy(vi, ints, sem)
+    c.start()
+    c.wait()
+
+
+def int_scratch():
+    return [
+        pltpu.VMEM((8, TILE), jnp.int32),
+        pltpu.SMEM((8, TILE), jnp.int32),
+        pltpu.SemaphoreType.DMA,
+    ]
+
+
+def dense_kernel(parts, weight, exit_weight, bias, small, sent, wb):
+    nodes = parts.shape[1]
     total = f32(parts[0])
     for j in range(1, parts.shape[0]):
         total += f32(parts[j])
@@ -110,12 +188,12 @@
     expd = jnp.exp(logits)
     probs = expd / jnp.sum(expd, axis=1, keepdims=True)
     ids = f32(lax.broadcasted_iota(jnp.int32, logits.shape, 1))
-    columns = jnp.transpose(f32(ints[...]))
-    labels = jnp.concatenate([columns[:, 1:2], columns[:, 2:3]], axis=0)
-    mask = jnp.concatenate([columns[:, 3:4], columns[:, 4:5]], axis=0)
+    columns = jnp.transpose(f32(small[nodes : nodes + PROWS]))
+    labels = jnp.concatenate([columns[:, 3:4], columns[:, 4:5]], axis=0)
+    mask = jnp.concatenate([columns[:, 5:6], columns[:, 6:7]], axis=0)
     onehot = f32(labels == ids)
     dlogits = bf(mask * (probs - onehot))
-    dact = f32(up[...]) + lax.dot_general(
+    dact = f32(small[0:nodes]) + lax.dot_general(
         dlogits, ew, NT, preferred_element_type=jnp.float32
     )
     dpre = bf(dact * sig * (1.0 + pre * (1.0 - sig)))
@@ -129,51 +207,50 @@
     bsum = jnp.sum(f32(dlogits), axis=0, keepdims=True)
     wb[BIAS_AT : BIAS_AT + 1] = bsum[:, 0:TILE]
     wb[BIAS_AT + 1 : BIAS_AT + 2, 0 : classes - TILE] = bsum[:, TILE:]
-    nodes = dagg.shape[0]
     for j in range(sent.shape[0]):
         sent[j, 0:nodes] = dagg
         sent[j, nodes : nodes + WROWS] = bf(wb[j * WROWS : (j + 1) * WROWS])
 
 
-def backward_kernel(ints, here, a, g, hu, rest, hv, rv, lv, ov, w, acc):
+def backward_kernel(here, packed, g, u, hv, rv, lv, ov, w, vi, ints, sem, acc):
+    read_ints(packed, vi, ints, sem)
     nodes = 2 * TILE
+    slots = (packed.shape[0] - nodes - PROWS) // TILE
     acc[...] = jnp.zeros_like(acc)
     core, mine = here[0], here[1]
-    n = ints[0, 64]
+    n = ints[2, 0]
     group = 4
-    for base in range(0, a.shape[0], group):
+    for base in range(0, slots, group):
         prods = []
         for s in range(base, base + group):
             t = ints[0, s]
             start = pl.multiple_of((t % 2) * TILE, TILE)
             gb = g[t // 2, pl.ds(start, TILE), :]
-            prods.append(lax.dot_general(a[s], gb, TN, preferred_element_type=jnp.float32))
+            prods.append(lax.dot_general(tile(packed, s), gb, TN, preferred_element_type=jnp.float32))
         for s, p in zip(range(base, base + group), prods):
-            c, q, k, half = split_col(ints[0, 32 + s])
+            c, q, k, half = split_col(ints[1, s])
             at = ((c + core) % 2) * 32 + ((k - mine + 4) % 4) * 8 + q * 2 + half
             acc[jnp.where(s < n, at, 64)] += p
     ov[...] = bf(acc[0:8])
     rv[...] = bf(acc[8:16])
     hv[...] = bf(acc[16:24])
     lv[...] = bf(acc[24:32])
-    rest[0:16] = bf(acc[32:48])
-    rest[16:24] = bf(acc[56:64])
+    for i in range(32):
+        u[i * TILE : (i + 1) * TILE] = bf(acc[32 + i])
     total = f32(g[0, nodes : nodes + WROWS])
     for j in range(1, g.shape[0]):
         total += f32(g[j, nodes : nodes + WROWS])
     ws = bf(total)
-    for i in range(8):
-        hu[i * TILE : (i + 1) * TILE] = bf(acc[48 + i])
-    hu[8 * TILE : 8 * TILE + WROWS] = ws
+    u[32 * TILE : 32 * TILE + WROWS] = ws
     w[...] = ws
 
 
-def fold1_kernel(hv, xh, w, a, b, ow):
+def fold1_kernel(hv, xs, w, a, b, ow):
     for i in range(4):
         rows = slice(i * TILE, (i + 1) * TILE)
-        a[rows] = bf(f32(hv[i]) + f32(xh[rows]))
-        b[rows] = bf(f32(hv[4 + i]) + f32(xh[(4 + i) * TILE : (5 + i) * TILE]))
-    ws = bf(f32(w[...]) + f32(xh[8 * TILE : 8 * TILE + WROWS]))
+        a[rows] = bf(f32(hv[i]) + block(xs, 16 + i))
+        b[rows] = bf(f32(hv[4 + i]) + block(xs, 20 + i))
+    ws = bf(f32(w[...]) + f32(xs[32 * TILE : 32 * TILE + WROWS]))
     a[4 * TILE : 4 * TILE + WROWS] = ws
     b[4 * TILE : 4 * TILE + WROWS] = ws
     ow[...] = ws
@@ -182,10 +259,10 @@
 def fold2_kernel(here, rv, lv, xs, ra, rb, w, r, l, ow):
     for i in range(4):
         rows = slice(i * TILE, (i + 1) * TILE)
-        r[i] = bf(f32(rv[i]) + f32(xs[8 + i]) + f32(ra[rows]))
-        l[4 + i] = bf(f32(lv[4 + i]) + f32(xs[20 + i]) + f32(rb[rows]))
-        r[4 + i] = bf(f32(rv[4 + i]) + f32(xs[12 + i]))
-        l[i] = bf(f32(lv[i]) + f32(xs[16 + i]))
+        r[i] = bf(f32(rv[i]) + block(xs, 8 + i) + f32(ra[rows]))
+        l[4 + i] = bf(f32(lv[4 + i]) + block(xs, 28 + i) + f32(rb[rows]))
+        r[4 + i] = bf(f32(rv[4 + i]) + block(xs, 12 + i))
+        l[i] = bf(f32(lv[i]) + block(xs, 24 + i))
     tail = slice(4 * TILE, 4 * TILE + WROWS)
     partner = jnp.where(here[1] % 2 == 1, f32(ra[tail]), f32(rb[tail]))
     ow[...] = f32(w[...]) + partner
@@ -196,7 +273,7 @@
     for j in range(FAR):
         for h in range(2):
             i = 2 * j + h
-            s = f32(ov[i]) + f32(xs[i]) + f32(rn[i]) + f32(rp[i])
+            s = f32(ov[i]) + block(xs, i) + f32(rn[i]) + f32(rp[i])
             o[j, h * TILE : (h + 1) * TILE] = bf(s)
         o[j, 2 * TILE : 2 * TILE + WROWS] = ws
 
@@ -237,7 +314,6 @@
     hidden = features.shape[-1]
     classes = exit_weight.shape[1]
     nodes = features.shape[1]
-    slots = tile_rows.shape[-1]
     plane = 16
     nodes_total = nodes * 2 * Z * plane
     scale = jnp.full((1,), float(nodes_total) ** (-0.5), jnp.float32)
@@ -250,36 +326,41 @@
         return pltpu.VMEM((n, TILE, hidden), jnp.float32)
 
     feats = swap(features[0])
-    ints = jnp.concatenate(
-        [
-            tile_rows.reshape(slots),
-            tile_cols.reshape(slots),
-            tile_count.reshape(1),
-            jnp.zeros((TILE - 2 * slots - 1,), jnp.int32),
-            labels.reshape(nodes),
-            label_mask.reshape(nodes),
-            jnp.zeros((3 * TILE,), jnp.int32),
-        ]
-    ).reshape(8, TILE)
-    ints = swap(ints)
-    values = swap(tile_values[0, 0])
-    up = swap(upstream[0])
+    packed = pack(
+        tile_values.reshape(-1, hidden),
+        upstream[0],
+        tile_rows[0],
+        tile_cols[0],
+        tile_count,
+        labels,
+        label_mask,
+    )
+    packed, feats = lax.optimization_barrier((packed, feats))
+    packed = swap(packed)
 
     far = lax.all_gather(feats, "q", axis=0)
+    far, packed = lax.optimization_barrier((far, packed))
     nxt = shift(far, -1)
     prv = shift(far, 1)
     ha = shift(far[: FAR // 2], -2)
     hb = shift(far[FAR // 2 :], 2)
-    mine = [blocks(v) for v in (far, nxt, prv, ha, hb)]
-    across = other_core(jnp.concatenate(mine, axis=0))
-
-    partial_value = call(
+    near = call(
+        window_kernel,
+        "window",
+        out((32, TILE, hidden)),
+        (),
+        [blocks(v) for v in (far, nxt, prv, ha, hb)],
+    )
+    across = other_core(near)
+
+    partial_value, small = call(
         forward_kernel,
         "forward_products",
-        out((2 * plane, TILE, hidden)),
-        (ints, here),
-        (values, *mine, across),
-        (pltpu.VMEM((64, TILE, hidden), jnp.bfloat16), acc(2 * plane + 1)),
+        (out((2 * plane, TILE, hidden)), out((nodes + PROWS, hidden))),
+        (here,),
+        (packed, near, across),
+        int_scratch()
+        + [pltpu.VMEM((64, TILE, hidden), jnp.bfloat16), acc(2 * plane + 1)],
     )
     parts = lax.all_to_all(
         partial_value.reshape(plane, nodes, hidden), PLANE, 0, 0, tiled=True
@@ -289,33 +370,31 @@
         "dense",
         out((plane, nodes + WROWS, hidden)),
         (),
-        (parts, weight, exit_weight, exit_bias.reshape(1, classes), ints, up),
+        (parts, weight, exit_weight, exit_bias.reshape(1, classes), small),
         (pltpu.VMEM((plane * WROWS, hidden), jnp.float32),),
     )
     got = lax.all_to_all(sent, PLANE, 0, 0, tiled=True)
     half = out((8, TILE, hidden))
-    hu, rest, hv, rv, lv, ov, w = call(
+    u, hv, rv, lv, ov, w = call(
         backward_kernel,
         "backward_products",
         (
-            out((8 * TILE + WROWS, hidden)),
-            out((24, TILE, hidden)),
+            out((32 * TILE + WROWS, hidden)),
             half,
             half,
             half,
             half,
             out((WROWS, hidden)),
         ),
-        (ints, here),
-        (values, got),
-        (acc(65),),
-    )
-
-    xh = other_core(hu)
-    xs = other_core(rest)
+        (here,),
+        (packed, got),
+        int_scratch() + [acc(65)],
+    )
+
+    xs = other_core(u)
     side = out((4 * TILE + WROWS, hidden))
     a, b, w = call(
-        fold1_kernel, "fold1", (side, side, out((WROWS, hidden))), (), (hv, xh, w)
+        fold1_kernel, "fold1", (side, side, out((WROWS, hidden))), (), (hv, xs, w)
     )
     ra = shift(a, 1)
     rb = shift(b, -1)

time: 189 us -> 186 us (0.984)
  starting transfers between devices: 56.8 us -> 52.8 us
  local copies, waits for them, and re-layouts: 4.36 us -> 0.77 us
  Pallas kernels: 8.12 us -> 11.6 us
    ppermute x8, starting transfers between devices: 24.4 us -> 27.6 us  [shift(): return lax.ppermute(v, RING, [(z, (z + d) % Z) for z in range(Z)])]
    unnamed x22 -> x8, local copies, waits for them, and re-layouts: 3.6 us -> 0.75 us
    ppermute x3 -> x2, waiting for transfers between devices: 2.35 us -> 5.18 us  [other_core(): return lax.ppermute(v, 'core', [(0, 1), (1, 0)])]
    ppermute x3 -> x2, starting transfers between devices: 6.34 us -> 3.84 us  [other_core(): return lax.ppermute(v, 'core', [(0, 1), (1, 0)])]
    ppermute x1, starting transfers between devices: 6.3 us -> 3.96 us  [local(): rw = lax.ppermute(w, 'k', [(k, k ^ 2) for k in range(NEAR)])]
    pallas_call x0 -> x1, Pallas kernels: none -> 2.3 us  [pack(): pl.pallas_call(pack_kernel, out_shape=out((tiles.shape[0] + up.shape[0] +...]
    ppermute x8, waiting for transfers between devices: 11.3 us -> 9.36 us  [shift(): return lax.ppermute(v, RING, [(z, (z + d) % Z) for z in range(Z)])]
    ppermute x5 -> x3, starting transfers between devices: 5.35 us -> 4.07 us  [swap(): return lax.ppermute(v, ('x', 'core'), [(0, 0), (1, 2), (2, 1), (3, 3)])]
  transfers between devices with their start and end apart: 19 -> 16, of which waited for: 9 -> 9; matrix products, arithmetic and copies ran while one was open for 2% -> 0% of each run, Pallas kernels for 0% -> 1%
where the time goes in v4:
time: 186 us; the launch traced here: 185 us
  blocking collectives  75.2 us (40%)
  starting transfers between devices  52.8 us (28%)
  waiting for transfers between devices  43.3 us (23%)
  Pallas kernels  11.6 us (6%)
    ppermute x8, starting transfers between devices, shift(): return lax.ppermute(v, RING, [(z, (z + d) % Z) for z in range(Z)])  27.6 us
    all_to_all x1, blocking collectives, local(): last = lax.all_to_all(joined, 'q', 0, 0, tiled=True)  26.9 us
    all_gather x1, blocking collectives, local(): far = lax.all_gather(feats, 'q', axis=0)  25.6 us
    all_to_all x1, blocking collectives, local(): got = lax.all_to_all(sent, PLANE, 0, 0, tiled=True)  22.8 us
    all_to_all x1, waiting for transfers between devices, local(): lax.all_to_all(partial_value.reshape(plane, nodes, hidden), PLANE, 0, 0,...  17.5 us
    all_to_all x1, starting transfers between devices, local(): lax.all_to_all(partial_value.reshape(plane, nodes, hidden), PLANE, 0, 0,...  9.86 us
    ppermute x8, waiting for transfers between devices, shift(): return lax.ppermute(v, RING, [(z, (z + d) % Z) for z in range(Z)])  9.36 us
    pallas_call x9, Pallas kernels, call(): pl.pallas_call(kernel, out_shape=outs, in_specs=[smem()] * len(scalars) +...  9.26 us
  transfers between devices with their start and end apart: 16, of which 9 were waited for; matrix products, arithmetic and copies ran while one was open for 0% of the time, Pallas kernels for 1%

profile of v4, /device:TPU:32, one launch (start us, length us, event | category | flops | bytes accessed | tf_op | source)
XLA Modules:
  0.0 185.3 jit_solution(6548199345542974084)
XLA Ops:
  0.6 1.5 collective-permute-start
  2.8 2.3 %pack.1 = bf16[4368,128]{1,0:T(8,128)(2,1)} custom-call(bf16[4096,128]{1,0:T(8,128)(2,1)} %bitcast.27, bf16[256,128]{1,0:T(8,128)(2,1)} %bitcast.29, s32[1,32]{1,0:T(1,128)} %bitcast.30, s32[1,32]{1,0:T(1,128)} %bitcast.31, s32[1,1]{1,0:T(1,128)S(6)} %copy.17.count, s32[1,256]{1,0:T(1,128)} %labels.1, s32[1,256]{1,0:T(1,128)} %mask.1), custom_call_target="tpu_custom_call" | custom-call | tf_op jit(solution)/shard_map/pack/pallas_call | solution.py:148
  5.1 1.9 %collective-permute-start.1 = (bf16[4368,128]{1,0:T(8,128)(2,1)}, bf16[4368,128]{1,0:T(8,128)(2,1)S(1)}, u32[]{:S(2)}, u32[]{:S(2)}) collective-permute-start(bf16[4368,128]{1,0:T(8,128)(2,1)} %pack.1), channel_id=1, source_target_pairs={{0,0},{1,256},{256,1},{257,257},{2,2},{3,258},{258,3},{259,259},{4... | collective-permute-start | bytes 3354632 | tf_op jit(solution)/shard_map/ppermute | solution.py:33
  7.0 25.6 %all-gather = bf16[1024,128]{1,0:T(8,128)(2,1)S(1)} all-gather(bf16[256,128]{1,0:T(8,128)(2,1)S(1)} %collective-permute-done), channel_id=2, replica_groups=mesh['x'=2,'q'=4,'k'=4,'h'=2,'y'=4,'core'=2] {'q'}, dimensions={0}, use_global_device_ids=true | all-gather | bytes 327680 | tf_op jit(solution)/shard_map/all_gather | solution.py:341
  32.6 2.8 %collective-permute-start.3 = (bf16[4,256,128]{2,1,0:T(8,128)(2,1)S(1)}, bf16[4,256,128]{2,1,0:T(8,128)(2,1)S(1)}, u32[]{:S(2)}, u32[]{:S(2)}) collective-permute-start(bf16[4,256,128]{2,1,0:T(8,128)(2,1)S(1)} %bitcast.18), channel_id=1, source_target_pairs={{0,16},{16,32},{32,48},{48,64},{64,80},{80,96},{96,112},{112,128},... | collective-permute-start | bytes 786440 | tf_op jit(solution)/shard_map/ppermute | solution.py:25
  35.4 3.4 %collective-permute-start.2 = (bf16[4,256,128]{2,1,0:T(8,128)(2,1)S(1)}, bf16[4,256,128]{2,1,0:T(8,128)(2,1)S(1)}, u32[]{:S(2)}, u32[]{:S(2)}) collective-permute-start(bf16[4,256,128]{2,1,0:T(8,128)(2,1)S(1)} %bitcast.19), channel_id=1, source_target_pairs={{0,240},{16,0},{32,16},{48,32},{64,48},{80,64},{96,80},{112,96},{1... | collective-permute-start | bytes 786440 | tf_op jit(solution)/shard_map/ppermute | solution.py:25
  38.8 2.9 %collective-permute-start.5 = (bf16[2,256,128]{2,1,0:T(8,128)(2,1)S(1)}, bf16[2,256,128]{2,1,0:T(8,128)(2,1)S(1)}, u32[]{:S(2)}, u32[]{:S(2)}) collective-permute-start(bf16[2,256,128]{2,1,0:T(8,128)(2,1)S(1)} %get-tuple-element.50), channel_id=1, source_target_pairs={{0,32},{16,48},{32,64},{48,80},{64,96},{80,112},{96,128},{112,144}... | collective-permute-start | bytes 393224 | tf_op jit(solution)/shard_map/ppermute | solution.py:25
  41.7 5.1 %collective-permute-start.4 = (bf16[2,256,128]{2,1,0:T(8,128)(2,1)S(1)}, bf16[2,256,128]{2,1,0:T(8,128)(2,1)S(1)}, u32[]{:S(2)}, u32[]{:S(2)}) collective-permute-start(bf16[2,256,128]{2,1,0:T(8,128)(2,1)S(1)} %get-tuple-element.51), channel_id=1, source_target_pairs={{0,224},{16,240},{32,0},{48,16},{64,32},{80,48},{96,64},{112,80},{... | collective-permute-start | bytes 393224 | tf_op jit(solution)/shard_map/ppermute | solution.py:25
  46.8 2.2 %collective-permute-done.5 = bf16[2,256,128]{2,1,0:T(8,128)(2,1)S(1)} collective-permute-done((bf16[2,256,128]{2,1,0:T(8,128)(2,1)S(1)}, bf16[2,256,128]{2,1,0:T(8,128)(2,1)S(1)}, u32[]{:S(2)}, u32[]{:S(2)}) %collective-permute-start.5) | collective-permute-done | bytes 131104 | tf_op jit(solution)/shard_map/ppermute | solution.py:25
  49.0 1.7 collective-permute-done.4
  50.8 1.9 %collective-permute-start.6 = (bf16[32,128,128]{2,1,0:T(8,128)(2,1)S(1)}, bf16[32,128,128]{2,1,0:T(8,128)(2,1)S(1)}, u32[]{:S(2)}, u32[]{:S(2)}) collective-permute-start(bf16[32,128,128]{2,1,0:T(8,128)(2,1)S(1)} %window.1.near), channel_id=1, source_target_pairs={{0,1},{1,0},{2,3},{3,2},{4,5},{5,4},{6,7},{7,6},{8,9},{9,8},{10,11... | collective-permute-start | bytes 3145736 | tf_op jit(solution)/shard_map/ppermute | solution.py:29
  52.8 2.5 %collective-permute-done.6.across = bf16[32,128,128]{2,1,0:T(8,128)(2,1)S(1)} collective-permute-done((bf16[32,128,128]{2,1,0:T(8,128)(2,1)S(1)}, bf16[32,128,128]{2,1,0:T(8,128)(2,1)S(1)}, u32[]{:S(2)}, u32[]{:S(2)}) %collective-permute-start.6) | collective-permute-done | bytes 1048608 | tf_op jit(solution)/shard_map/ppermute | solution.py:29
  55.4 3.3 %forward_products.1 = (bf16[32,128,128]{2,1,0:T(8,128)(2,1)}, bf16[272,128]{1,0:T(8,128)(2,1)S(1)}) custom-call(s32[2]{0:T(128)S(1)} %pad_add_fusion.here, bf16[4368,128]{1,0:T(8,128)(2,1)S(1)} %collective-permute-done.1.packed, bf16[32,128,128]{2,1,0:T(8,128)(2,1)S(1)} %window.1.near, bf16[32,128,128]{2,1,0:T(8,128)(2,1)S(1)} %collective-permute-done.6.across), custom_call_target="tpu_custom_call" | custom-call | tf_op jit(solution)/shard_map/forward_products/pallas_call | solution.py:69
  58.7 9.9 %all-to-all-start = ((bf16[16,256,128]{2,1,0:T(8,128)(2,1)}), bf16[16,256,128]{2,1,0:T(8,128)(2,1)S(1)}, u32[]{:S(2)}, u32[]{:S(2)}) async-start(bf16[16,256,128]{2,1,0:T(8,128)(2,1)} %bitcast.13), calls=%async_computation | async-start | bytes 2097152 | tf_op jit(solution)/shard_map/all_to_all | solution.py:365
  68.7 17.5 %all-to-all-done.parts = bf16[16,256,128]{2,1,0:T(8,128)(2,1)S(1)} async-done(((bf16[16,256,128]{2,1,0:T(8,128)(2,1)}), bf16[16,256,128]{2,1,0:T(8,128)(2,1)S(1)}, u32[]{:S(2)}, u32[]{:S(2)}) %all-to-all-start) | async-done | bytes 1048608 | tf_op jit(solution)/shard_map/all_to_all | solution.py:365
  86.2 0.8 dense.1
  87.0 22.8 %all_to_all.20.g = bf16[16,288,128]{2,1,0:T(8,128)(2,1)S(1)} all-to-all(bf16[16,288,128]{2,1,0:T(8,128)(2,1)S(1)} %dense.1), channel_id=1, replica_groups=mesh['x'=2,'q'=4,'k'=4,'h'=2,'y'=4,'core'=2] {'h','y','x'}, dimensions={0} | all-to-all | bytes 2359296 | tf_op jit(solution)/shard_map/all_to_all | solution.py:376
  109.8 2.8 %backward_products.1 = (bf16[4128,128]{1,0:T(8,128)(2,1)S(1)}, bf16[8,128,128]{2,1,0:T(8,128)(2,1)S(1)}, bf16[8,128,128]{2,1,0:T(8,128)(2,1)S(1)}, bf16[8,128,12...) custom-call(s32[2]{0:T(128)S(1)} %pad_add_fusion.here, ...), custom_call_target="tpu_custom_call" | custom-call | tf_op jit(solution)/shard_map/backward_products/pallas_call | solution.py:69
  112.6 1.9 %collective-permute-start.7 = (bf16[4128,128]{1,0:T(8,128)(2,1)S(1)}, bf16[4128,128]{1,0:T(8,128)(2,1)S(1)}, u32[]{:S(2)}, u32[]{:S(2)}) collective-permute-start(bf16[4128,128]{1,0:T(8,128)(2,1)S(1)} %get-tuple-element.34), channel_id=1, source_target_pairs={{0,1},{1,0},{2,3},{3,2},{4,5},{5,4},{6,7},{7,6},{8,9},{9,8},{10,11... | collective-permute-start | bytes 3170312 | tf_op jit(solution)/shard_map/ppermute | solution.py:29
  114.5 2.6 %collective-permute-done.7.xs = bf16[4128,128]{1,0:T(8,128)(2,1)S(1)} collective-permute-done((bf16[4128,128]{1,0:T(8,128)(2,1)S(1)}, bf16[4128,128]{1,0:T(8,128)(2,1)S(1)}, u32[]{:S(2)}, u32[]{:S(2)}) %collective-permute-start.7) | collective-permute-done | bytes 1056800 | tf_op jit(solution)/shard_map/ppermute | solution.py:29
  117.2 5.6 %collective-permute-start.8 = (bf16[544,128]{1,0:T(8,128)(2,1)S(1)}, bf16[544,128]{1,0:T(8,128)(2,1)S(1)}, u32[]{:S(2)}, u32[]{:S(2)}) collective-permute-start(bf16[544,128]{1,0:T(8,128)(2,1)S(1)} %get-tuple-element.39), channel_id=1, source_target_pairs={{0,16},{16,32},{32,48},{48,64},{64,80},{80,96},{96,112},{112,128},... | collective-permute-start | bytes 417800 | tf_op jit(solution)/shard_map/ppermute | solution.py:25
  122.9 1.9 %collective-permute-start.9 = (bf16[544,128]{1,0:T(8,128)(2,1)S(1)}, bf16[544,128]{1,0:T(8,128)(2,1)S(1)}, u32[]{:S(2)}, u32[]{:S(2)}) collective-permute-start(bf16[544,128]{1,0:T(8,128)(2,1)S(1)} %get-tuple-element.40), channel_id=1, source_target_pairs={{0,240},{16,0},{32,16},{48,32},{64,48},{80,64},{96,80},{112,96},{1... | collective-permute-start | bytes 417800 | tf_op jit(solution)/shard_map/ppermute | solution.py:25
  124.8 1.3 collective-permute-done.8.ra
  126.1 4.1 %collective-permute-done.9.rb = bf16[544,128]{1,0:T(8,128)(2,1)S(1)} collective-permute-done((bf16[544,128]{1,0:T(8,128)(2,1)S(1)}, bf16[544,128]{1,0:T(8,128)(2,1)S(1)}, u32[]{:S(2)}, u32[]{:S(2)}) %collective-permute-start.9) | collective-permute-done | bytes 139296 | tf_op jit(solution)/shard_map/ppermute | solution.py:25
  130.9 2.2 %collective-permute-start.10 = (bf16[8,128,128]{2,1,0:T(8,128)(2,1)S(1)}, bf16[8,128,128]{2,1,0:T(8,128)(2,1)S(1)}, u32[]{:S(2)}, u32[]{:S(2)}) collective-permute-start(bf16[8,128,128]{2,1,0:T(8,128)(2,1)S(1)} %get-tuple-element.42), channel_id=1, source_target_pairs={{0,16},{16,32},{32,48},{48,64},{64,80},{80,96},{96,112},{112,128},... | collective-permute-start | bytes 786440 | tf_op jit(solution)/shard_map/ppermute | solution.py:25
  133.2 3.6 %collective-permute-start.11 = (bf16[8,128,128]{2,1,0:T(8,128)(2,1)S(1)}, bf16[8,128,128]{2,1,0:T(8,128)(2,1)S(1)}, u32[]{:S(2)}, u32[]{:S(2)}) collective-permute-start(bf16[8,128,128]{2,1,0:T(8,128)(2,1)S(1)} %get-tuple-element.43), channel_id=1, source_target_pairs={{0,240},{16,0},{32,16},{48,32},{64,48},{80,64},{96,80},{112,96},{1... | collective-permute-start | bytes 786440 | tf_op jit(solution)/shard_map/ppermute | solution.py:25
  136.8 4.0 %collective-permute-start.12 = (f32[32,128]{1,0:T(8,128)S(1)}, f32[32,128]{1,0:T(8,128)S(1)}, u32[]{:S(2)}, u32[]{:S(2)}) collective-permute-start(f32[32,128]{1,0:T(8,128)S(1)} %get-tuple-element.44.w), channel_id=1, source_target_pairs={{0,32},{16,48},{32,0},{48,16},{1,33},{17,49},{33,1},{49,17},{2,34}... | collective-permute-start | bytes 49160 | tf_op jit(solution)/shard_map/ppermute | solution.py:410
  140.8 3.3 %collective-permute-done.12.rw = f32[32,128]{1,0:T(8,128)S(1)} collective-permute-done((f32[32,128]{1,0:T(8,128)S(1)}, f32[32,128]{1,0:T(8,128)S(1)}, u32[]{:S(2)}, u32[]{:S(2)}) %collective-permute-start.12) | collective-permute-done | bytes 16416 | tf_op jit(solution)/shard_map/ppermute | solution.py:410
  144.2 26.9 %all_to_all.21.parts = bf16[4,288,128]{2,1,0:T(8,128)(2,1)S(1)} all-to-all(bf16[4,288,128]{2,1,0:T(8,128)(2,1)S(1)} %join.1), channel_id=1, replica_groups=mesh['x'=2,'q'=4,'k'=4,'h'=2,'y'=4,'core'=2] {'q'}, dimensions={0} | all-to-all | bytes 589824 | tf_op jit(solution)/shard_map/all_to_all | solution.py:418
  171.1 0.7 finish.1
  171.8 3.5 %all-to-all-start.3 = ((f32[16,32,128]{2,1,0:T(8,128)}), f32[16,32,128]{2,1,0:T(8,128)S(1)}, u32[]{:S(2)}, u32[]{:S(2)}) async-start(f32[16,32,128]{2,1,0:T(8,128)} %get-tuple-element.46), calls=%async_computation.3 | async-start | bytes 524288 | tf_op jit(solution)/shard_map/all_to_all | solution.py:427
  176.1 8.0 %all-to-all-done.3.wall = f32[16,32,128]{2,1,0:T(8,128)S(1)} async-done(((f32[16,32,128]{2,1,0:T(8,128)}), f32[16,32,128]{2,1,0:T(8,128)S(1)}, u32[]{:S(2)}, u32[]{:S(2)}) %all-to-all-start.3) | async-done | bytes 262176 | tf_op jit(solution)/shard_map/all_to_all | solution.py:427
  (23 shorter events, 3.2 us)
Async XLA Ops:
  0.6 4.5 %collective-permute-start = (bf16[256,128]{1,0:T(8,128)(2,1)}, bf16[256,128]{1,0:T(8,128)(2,1)S(1)}, u32[]{:S(2)}, u32[]{:S(2)}) collective-permute-start(bf16[256,128]{1,0:T(8,128)(2,1)} %bitcast.33), channel_id=1, source_target_pairs={{0,0},{1,256},{256,1},{257,257},{2,2},{3,258},{258,3},{259,259},{4... | collective-permute-start | bytes 196616 | tf_op jit(solution)/shard_map/ppermute | solution.py:33
  5.1 27.5 %collective-permute-start.1 = (bf16[4368,128]{1,0:T(8,128)(2,1)}, bf16[4368,128]{1,0:T(8,128)(2,1)S(1)}, u32[]{:S(2)}, u32[]{:S(2)}) collective-permute-start(bf16[4368,128]{1,0:T(8,128)(2,1)} %pack.1), channel_id=1, source_target_pairs={{0,0},{1,256},{256,1},{257,257},{2,2},{3,258},{258,3},{259,259},{4... | collective-permute-start | bytes 3354632 | tf_op jit(solution)/shard_map/ppermute | solution.py:33
  32.6 18.2 %collective-permute-start.3 = (bf16[4,256,128]{2,1,0:T(8,128)(2,1)S(1)}, bf16[4,256,128]{2,1,0:T(8,128)(2,1)S(1)}, u32[]{:S(2)}, u32[]{:S(2)}) collective-permute-start(bf16[4,256,128]{2,1,0:T(8,128)(2,1)S(1)} %bitcast.18), channel_id=1, source_target_pairs={{0,16},{16,32},{32,48},{48,64},{64,80},{80,96},{96,112},{112,128},... | collective-permute-start | bytes 786440 | tf_op jit(solution)/shard_map/ppermute | solution.py:25
  35.4 15.3 %collective-permute-start.2 = (bf16[4,256,128]{2,1,0:T(8,128)(2,1)S(1)}, bf16[4,256,128]{2,1,0:T(8,128)(2,1)S(1)}, u32[]{:S(2)}, u32[]{:S(2)}) collective-permute-start(bf16[4,256,128]{2,1,0:T(8,128)(2,1)S(1)} %bitcast.19), channel_id=1, source_target_pairs={{0,240},{16,0},{32,16},{48,32},{64,48},{80,64},{96,80},{112,96},{1... | collective-permute-start | bytes 786440 | tf_op jit(solution)/shard_map/ppermute | solution.py:25
  38.8 10.2 %collective-permute-start.5 = (bf16[2,256,128]{2,1,0:T(8,128)(2,1)S(1)}, bf16[2,256,128]{2,1,0:T(8,128)(2,1)S(1)}, u32[]{:S(2)}, u32[]{:S(2)}) collective-permute-start(bf16[2,256,128]{2,1,0:T(8,128)(2,1)S(1)} %get-tuple-element.50), channel_id=1, source_target_pairs={{0,32},{16,48},{32,64},{48,80},{64,96},{80,112},{96,128},{112,144}... | collective-permute-start | bytes 393224 | tf_op jit(solution)/shard_map/ppermute | solution.py:25
  41.7 9.1 %collective-permute-start.4 = (bf16[2,256,128]{2,1,0:T(8,128)(2,1)S(1)}, bf16[2,256,128]{2,1,0:T(8,128)(2,1)S(1)}, u32[]{:S(2)}, u32[]{:S(2)}) collective-permute-start(bf16[2,256,128]{2,1,0:T(8,128)(2,1)S(1)} %get-tuple-element.51), channel_id=1, source_target_pairs={{0,224},{16,240},{32,0},{48,16},{64,32},{80,48},{96,64},{112,80},{... | collective-permute-start | bytes 393224 | tf_op jit(solution)/shard_map/ppermute | solution.py:25
  50.8 4.6 %collective-permute-start.6 = (bf16[32,128,128]{2,1,0:T(8,128)(2,1)S(1)}, bf16[32,128,128]{2,1,0:T(8,128)(2,1)S(1)}, u32[]{:S(2)}, u32[]{:S(2)}) collective-permute-start(bf16[32,128,128]{2,1,0:T(8,128)(2,1)S(1)} %window.1.near), channel_id=1, source_target_pairs={{0,1},{1,0},{2,3},{3,2},{4,5},{5,4},{6,7},{7,6},{8,9},{9,8},{10,11... | collective-permute-start | bytes 3145736 | tf_op jit(solution)/shard_map/ppermute | solution.py:29
  58.7 9.9 %copy-start.2 = (bf16[128,172]{0,1:T(8,128)(2,1)S(1)}, bf16[128,172]{0,1:T(8,128)(2,1)}, u32[]{:S(2)}) copy-start(bf16[128,172]{0,1:T(8,128)(2,1)} %param.17) | copy-start | bytes 132100
  58.7 27.5 %copy-start = (bf16[128,128]{1,0:T(8,128)(2,1)S(1)}, bf16[128,128]{1,0:T(8,128)(2,1)}, u32[]{:S(2)}) copy-start(bf16[128,128]{1,0:T(8,128)(2,1)} %weight.1) | copy-start | bytes 98308
  58.7 27.5 %copy-start.1 = (f32[172]{0:T(256)S(1)}, f32[172]{0:T(256)}, u32[]{:S(2)}) copy-start(f32[172]{0:T(256)} %param.18) | copy-start | bytes 2068
  58.7 27.5 %all-to-all-start = ((bf16[16,256,128]{2,1,0:T(8,128)(2,1)}), bf16[16,256,128]{2,1,0:T(8,128)(2,1)S(1)}, u32[]{:S(2)}, u32[]{:S(2)}) async-start(bf16[16,256,128]{2,1,0:T(8,128)(2,1)} %bitcast.13), calls=%async_computation | async-start | bytes 2097152 | tf_op jit(solution)/shard_map/all_to_all | solution.py:365
  112.6 4.6 %collective-permute-start.7 = (bf16[4128,128]{1,0:T(8,128)(2,1)S(1)}, bf16[4128,128]{1,0:T(8,128)(2,1)S(1)}, u32[]{:S(2)}, u32[]{:S(2)}) collective-permute-start(bf16[4128,128]{1,0:T(8,128)(2,1)S(1)} %get-tuple-element.34), channel_id=1, source_target_pairs={{0,1},{1,0},{2,3},{3,2},{4,5},{5,4},{6,7},{7,6},{8,9},{9,8},{10,11... | collective-permute-start | bytes 3170312 | tf_op jit(solution)/shard_map/ppermute | solution.py:29
  117.2 8.9 %collective-permute-start.8 = (bf16[544,128]{1,0:T(8,128)(2,1)S(1)}, bf16[544,128]{1,0:T(8,128)(2,1)S(1)}, u32[]{:S(2)}, u32[]{:S(2)}) collective-permute-start(bf16[544,128]{1,0:T(8,128)(2,1)S(1)} %get-tuple-element.39), channel_id=1, source_target_pairs={{0,16},{16,32},{32,48},{48,64},{64,80},{80,96},{96,112},{112,128},... | collective-permute-start | bytes 417800 | tf_op jit(solution)/shard_map/ppermute | solution.py:25
  122.9 7.3 %collective-permute-start.9 = (bf16[544,128]{1,0:T(8,128)(2,1)S(1)}, bf16[544,128]{1,0:T(8,128)(2,1)S(1)}, u32[]{:S(2)}, u32[]{:S(2)}) collective-permute-start(bf16[544,128]{1,0:T(8,128)(2,1)S(1)} %get-tuple-element.40), channel_id=1, source_target_pairs={{0,240},{16,0},{32,16},{48,32},{64,48},{80,64},{96,80},{112,96},{1... | collective-permute-start | bytes 417800 | tf_op jit(solution)/shard_map/ppermute | solution.py:25
  130.9 13.1 %collective-permute-start.10 = (bf16[8,128,128]{2,1,0:T(8,128)(2,1)S(1)}, bf16[8,128,128]{2,1,0:T(8,128)(2,1)S(1)}, u32[]{:S(2)}, u32[]{:S(2)}) collective-permute-start(bf16[8,128,128]{2,1,0:T(8,128)(2,1)S(1)} %get-tuple-element.42), channel_id=1, source_target_pairs={{0,16},{16,32},{32,48},{48,64},{64,80},{80,96},{96,112},{112,128},... | collective-permute-start | bytes 786440 | tf_op jit(solution)/shard_map/ppermute | solution.py:25
  133.2 10.9 %collective-permute-start.11 = (bf16[8,128,128]{2,1,0:T(8,128)(2,1)S(1)}, bf16[8,128,128]{2,1,0:T(8,128)(2,1)S(1)}, u32[]{:S(2)}, u32[]{:S(2)}) collective-permute-start(bf16[8,128,128]{2,1,0:T(8,128)(2,1)S(1)} %get-tuple-element.43), channel_id=1, source_target_pairs={{0,240},{16,0},{32,16},{48,32},{64,48},{80,64},{96,80},{112,96},{1... | collective-permute-start | bytes 786440 | tf_op jit(solution)/shard_map/ppermute | solution.py:25
  136.8 7.3 %collective-permute-start.12 = (f32[32,128]{1,0:T(8,128)S(1)}, f32[32,128]{1,0:T(8,128)S(1)}, u32[]{:S(2)}, u32[]{:S(2)}) collective-permute-start(f32[32,128]{1,0:T(8,128)S(1)} %get-tuple-element.44.w), channel_id=1, source_target_pairs={{0,32},{16,48},{32,0},{48,16},{1,33},{17,49},{33,1},{49,17},{2,34}... | collective-permute-start | bytes 49160 | tf_op jit(solution)/shard_map/ppermute | solution.py:410
  171.8 12.2 %all-to-all-start.3 = ((f32[16,32,128]{2,1,0:T(8,128)}), f32[16,32,128]{2,1,0:T(8,128)S(1)}, u32[]{:S(2)}, u32[]{:S(2)}) async-start(f32[16,32,128]{2,1,0:T(8,128)} %get-tuple-element.46), calls=%async_computation.3 | async-start | bytes 524288 | tf_op jit(solution)/shard_map/all_to_all | solution.py:427
  175.4 0.7 collective-permute-start.13

commit v5 on v4

--- a/solution.py
+++ b/solution.py
@@ -1,3 +1,5 @@
+import functools
+
 import jax
 import jax.numpy as jnp
 from jax import lax
@@ -11,6 +13,7 @@
 NEAR = 4
 FAR = Z // NEAR
 WROWS = 32
+WUSED = 24
 BIAS_AT = 304
 PROWS = 16
 RING = ("q", "k")
@@ -89,14 +92,12 @@
     o[28:32] = hb[...]
 
 
-def forward_kernel(here, packed, near, across, o, small, vi, ints, sem, xs, acc):
-    read_ints(packed, vi, ints, sem)
-    slots = (packed.shape[0] - small.shape[0]) // TILE
-    small[...] = packed[slots * TILE : slots * TILE + small.shape[0]]
+def forward_kernel(ints, packed, near, across, o, xs, acc):
+    slots = (packed.shape[0] - PROWS) // TILE - 2
     xs[0:32] = near[...]
     xs[32:64] = across[...]
     acc[...] = jnp.zeros_like(acc)
-    core, mine = here[0], here[1]
+    core, mine = position()
     n = ints[2, 0]
     group = 4
     for base in range(0, slots, group):
@@ -157,20 +158,8 @@
     )(*arrays)
 
 
-def read_ints(packed, vi, ints, sem):
-    rows = packed.shape[0]
-    vi[...] = f32(packed[rows - PROWS : rows])[0:8].astype(jnp.int32)
-    c = pltpu.make_async_copy(vi, ints, sem)
-    c.start()
-    c.wait()
-
-
-def int_scratch():
-    return [
-        pltpu.VMEM((8, TILE), jnp.int32),
-        pltpu.SMEM((8, TILE), jnp.int32),
-        pltpu.SemaphoreType.DMA,
-    ]
+def position():
+    return lax.axis_index("core"), lax.axis_index("k")
 
 
 def dense_kernel(parts, weight, exit_weight, bias, small, sent, wb):
@@ -209,15 +198,14 @@
     wb[BIAS_AT + 1 : BIAS_AT + 2, 0 : classes - TILE] = bsum[:, TILE:]
     for j in range(sent.shape[0]):
         sent[j, 0:nodes] = dagg
-        sent[j, nodes : nodes + WROWS] = bf(wb[j * WROWS : (j + 1) * WROWS])
-
-
-def backward_kernel(here, packed, g, u, hv, rv, lv, ov, w, vi, ints, sem, acc):
-    read_ints(packed, vi, ints, sem)
+        sent[j, nodes : nodes + WROWS] = bf(wb[j * WUSED : j * WUSED + WROWS])
+
+
+def backward_kernel(ints, packed, g, u, hv, rv, lv, ov, w, acc):
     nodes = 2 * TILE
-    slots = (packed.shape[0] - nodes - PROWS) // TILE
+    slots = (packed.shape[0] - PROWS) // TILE - 2
     acc[...] = jnp.zeros_like(acc)
-    core, mine = here[0], here[1]
+    core, mine = position()
     n = ints[2, 0]
     group = 4
     for base in range(0, slots, group):
@@ -245,57 +233,66 @@
     w[...] = ws
 
 
-def fold1_kernel(hv, xs, w, a, b, ow):
+def fold_kernel(hv, rv, lv, xs, w, a, b, r, l, ow):
+    ws = bf(f32(w[...]) + f32(xs[32 * TILE : 32 * TILE + WROWS]))
     for i in range(4):
         rows = slice(i * TILE, (i + 1) * TILE)
         a[rows] = bf(f32(hv[i]) + block(xs, 16 + i))
         b[rows] = bf(f32(hv[4 + i]) + block(xs, 20 + i))
-    ws = bf(f32(w[...]) + f32(xs[32 * TILE : 32 * TILE + WROWS]))
-    a[4 * TILE : 4 * TILE + WROWS] = ws
-    b[4 * TILE : 4 * TILE + WROWS] = ws
+    for i in range(8):
+        rows = slice(i * TILE, (i + 1) * TILE)
+        r[rows] = bf(f32(rv[i]) + block(xs, 8 + i))
+        l[rows] = bf(f32(lv[i]) + block(xs, 24 + i))
+    for v in (a, b, r, l):
+        v[v.shape[0] - WROWS : v.shape[0]] = ws
     ow[...] = ws
 
 
-def fold2_kernel(here, rv, lv, xs, ra, rb, w, r, l, ow):
-    for i in range(4):
-        rows = slice(i * TILE, (i + 1) * TILE)
-        r[i] = bf(f32(rv[i]) + block(xs, 8 + i) + f32(ra[rows]))
-        l[4 + i] = bf(f32(lv[4 + i]) + block(xs, 28 + i) + f32(rb[rows]))
-        r[4 + i] = bf(f32(rv[4 + i]) + block(xs, 12 + i))
-        l[i] = bf(f32(lv[i]) + block(xs, 24 + i))
-    tail = slice(4 * TILE, 4 * TILE + WROWS)
-    partner = jnp.where(here[1] % 2 == 1, f32(ra[tail]), f32(rb[tail]))
-    ow[...] = f32(w[...]) + partner
-
-
-def join_kernel(ov, xs, rn, rp, w, rw, o):
-    ws = bf(w[...] + rw[...])
+def join_kernel(ov, xs, ra, rb, rn, rp, w, o):
+    near, far = slice(8 * TILE, 8 * TILE + WROWS), slice(4 * TILE, 4 * TILE + WROWS)
+    used = slice(0, WUSED)
+    odd = position()[1] % 2 == 1
+    before, after = f32(rn[near]), f32(rp[near])
+    pair = f32(w[...]) + jnp.where(odd, before, after)
+    beside = jnp.where(odd, after, before) + jnp.where(odd, f32(rb[far]), f32(ra[far]))
+    both = bf(jnp.concatenate([pair[used], beside[used]], axis=0))
     for j in range(FAR):
         for h in range(2):
             i = 2 * j + h
-            s = f32(ov[i]) + block(xs, i) + f32(rn[i]) + f32(rp[i])
+            s = f32(ov[i]) + block(xs, i) + block(rn, i) + block(rp, i)
+            s += block(ra, i) if i < 4 else block(rb, i - 4)
             o[j, h * TILE : (h + 1) * TILE] = bf(s)
-        o[j, 2 * TILE : 2 * TILE + WROWS] = ws
+        o[j, 2 * TILE : 2 * TILE + 2 * WUSED] = both
 
 
 def finish_kernel(parts, o, w):
-    total = f32(parts[0])
-    for j in range(1, parts.shape[0]):
-        total += f32(parts[j])
     nodes = o.shape[0]
-    o[...] = bf(total[0:nodes])
+    both = slice(nodes, nodes + 2 * WUSED)
+    total = f32(parts[0, both])
+    for j in range(1, FAR):
+        total += f32(parts[j, both])
+    k = position()[1]
+    first = jnp.where(k == 0, 1, jnp.where(k == 3, 3, 0))
+    other = f32(parts[first, both])
+    for j in range(1, FAR):
+        other += f32(parts[(first + j) % FAR, both])
+    total = total[0:WUSED] + other[WUSED : 2 * WUSED]
     for j in range(w.shape[0]):
-        w[j] = total[nodes : nodes + WROWS]
+        w[j] = total
+    s = f32(parts[0, 0:nodes])
+    for j in range(1, FAR):
+        s += f32(parts[j, 0:nodes])
+    o[...] = bf(s)
 
 
 def unpack_kernel(scale, wall, layer, exit_t, bias, wb):
     for j in range(wall.shape[0]):
-        wb[j * WROWS : (j + 1) * WROWS] = wall[j] * scale[0]
+        wb[j * WUSED : (j + 1) * WUSED] = wall[j] * scale
     classes = exit_t.shape[0]
     layer[...] = wb[0:TILE]
     exit_t[...] = wb[TILE : TILE + classes]
-    bias[:, 0:TILE] = wb[BIAS_AT : BIAS_AT + 1]
-    bias[:, TILE:classes] = wb[BIAS_AT + 1 : BIAS_AT + 2, 0 : classes - TILE]
+    bias[0:TILE] = wb[BIAS_AT]
+    bias[TILE:classes] = wb[BIAS_AT + 1, 0 : classes - TILE]
 
 
 def local(
@@ -316,8 +313,7 @@
     nodes = features.shape[1]
     plane = 16
     nodes_total = nodes * 2 * Z * plane
-    scale = jnp.full((1,), float(nodes_total) ** (-0.5), jnp.float32)
-    here = jnp.stack([lax.axis_index("core"), lax.axis_index("k")]).astype(jnp.int32)
+    scale = float(nodes_total) ** (-0.5)
 
     def blocks(v):
         return v.reshape(-1, TILE, hidden)
@@ -353,14 +349,16 @@
     )
     across = other_core(near)
 
-    partial_value, small = call(
+    top = packed.shape[0] - nodes - PROWS
+    ints = packed[top + nodes : top + nodes + 8].astype(jnp.int32)
+    small = packed[top:]
+    partial_value = call(
         forward_kernel,
         "forward_products",
-        (out((2 * plane, TILE, hidden)), out((nodes + PROWS, hidden))),
-        (here,),
+        out((2 * plane, TILE, hidden)),
+        (ints,),
         (packed, near, across),
-        int_scratch()
-        + [pltpu.VMEM((64, TILE, hidden), jnp.bfloat16), acc(2 * plane + 1)],
+        (pltpu.VMEM((64, TILE, hidden), jnp.bfloat16), acc(2 * plane + 1)),
     )
     parts = lax.all_to_all(
         partial_value.reshape(plane, nodes, hidden), PLANE, 0, 0, tiled=True
@@ -371,7 +369,7 @@
         out((plane, nodes + WROWS, hidden)),
         (),
         (parts, weight, exit_weight, exit_bias.reshape(1, classes), small),
-        (pltpu.VMEM((plane * WROWS, hidden), jnp.float32),),
+        (pltpu.VMEM((plane * WUSED + WROWS, hidden), jnp.float32),),
     )
     got = lax.all_to_all(sent, PLANE, 0, 0, tiled=True)
     half = out((8, TILE, hidden))
@@ -386,58 +384,54 @@
             half,
             out((WROWS, hidden)),
         ),
-        (here,),
+        (ints,),
         (packed, got),
-        int_scratch() + [acc(65)],
+        (acc(65),),
     )
 
     xs = other_core(u)
-    side = out((4 * TILE + WROWS, hidden))
-    a, b, w = call(
-        fold1_kernel, "fold1", (side, side, out((WROWS, hidden))), (), (hv, xs, w)
-    )
-    ra = shift(a, 1)
-    rb = shift(b, -1)
-    rr, ll, w = call(
-        fold2_kernel,
-        "fold2",
-        (half, half, out((WROWS, hidden), jnp.float32)),
-        (here,),
-        (rv, lv, xs, ra, rb, w),
-    )
-    rn = shift(rr, 1)
-    rp = shift(ll, -1)
-    rw = lax.ppermute(w, "k", [(k, k ^ 2) for k in range(NEAR)])
+    side, full = out((4 * TILE + WROWS, hidden)), out((8 * TILE + WROWS, hidden))
+    a, b, r, l, w = call(
+        fold_kernel,
+        "fold",
+        (side, side, full, full, out((WROWS, hidden))),
+        (),
+        (hv, rv, lv, xs, w),
+    )
+    rn = shift(r, 1)
+    rp = shift(l, -1)
+    ra = shift(a, 2)
+    rb = shift(b, -2)
     joined = call(
         join_kernel,
         "join",
-        out((FAR, nodes + WROWS, hidden)),
-        (),
-        (ov, xs, rn, rp, w, rw),
+        out((FAR, nodes + 2 * WUSED, hidden)),
+        (),
+        (ov, xs, ra, rb, rn, rp, w),
     )
     last = lax.all_to_all(joined, "q", 0, 0, tiled=True)
     grad_input, wsum = call(
         finish_kernel,
         "finish",
-        (out((nodes, hidden)), out((plane, WROWS, hidden), jnp.float32)),
+        (out((nodes, hidden)), out((plane, WUSED, hidden), jnp.float32)),
         (),
         (last,),
     )
     grad_input = swap(grad_input)
     wall = lax.all_to_all(wsum, PLANE, 0, 0, tiled=True)
     layer_total, exit_t, bias_total = call(
-        unpack_kernel,
+        functools.partial(unpack_kernel, scale),
         "unpack",
         (
             out((TILE, hidden), jnp.float32),
             out((classes, hidden), jnp.float32),
-            out((1, classes), jnp.float32),
+            out((classes,), jnp.float32),
         ),
-        (scale,),
+        (),
         (wall,),
-        (pltpu.VMEM((plane * WROWS, hidden), jnp.float32),),
-    )
-    return (grad_input[None], layer_total, exit_t.T, bias_total.reshape(classes))
+        (pltpu.VMEM((plane * WUSED, hidden), jnp.float32),),
+    )
+    return (grad_input[None], layer_total, exit_t.T, bias_total)
 
 
 def solution(mesh):

time: 186 us -> 181 us (0.973)
  the two profiles are of different devices: /device:TPU:32 before, /device:TPU:64 now
where the time goes in v5:
time: 181 us; the launch traced here: 180 us
  blocking collectives  74.1 us (41%)
  waiting for transfers between devices  49.6 us (27%)
  starting transfers between devices  44.5 us (25%)
  Pallas kernels  9.91 us (5%)
    all_to_all x1, blocking collectives, local(): last = lax.all_to_all(joined, 'q', 0, 0, tiled=True)  26.8 us
    ppermute x8, starting transfers between devices, shift(): return lax.ppermute(v, RING, [(z, (z + d) % Z) for z in range(Z)])  25.2 us
    all_gather x1, blocking collectives, local(): far = lax.all_gather(feats, 'q', axis=0)  24.5 us
    all_to_all x1, blocking collectives, local(): got = lax.all_to_all(sent, PLANE, 0, 0, tiled=True)  22.8 us
    ppermute x8, waiting for transfers between devices, shift(): return lax.ppermute(v, RING, [(z, (z + d) % Z) for z in range(Z)])  19.2 us
    all_to_all x1, waiting for transfers between devices, local(): lax.all_to_all(partial_value.reshape(plane, nodes, hidden), PLANE, 0, 0,...  17.5 us
    all_to_all x1, starting transfers between devices, local(): lax.all_to_all(partial_value.reshape(plane, nodes, hidden), PLANE, 0, 0,...  7.92 us
    all_to_all x1, waiting for transfers between devices, local(): wall = lax.all_to_all(wsum, PLANE, 0, 0, tiled=True)  7.62 us
  transfers between devices with their start and end apart: 15, of which 8 were waited for; matrix products, arithmetic and copies ran while one was open for 0% of the time, Pallas kernels for 1%

profile of v5, /device:TPU:64, one launch (start us, length us, event | category | flops | bytes accessed | tf_op | source)
XLA Modules:
  0.0 180.4 jit_solution(34735676647654749)
XLA Ops:
  0.6 1.5 collective-permute-start
  2.8 2.3 %pack.1 = bf16[4368,128]{1,0:T(8,128)(2,1)} custom-call(bf16[4096,128]{1,0:T(8,128)(2,1)} %bitcast.24, bf16[256,128]{1,0:T(8,128)(2,1)} %bitcast.26, s32[1,32]{1,0:T(1,128)} %bitcast.27, s32[1,32]{1,0:T(1,128)} %bitcast.28, s32[1,1]{1,0:T(1,128)S(6)} %copy.17.count, s32[1,256]{1,0:T(1,128)} %labels.1, s32[1,256]{1,0:T(1,128)} %mask.1), custom_call_target="tpu_custom_call" | custom-call | tf_op jit(solution)/shard_map/pack/pallas_call | solution.py:149
  5.1 1.9 %collective-permute-start.1 = (bf16[4368,128]{1,0:T(8,128)(2,1)}, bf16[4368,128]{1,0:T(8,128)(2,1)S(1)}, u32[]{:S(2)}, u32[]{:S(2)}) collective-permute-start(bf16[4368,128]{1,0:T(8,128)(2,1)} %pack.1), channel_id=1, source_target_pairs={{0,0},{1,256},{256,1},{257,257},{2,2},{3,258},{258,3},{259,259},{4... | collective-permute-start | bytes 3354632 | tf_op jit(solution)/shard_map/ppermute | solution.py:36
  7.0 24.5 %all-gather = bf16[1024,128]{1,0:T(8,128)(2,1)S(1)} all-gather(bf16[256,128]{1,0:T(8,128)(2,1)S(1)} %collective-permute-done), channel_id=2, replica_groups=mesh['x'=2,'q'=4,'k'=4,'h'=2,'y'=4,'core'=2] {'q'}, dimensions={0}, use_global_device_ids=true | all-gather | bytes 327680 | tf_op jit(solution)/shard_map/all_gather | solution.py:337
  31.5 3.1 %collective-permute-start.3 = (bf16[4,256,128]{2,1,0:T(8,128)(2,1)S(1)}, bf16[4,256,128]{2,1,0:T(8,128)(2,1)S(1)}, u32[]{:S(2)}, u32[]{:S(2)}) collective-permute-start(bf16[4,256,128]{2,1,0:T(8,128)(2,1)S(1)} %bitcast.15), channel_id=1, source_target_pairs={{0,16},{16,32},{32,48},{48,64},{64,80},{80,96},{96,112},{112,128},... | collective-permute-start | bytes 786440 | tf_op jit(solution)/shard_map/ppermute | solution.py:28
  34.6 2.8 %collective-permute-start.2 = (bf16[4,256,128]{2,1,0:T(8,128)(2,1)S(1)}, bf16[4,256,128]{2,1,0:T(8,128)(2,1)S(1)}, u32[]{:S(2)}, u32[]{:S(2)}) collective-permute-start(bf16[4,256,128]{2,1,0:T(8,128)(2,1)S(1)} %bitcast.16), channel_id=1, source_target_pairs={{0,240},{16,0},{32,16},{48,32},{64,48},{80,64},{96,80},{112,96},{1... | collective-permute-start | bytes 786440 | tf_op jit(solution)/shard_map/ppermute | solution.py:28
  37.4 4.8 %collective-permute-start.5 = (bf16[2,256,128]{2,1,0:T(8,128)(2,1)S(1)}, bf16[2,256,128]{2,1,0:T(8,128)(2,1)S(1)}, u32[]{:S(2)}, u32[]{:S(2)}) collective-permute-start(bf16[2,256,128]{2,1,0:T(8,128)(2,1)S(1)} %get-tuple-element.44), channel_id=1, source_target_pairs={{0,32},{16,48},{32,64},{48,80},{64,96},{80,112},{96,128},{112,144}... | collective-permute-start | bytes 393224 | tf_op jit(solution)/shard_map/ppermute | solution.py:28
  42.2 2.0 %collective-permute-start.4 = (bf16[2,256,128]{2,1,0:T(8,128)(2,1)S(1)}, bf16[2,256,128]{2,1,0:T(8,128)(2,1)S(1)}, u32[]{:S(2)}, u32[]{:S(2)}) collective-permute-start(bf16[2,256,128]{2,1,0:T(8,128)(2,1)S(1)} %get-tuple-element.45), channel_id=1, source_target_pairs={{0,224},{16,240},{32,0},{48,16},{64,32},{80,48},{96,64},{112,80},{... | collective-permute-start | bytes 393224 | tf_op jit(solution)/shard_map/ppermute | solution.py:28
  44.2 5.1 %collective-permute-done.5 = bf16[2,256,128]{2,1,0:T(8,128)(2,1)S(1)} collective-permute-done((bf16[2,256,128]{2,1,0:T(8,128)(2,1)S(1)}, bf16[2,256,128]{2,1,0:T(8,128)(2,1)S(1)}, u32[]{:S(2)}, u32[]{:S(2)}) %collective-permute-start.5) | collective-permute-done | bytes 131104 | tf_op jit(solution)/shard_map/ppermute | solution.py:28
  49.3 5.2 %collective-permute-done.4 = bf16[2,256,128]{2,1,0:T(8,128)(2,1)S(1)} collective-permute-done((bf16[2,256,128]{2,1,0:T(8,128)(2,1)S(1)}, bf16[2,256,128]{2,1,0:T(8,128)(2,1)S(1)}, u32[]{:S(2)}, u32[]{:S(2)}) %collective-permute-start.4) | collective-permute-done | bytes 131104 | tf_op jit(solution)/shard_map/ppermute | solution.py:28
  54.6 1.9 %collective-permute-start.6 = (bf16[32,128,128]{2,1,0:T(8,128)(2,1)S(1)}, bf16[32,128,128]{2,1,0:T(8,128)(2,1)S(1)}, u32[]{:S(2)}, u32[]{:S(2)}) collective-permute-start(bf16[32,128,128]{2,1,0:T(8,128)(2,1)S(1)} %window.1.near), channel_id=1, source_target_pairs={{0,1},{1,0},{2,3},{3,2},{4,5},{5,4},{6,7},{7,6},{8,9},{9,8},{10,11... | collective-permute-start | bytes 3145736 | tf_op jit(solution)/shard_map/ppermute | solution.py:32
  56.5 2.6 %collective-permute-done.6.across = bf16[32,128,128]{2,1,0:T(8,128)(2,1)S(1)} collective-permute-done((bf16[32,128,128]{2,1,0:T(8,128)(2,1)S(1)}, bf16[32,128,128]{2,1,0:T(8,128)(2,1)S(1)}, u32[]{:S(2)}, u32[]{:S(2)}) %collective-permute-start.6) | collective-permute-done | bytes 1048608 | tf_op jit(solution)/shard_map/ppermute | solution.py:32
  59.1 2.7 %forward_products.1 = bf16[32,128,128]{2,1,0:T(8,128)(2,1)} custom-call(s32[8,128]{1,0:T(8,128)S(1)} %slice_convert_fusion.ints, bf16[4368,128]{1,0:T(8,128)(2,1)S(1)} %collective-permute-done.1.packed, bf16[32,128,128]{2,1,0:T(8,128)(2,1)S(1)} %window.1.near, bf16[32,128,128]{2,1,0:T(8,128)(2,1)S(1)} %collective-permute-done.6.across), custom_call_target="tpu_custom_call" | custom-call | tf_op jit(solution)/shard_map/forward_products/pallas_call | solution.py:72
  61.9 7.9 %all-to-all-start = ((bf16[16,256,128]{2,1,0:T(8,128)(2,1)}), bf16[16,256,128]{2,1,0:T(8,128)(2,1)S(1)}, u32[]{:S(2)}, u32[]{:S(2)}) async-start(bf16[16,256,128]{2,1,0:T(8,128)(2,1)} %bitcast.11), calls=%async_computation | async-start | bytes 2097152 | tf_op jit(solution)/shard_map/all_to_all | solution.py:363
  69.9 17.5 %all-to-all-done.parts = bf16[16,256,128]{2,1,0:T(8,128)(2,1)S(1)} async-done(((bf16[16,256,128]{2,1,0:T(8,128)(2,1)}), bf16[16,256,128]{2,1,0:T(8,128)(2,1)S(1)}, u32[]{:S(2)}, u32[]{:S(2)}) %all-to-all-start) | async-done | bytes 1048608 | tf_op jit(solution)/shard_map/all_to_all | solution.py:363
  87.4 0.8 dense.1
  88.2 22.8 %all_to_all.20.g = bf16[16,288,128]{2,1,0:T(8,128)(2,1)S(1)} all-to-all(bf16[16,288,128]{2,1,0:T(8,128)(2,1)S(1)} %dense.1), channel_id=1, replica_groups=mesh['x'=2,'q'=4,'k'=4,'h'=2,'y'=4,'core'=2] {'h','y','x'}, dimensions={0} | all-to-all | bytes 2359296 | tf_op jit(solution)/shard_map/all_to_all | solution.py:374
  111.0 2.2 %backward_products.1 = (bf16[4128,128]{1,0:T(8,128)(2,1)S(1)}, bf16[8,128,128]{2,1,0:T(8,128)(2,1)S(1)}, bf16[8,128,128]{2,1,0:T(8,128)(2,1)S(1)}, bf16[8,128,12...) custom-call(s32[8,128]{1,0:T(8,128)S(1)} %slice_convert_fusion.ints, ...), custom_call_target="tpu_custom_call" | custom-call | tf_op jit(solution)/shard_map/backward_products/pallas_call | solution.py:72
  113.3 1.9 %collective-permute-start.7 = (bf16[4128,128]{1,0:T(8,128)(2,1)S(1)}, bf16[4128,128]{1,0:T(8,128)(2,1)S(1)}, u32[]{:S(2)}, u32[]{:S(2)}) collective-permute-start(bf16[4128,128]{1,0:T(8,128)(2,1)S(1)} %get-tuple-element.29), channel_id=1, source_target_pairs={{0,1},{1,0},{2,3},{3,2},{4,5},{5,4},{6,7},{7,6},{8,9},{9,8},{10,11... | collective-permute-start | bytes 3170312 | tf_op jit(solution)/shard_map/ppermute | solution.py:32
  115.2 2.6 %collective-permute-done.7.xs = bf16[4128,128]{1,0:T(8,128)(2,1)S(1)} collective-permute-done((bf16[4128,128]{1,0:T(8,128)(2,1)S(1)}, bf16[4128,128]{1,0:T(8,128)(2,1)S(1)}, u32[]{:S(2)}, u32[]{:S(2)}) %collective-permute-start.7) | collective-permute-done | bytes 1056800 | tf_op jit(solution)/shard_map/ppermute | solution.py:32
  118.0 1.9 %collective-permute-start.10 = (bf16[1056,128]{1,0:T(8,128)(2,1)S(1)}, bf16[1056,128]{1,0:T(8,128)(2,1)S(1)}, u32[]{:S(2)}, u32[]{:S(2)}) collective-permute-start(bf16[1056,128]{1,0:T(8,128)(2,1)S(1)} %get-tuple-element.36), channel_id=1, source_target_pairs={{0,16},{16,32},{32,48},{48,64},{64,80},{80,96},{96,112},{112,128},... | collective-permute-start | bytes 811016 | tf_op jit(solution)/shard_map/ppermute | solution.py:28
  120.0 3.9 %collective-permute-start.11 = (bf16[1056,128]{1,0:T(8,128)(2,1)S(1)}, bf16[1056,128]{1,0:T(8,128)(2,1)S(1)}, u32[]{:S(2)}, u32[]{:S(2)}) collective-permute-start(bf16[1056,128]{1,0:T(8,128)(2,1)S(1)} %get-tuple-element.37), channel_id=1, source_target_pairs={{0,240},{16,0},{32,16},{48,32},{64,48},{80,64},{96,80},{112,96},{1... | collective-permute-start | bytes 811016 | tf_op jit(solution)/shard_map/ppermute | solution.py:28
  123.9 4.0 %collective-permute-start.8 = (bf16[544,128]{1,0:T(8,128)(2,1)S(1)}, bf16[544,128]{1,0:T(8,128)(2,1)S(1)}, u32[]{:S(2)}, u32[]{:S(2)}) collective-permute-start(bf16[544,128]{1,0:T(8,128)(2,1)S(1)} %get-tuple-element.34), channel_id=1, source_target_pairs={{0,32},{16,48},{32,64},{48,80},{64,96},{80,112},{96,128},{112,144}... | collective-permute-start | bytes 417800 | tf_op jit(solution)/shard_map/ppermute | solution.py:28
  127.9 2.8 %collective-permute-start.9 = (bf16[544,128]{1,0:T(8,128)(2,1)S(1)}, bf16[544,128]{1,0:T(8,128)(2,1)S(1)}, u32[]{:S(2)}, u32[]{:S(2)}) collective-permute-start(bf16[544,128]{1,0:T(8,128)(2,1)S(1)} %get-tuple-element.35), channel_id=1, source_target_pairs={{0,224},{16,240},{32,0},{48,16},{64,32},{80,48},{96,64},{112,80},{... | collective-permute-start | bytes 417800 | tf_op jit(solution)/shard_map/ppermute | solution.py:28
  130.7 3.4 %collective-permute-done.8.ra = bf16[544,128]{1,0:T(8,128)(2,1)S(1)} collective-permute-done((bf16[544,128]{1,0:T(8,128)(2,1)S(1)}, bf16[544,128]{1,0:T(8,128)(2,1)S(1)}, u32[]{:S(2)}, u32[]{:S(2)}) %collective-permute-start.8) | collective-permute-done | bytes 139296 | tf_op jit(solution)/shard_map/ppermute | solution.py:28
  134.0 5.5 %collective-permute-done.9.rb = bf16[544,128]{1,0:T(8,128)(2,1)S(1)} collective-permute-done((bf16[544,128]{1,0:T(8,128)(2,1)S(1)}, bf16[544,128]{1,0:T(8,128)(2,1)S(1)}, u32[]{:S(2)}, u32[]{:S(2)}) %collective-permute-start.9) | collective-permute-done | bytes 139296 | tf_op jit(solution)/shard_map/ppermute | solution.py:28
  139.7 26.8 %all_to_all.21.parts = bf16[4,304,128]{2,1,0:T(8,128)(2,1)S(1)} all-to-all(bf16[4,304,128]{2,1,0:T(8,128)(2,1)S(1)} %join.1), channel_id=1, replica_groups=mesh['x'=2,'q'=4,'k'=4,'h'=2,'y'=4,'core'=2] {'q'}, dimensions={0} | all-to-all | bytes 622592 | tf_op jit(solution)/shard_map/all_to_all | solution.py:412
  166.5 0.7 finish.1
  167.3 3.5 %all-to-all-start.3 = ((f32[16,24,128]{2,1,0:T(8,128)}), f32[16,24,128]{2,1,0:T(8,128)S(1)}, u32[]{:S(2)}, u32[]{:S(2)}) async-start(f32[16,24,128]{2,1,0:T(8,128)} %get-tuple-element.40), calls=%async_computation.3 | async-start | bytes 393216 | tf_op jit(solution)/shard_map/all_to_all | solution.py:421
  170.8 0.7 collective-permute-start.12
  171.5 7.6 %all-to-all-done.3.wall = f32[16,24,128]{2,1,0:T(8,128)S(1)} async-done(((f32[16,24,128]{2,1,0:T(8,128)}), f32[16,24,128]{2,1,0:T(8,128)S(1)}, u32[]{:S(2)}, u32[]{:S(2)}) %all-to-all-start.3) | async-done | bytes 196640 | tf_op jit(solution)/shard_map/all_to_all | solution.py:421
  179.1 0.7 unpack.1
  (21 shorter events, 1.2 us)
Async XLA Ops:
  0.6 4.5 %collective-permute-start = (bf16[256,128]{1,0:T(8,128)(2,1)}, bf16[256,128]{1,0:T(8,128)(2,1)S(1)}, u32[]{:S(2)}, u32[]{:S(2)}) collective-permute-start(bf16[256,128]{1,0:T(8,128)(2,1)} %bitcast.30), channel_id=1, source_target_pairs={{0,0},{1,256},{256,1},{257,257},{2,2},{3,258},{258,3},{259,259},{4... | collective-permute-start | bytes 196616 | tf_op jit(solution)/shard_map/ppermute | solution.py:36
  5.1 26.4 %collective-permute-start.1 = (bf16[4368,128]{1,0:T(8,128)(2,1)}, bf16[4368,128]{1,0:T(8,128)(2,1)S(1)}, u32[]{:S(2)}, u32[]{:S(2)}) collective-permute-start(bf16[4368,128]{1,0:T(8,128)(2,1)} %pack.1), channel_id=1, source_target_pairs={{0,0},{1,256},{256,1},{257,257},{2,2},{3,258},{258,3},{259,259},{4... | collective-permute-start | bytes 3354632 | tf_op jit(solution)/shard_map/ppermute | solution.py:36
  31.5 23.0 %collective-permute-start.3 = (bf16[4,256,128]{2,1,0:T(8,128)(2,1)S(1)}, bf16[4,256,128]{2,1,0:T(8,128)(2,1)S(1)}, u32[]{:S(2)}, u32[]{:S(2)}) collective-permute-start(bf16[4,256,128]{2,1,0:T(8,128)(2,1)S(1)} %bitcast.15), channel_id=1, source_target_pairs={{0,16},{16,32},{32,48},{48,64},{64,80},{80,96},{96,112},{112,128},... | collective-permute-start | bytes 786440 | tf_op jit(solution)/shard_map/ppermute | solution.py:28
  34.6 19.9 %collective-permute-start.2 = (bf16[4,256,128]{2,1,0:T(8,128)(2,1)S(1)}, bf16[4,256,128]{2,1,0:T(8,128)(2,1)S(1)}, u32[]{:S(2)}, u32[]{:S(2)}) collective-permute-start(bf16[4,256,128]{2,1,0:T(8,128)(2,1)S(1)} %bitcast.16), channel_id=1, source_target_pairs={{0,240},{16,0},{32,16},{48,32},{64,48},{80,64},{96,80},{112,96},{1... | collective-permute-start | bytes 786440 | tf_op jit(solution)/shard_map/ppermute | solution.py:28
  37.4 11.9 %collective-permute-start.5 = (bf16[2,256,128]{2,1,0:T(8,128)(2,1)S(1)}, bf16[2,256,128]{2,1,0:T(8,128)(2,1)S(1)}, u32[]{:S(2)}, u32[]{:S(2)}) collective-permute-start(bf16[2,256,128]{2,1,0:T(8,128)(2,1)S(1)} %get-tuple-element.44), channel_id=1, source_target_pairs={{0,32},{16,48},{32,64},{48,80},{64,96},{80,112},{96,128},{112,144}... | collective-permute-start | bytes 393224 | tf_op jit(solution)/shard_map/ppermute | solution.py:28
  42.2 12.3 %collective-permute-start.4 = (bf16[2,256,128]{2,1,0:T(8,128)(2,1)S(1)}, bf16[2,256,128]{2,1,0:T(8,128)(2,1)S(1)}, u32[]{:S(2)}, u32[]{:S(2)}) collective-permute-start(bf16[2,256,128]{2,1,0:T(8,128)(2,1)S(1)} %get-tuple-element.45), channel_id=1, source_target_pairs={{0,224},{16,240},{32,0},{48,16},{64,32},{80,48},{96,64},{112,80},{... | collective-permute-start | bytes 393224 | tf_op jit(solution)/shard_map/ppermute | solution.py:28
  54.6 4.6 %collective-permute-start.6 = (bf16[32,128,128]{2,1,0:T(8,128)(2,1)S(1)}, bf16[32,128,128]{2,1,0:T(8,128)(2,1)S(1)}, u32[]{:S(2)}, u32[]{:S(2)}) collective-permute-start(bf16[32,128,128]{2,1,0:T(8,128)(2,1)S(1)} %window.1.near), channel_id=1, source_target_pairs={{0,1},{1,0},{2,3},{3,2},{4,5},{5,4},{6,7},{7,6},{8,9},{9,8},{10,11... | collective-permute-start | bytes 3145736 | tf_op jit(solution)/shard_map/ppermute | solution.py:32
  61.9 7.9 %copy-start.2 = (bf16[128,172]{0,1:T(8,128)(2,1)S(1)}, bf16[128,172]{0,1:T(8,128)(2,1)}, u32[]{:S(2)}) copy-start(bf16[128,172]{0,1:T(8,128)(2,1)} %param.17) | copy-start | bytes 132100
  61.9 25.6 %copy-start = (bf16[128,128]{1,0:T(8,128)(2,1)S(1)}, bf16[128,128]{1,0:T(8,128)(2,1)}, u32[]{:S(2)}) copy-start(bf16[128,128]{1,0:T(8,128)(2,1)} %weight.1) | copy-start | bytes 98308
  61.9 25.6 %copy-start.1 = (f32[172]{0:T(256)S(1)}, f32[172]{0:T(256)}, u32[]{:S(2)}) copy-start(f32[172]{0:T(256)} %param.18) | copy-start | bytes 2068
  61.9 25.6 %all-to-all-start = ((bf16[16,256,128]{2,1,0:T(8,128)(2,1)}), bf16[16,256,128]{2,1,0:T(8,128)(2,1)S(1)}, u32[]{:S(2)}, u32[]{:S(2)}) async-start(bf16[16,256,128]{2,1,0:T(8,128)(2,1)} %bitcast.11), calls=%async_computation | async-start | bytes 2097152 | tf_op jit(solution)/shard_map/all_to_all | solution.py:363
  113.3 4.6 %collective-permute-start.7 = (bf16[4128,128]{1,0:T(8,128)(2,1)S(1)}, bf16[4128,128]{1,0:T(8,128)(2,1)S(1)}, u32[]{:S(2)}, u32[]{:S(2)}) collective-permute-start(bf16[4128,128]{1,0:T(8,128)(2,1)S(1)} %get-tuple-element.29), channel_id=1, source_target_pairs={{0,1},{1,0},{2,3},{3,2},{4,5},{5,4},{6,7},{7,6},{8,9},{9,8},{10,11... | collective-permute-start | bytes 3170312 | tf_op jit(solution)/shard_map/ppermute | solution.py:32
  118.0 21.5 %collective-permute-start.10 = (bf16[1056,128]{1,0:T(8,128)(2,1)S(1)}, bf16[1056,128]{1,0:T(8,128)(2,1)S(1)}, u32[]{:S(2)}, u32[]{:S(2)}) collective-permute-start(bf16[1056,128]{1,0:T(8,128)(2,1)S(1)} %get-tuple-element.36), channel_id=1, source_target_pairs={{0,16},{16,32},{32,48},{48,64},{64,80},{80,96},{96,112},{112,128},... | collective-permute-start | bytes 811016 | tf_op jit(solution)/shard_map/ppermute | solution.py:28
  120.0 19.6 %collective-permute-start.11 = (bf16[1056,128]{1,0:T(8,128)(2,1)S(1)}, bf16[1056,128]{1,0:T(8,128)(2,1)S(1)}, u32[]{:S(2)}, u32[]{:S(2)}) collective-permute-start(bf16[1056,128]{1,0:T(8,128)(2,1)S(1)} %get-tuple-element.37), channel_id=1, source_target_pairs={{0,240},{16,0},{32,16},{48,32},{64,48},{80,64},{96,80},{112,96},{1... | collective-permute-start | bytes 811016 | tf_op jit(solution)/shard_map/ppermute | solution.py:28
  123.9 10.1 %collective-permute-start.8 = (bf16[544,128]{1,0:T(8,128)(2,1)S(1)}, bf16[544,128]{1,0:T(8,128)(2,1)S(1)}, u32[]{:S(2)}, u32[]{:S(2)}) collective-permute-start(bf16[544,128]{1,0:T(8,128)(2,1)S(1)} %get-tuple-element.34), channel_id=1, source_target_pairs={{0,32},{16,48},{32,64},{48,80},{64,96},{80,112},{96,128},{112,144}... | collective-permute-start | bytes 417800 | tf_op jit(solution)/shard_map/ppermute | solution.py:28
  127.9 11.7 %collective-permute-start.9 = (bf16[544,128]{1,0:T(8,128)(2,1)S(1)}, bf16[544,128]{1,0:T(8,128)(2,1)S(1)}, u32[]{:S(2)}, u32[]{:S(2)}) collective-permute-start(bf16[544,128]{1,0:T(8,128)(2,1)S(1)} %get-tuple-element.35), channel_id=1, source_target_pairs={{0,224},{16,240},{32,0},{48,16},{64,32},{80,48},{96,64},{112,80},{... | collective-permute-start | bytes 417800 | tf_op jit(solution)/shard_map/ppermute | solution.py:28
  167.3 11.8 %all-to-all-start.3 = ((f32[16,24,128]{2,1,0:T(8,128)}), f32[16,24,128]{2,1,0:T(8,128)S(1)}, u32[]{:S(2)}, u32[]{:S(2)}) async-start(f32[16,24,128]{2,1,0:T(8,128)} %get-tuple-element.40), calls=%async_computation.3 | async-start | bytes 393216 | tf_op jit(solution)/shard_map/all_to_all | solution.py:421
  170.8 0.7 collective-permute-start.12

commit v6 on v5

--- a/solution.py
+++ b/solution.py
@@ -21,7 +21,7 @@
 NT = (((1,), (1,)), ((), ()))
 TN = (((0,), (0,)), ((), ()))
 
-VMEM_LIMIT = 48 * 1024 * 1024
+VMEM_LIMIT = 24 * 1024 * 1024
 
 
 def shift(v, d):
@@ -265,8 +265,8 @@
         o[j, 2 * TILE : 2 * TILE + 2 * WUSED] = both
 
 
-def finish_kernel(parts, o, w):
-    nodes = o.shape[0]
+def total_kernel(parts, w):
+    nodes = parts.shape[1] - 2 * WUSED
     both = slice(nodes, nodes + 2 * WUSED)
     total = f32(parts[0, both])
     for j in range(1, FAR):
@@ -279,13 +279,18 @@
     total = total[0:WUSED] + other[WUSED : 2 * WUSED]
     for j in range(w.shape[0]):
         w[j] = total
+
+
+def finish_kernel(parts, o):
+    nodes = o.shape[0]
     s = f32(parts[0, 0:nodes])
     for j in range(1, FAR):
         s += f32(parts[j, 0:nodes])
     o[...] = bf(s)
 
 
-def unpack_kernel(scale, wall, layer, exit_t, bias, wb):
+def unpack_kernel(scale, wall, grad, o, layer, exit_t, bias, wb):
+    o[...] = grad[...]
     for j in range(wall.shape[0]):
         wb[j * WUSED : (j + 1) * WUSED] = wall[j] * scale
     classes = exit_t.shape[0]
@@ -410,25 +415,22 @@
         (ov, xs, ra, rb, rn, rp, w),
     )
     last = lax.all_to_all(joined, "q", 0, 0, tiled=True)
-    grad_input, wsum = call(
-        finish_kernel,
-        "finish",
-        (out((nodes, hidden)), out((plane, WUSED, hidden), jnp.float32)),
-        (),
-        (last,),
-    )
-    grad_input = swap(grad_input)
+    wsum = call(
+        total_kernel, "total", out((plane, WUSED, hidden), jnp.float32), (), (last,)
+    )
     wall = lax.all_to_all(wsum, PLANE, 0, 0, tiled=True)
-    layer_total, exit_t, bias_total = call(
+    grad_input = swap(call(finish_kernel, "finish", out((nodes, hidden)), (), (last,)))
+    grad_input, layer_total, exit_t, bias_total = call(
         functools.partial(unpack_kernel, scale),
         "unpack",
         (
+            out((nodes, hidden)),
             out((TILE, hidden), jnp.float32),
             out((classes, hidden), jnp.float32),
             out((classes,), jnp.float32),
         ),
         (),
-        (wall,),
+        (wall, grad_input),
         (pltpu.VMEM((plane * WUSED, hidden), jnp.float32),),
     )
     return (grad_input[None], layer_total, exit_t.T, bias_total)

time: 181 us -> 181 us (level)
    pallas_call x8 -> x9, Pallas kernels: 7.6 us -> 7.63 us  [call(): pl.pallas_call(kernel, out_shape=outs, in_specs=[smem()] * len(scalars) +...]
where the time goes in v6:
time: 181 us; the launch traced here: 180 us
  blocking collectives  74.1 us (41%)
  waiting for transfers between devices  48.1 us (27%)
  starting transfers between devices  45.9 us (25%)
  Pallas kernels  9.95 us (5%)
    all_to_all x1, blocking collectives, local(): last = lax.all_to_all(joined, 'q', 0, 0, tiled=True)  26.8 us
    ppermute x8, starting transfers between devices, shift(): return lax.ppermute(v, RING, [(z, (z + d) % Z) for z in range(Z)])  26.5 us
    all_gather x1, blocking collectives, local(): far = lax.all_gather(feats, 'q', axis=0)  24.5 us
    all_to_all x1, blocking collectives, local(): got = lax.all_to_all(sent, PLANE, 0, 0, tiled=True)  22.8 us
    ppermute x8, waiting for transfers between devices, shift(): return lax.ppermute(v, RING, [(z, (z + d) % Z) for z in range(Z)])  17.8 us
    all_to_all x1, waiting for transfers between devices, local(): lax.all_to_all(partial_value.reshape(plane, nodes, hidden), PLANE, 0, 0,...  17.5 us
    all_to_all x1, starting transfers between devices, local(): lax.all_to_all(partial_value.reshape(plane, nodes, hidden), PLANE, 0, 0,...  7.98 us
    pallas_call x9, Pallas kernels, call(): pl.pallas_call(kernel, out_shape=outs, in_specs=[smem()] * len(scalars) +...  7.63 us
  transfers between devices with their start and end apart: 15, of which 8 were waited for; matrix products, arithmetic and copies ran while one was open for 0% of the time, Pallas kernels for 1%

profile of v6, /device:TPU:64, one launch (start us, length us, event | category | flops | bytes accessed | tf_op | source)
XLA Modules:
  0.0 179.8 jit_solution(4696171171179014657)
XLA Ops:
  0.6 1.5 collective-permute-start
  2.8 2.3 %pack.1 = bf16[4368,128]{1,0:T(8,128)(2,1)} custom-call(bf16[4096,128]{1,0:T(8,128)(2,1)} %bitcast.24, bf16[256,128]{1,0:T(8,128)(2,1)} %bitcast.25, s32[1,32]{1,0:T(1,128)} %bitcast.26, s32[1,32]{1,0:T(1,128)} %bitcast.27, s32[1,1]{1,0:T(1,128)S(6)} %copy.16.count, s32[1,256]{1,0:T(1,128)} %labels.1, s32[1,256]{1,0:T(1,128)} %mask.1), custom_call_target="tpu_custom_call" | custom-call | tf_op jit(solution)/shard_map/pack/pallas_call | solution.py:149
  5.1 1.9 %collective-permute-start.1 = (bf16[4368,128]{1,0:T(8,128)(2,1)}, bf16[4368,128]{1,0:T(8,128)(2,1)S(1)}, u32[]{:S(2)}, u32[]{:S(2)}) collective-permute-start(bf16[4368,128]{1,0:T(8,128)(2,1)} %pack.1), channel_id=1, source_target_pairs={{0,0},{1,256},{256,1},{257,257},{2,2},{3,258},{258,3},{259,259},{4... | collective-permute-start | bytes 3354632 | tf_op jit(solution)/shard_map/ppermute | solution.py:36
  7.0 24.5 %all-gather = bf16[1024,128]{1,0:T(8,128)(2,1)S(1)} all-gather(bf16[256,128]{1,0:T(8,128)(2,1)S(1)} %collective-permute-done), channel_id=2, replica_groups=mesh['x'=2,'q'=4,'k'=4,'h'=2,'y'=4,'core'=2] {'q'}, dimensions={0}, use_global_device_ids=true | all-gather | bytes 327680 | tf_op jit(solution)/shard_map/all_gather | solution.py:342
  31.5 2.9 %collective-permute-start.3 = (bf16[4,256,128]{2,1,0:T(8,128)(2,1)S(1)}, bf16[4,256,128]{2,1,0:T(8,128)(2,1)S(1)}, u32[]{:S(2)}, u32[]{:S(2)}) collective-permute-start(bf16[4,256,128]{2,1,0:T(8,128)(2,1)S(1)} %bitcast.15), channel_id=1, source_target_pairs={{0,16},{16,32},{32,48},{48,64},{64,80},{80,96},{96,112},{112,128},... | collective-permute-start | bytes 786440 | tf_op jit(solution)/shard_map/ppermute | solution.py:28
  34.5 2.9 %collective-permute-start.2 = (bf16[4,256,128]{2,1,0:T(8,128)(2,1)S(1)}, bf16[4,256,128]{2,1,0:T(8,128)(2,1)S(1)}, u32[]{:S(2)}, u32[]{:S(2)}) collective-permute-start(bf16[4,256,128]{2,1,0:T(8,128)(2,1)S(1)} %bitcast.16), channel_id=1, source_target_pairs={{0,240},{16,0},{32,16},{48,32},{64,48},{80,64},{96,80},{112,96},{1... | collective-permute-start | bytes 786440 | tf_op jit(solution)/shard_map/ppermute | solution.py:28
  37.4 6.2 %collective-permute-start.5 = (bf16[2,256,128]{2,1,0:T(8,128)(2,1)S(1)}, bf16[2,256,128]{2,1,0:T(8,128)(2,1)S(1)}, u32[]{:S(2)}, u32[]{:S(2)}) collective-permute-start(bf16[2,256,128]{2,1,0:T(8,128)(2,1)S(1)} %get-tuple-element.42), channel_id=1, source_target_pairs={{0,32},{16,48},{32,64},{48,80},{64,96},{80,112},{96,128},{112,144}... | collective-permute-start | bytes 393224 | tf_op jit(solution)/shard_map/ppermute | solution.py:28
  43.6 1.9 %collective-permute-start.4 = (bf16[2,256,128]{2,1,0:T(8,128)(2,1)S(1)}, bf16[2,256,128]{2,1,0:T(8,128)(2,1)S(1)}, u32[]{:S(2)}, u32[]{:S(2)}) collective-permute-start(bf16[2,256,128]{2,1,0:T(8,128)(2,1)S(1)} %get-tuple-element.43), channel_id=1, source_target_pairs={{0,224},{16,240},{32,0},{48,16},{64,32},{80,48},{96,64},{112,80},{... | collective-permute-start | bytes 393224 | tf_op jit(solution)/shard_map/ppermute | solution.py:28
  45.5 2.9 %collective-permute-done.5 = bf16[2,256,128]{2,1,0:T(8,128)(2,1)S(1)} collective-permute-done((bf16[2,256,128]{2,1,0:T(8,128)(2,1)S(1)}, bf16[2,256,128]{2,1,0:T(8,128)(2,1)S(1)}, u32[]{:S(2)}, u32[]{:S(2)}) %collective-permute-start.5) | collective-permute-done | bytes 131104 | tf_op jit(solution)/shard_map/ppermute | solution.py:28
  48.4 6.0 %collective-permute-done.4 = bf16[2,256,128]{2,1,0:T(8,128)(2,1)S(1)} collective-permute-done((bf16[2,256,128]{2,1,0:T(8,128)(2,1)S(1)}, bf16[2,256,128]{2,1,0:T(8,128)(2,1)S(1)}, u32[]{:S(2)}, u32[]{:S(2)}) %collective-permute-start.4) | collective-permute-done | bytes 131104 | tf_op jit(solution)/shard_map/ppermute | solution.py:28
  54.5 1.9 %collective-permute-start.6 = (bf16[32,128,128]{2,1,0:T(8,128)(2,1)S(1)}, bf16[32,128,128]{2,1,0:T(8,128)(2,1)S(1)}, u32[]{:S(2)}, u32[]{:S(2)}) collective-permute-start(bf16[32,128,128]{2,1,0:T(8,128)(2,1)S(1)} %window.1.near), channel_id=1, source_target_pairs={{0,1},{1,0},{2,3},{3,2},{4,5},{5,4},{6,7},{7,6},{8,9},{9,8},{10,11... | collective-permute-start | bytes 3145736 | tf_op jit(solution)/shard_map/ppermute | solution.py:32
  56.5 2.6 %collective-permute-done.6.across = bf16[32,128,128]{2,1,0:T(8,128)(2,1)S(1)} collective-permute-done((bf16[32,128,128]{2,1,0:T(8,128)(2,1)S(1)}, bf16[32,128,128]{2,1,0:T(8,128)(2,1)S(1)}, u32[]{:S(2)}, u32[]{:S(2)}) %collective-permute-start.6) | collective-permute-done | bytes 1048608 | tf_op jit(solution)/shard_map/ppermute | solution.py:32
  59.1 2.7 %forward_products.1 = bf16[32,128,128]{2,1,0:T(8,128)(2,1)} custom-call(s32[8,128]{1,0:T(8,128)S(1)} %slice_convert_fusion.ints, bf16[4368,128]{1,0:T(8,128)(2,1)S(1)} %collective-permute-done.1.packed, bf16[32,128,128]{2,1,0:T(8,128)(2,1)S(1)} %window.1.near, bf16[32,128,128]{2,1,0:T(8,128)(2,1)S(1)} %collective-permute-done.6.across), custom_call_target="tpu_custom_call" | custom-call | tf_op jit(solution)/shard_map/forward_products/pallas_call | solution.py:72
  61.8 8.0 %all-to-all-start = ((bf16[16,256,128]{2,1,0:T(8,128)(2,1)}), bf16[16,256,128]{2,1,0:T(8,128)(2,1)S(1)}, u32[]{:S(2)}, u32[]{:S(2)}) async-start(bf16[16,256,128]{2,1,0:T(8,128)(2,1)} %bitcast.11), calls=%async_computation | async-start | bytes 2097152 | tf_op jit(solution)/shard_map/all_to_all | solution.py:368
  69.9 17.5 %all-to-all-done.parts = bf16[16,256,128]{2,1,0:T(8,128)(2,1)S(1)} async-done(((bf16[16,256,128]{2,1,0:T(8,128)(2,1)}), bf16[16,256,128]{2,1,0:T(8,128)(2,1)S(1)}, u32[]{:S(2)}, u32[]{:S(2)}) %all-to-all-start) | async-done | bytes 1048608 | tf_op jit(solution)/shard_map/all_to_all | solution.py:368
  87.4 0.8 dense.1
  88.2 22.8 %all_to_all.20.g = bf16[16,288,128]{2,1,0:T(8,128)(2,1)S(1)} all-to-all(bf16[16,288,128]{2,1,0:T(8,128)(2,1)S(1)} %dense.1), channel_id=1, replica_groups=mesh['x'=2,'q'=4,'k'=4,'h'=2,'y'=4,'core'=2] {'h','y','x'}, dimensions={0} | all-to-all | bytes 2359296 | tf_op jit(solution)/shard_map/all_to_all | solution.py:379
  111.1 2.2 %backward_products.1 = (bf16[4128,128]{1,0:T(8,128)(2,1)S(1)}, bf16[8,128,128]{2,1,0:T(8,128)(2,1)S(1)}, bf16[8,128,128]{2,1,0:T(8,128)(2,1)S(1)}, bf16[8,128,12...) custom-call(s32[8,128]{1,0:T(8,128)S(1)} %slice_convert_fusion.ints, ...), custom_call_target="tpu_custom_call" | custom-call | tf_op jit(solution)/shard_map/backward_products/pallas_call | solution.py:72
  113.3 1.9 %collective-permute-start.7 = (bf16[4128,128]{1,0:T(8,128)(2,1)S(1)}, bf16[4128,128]{1,0:T(8,128)(2,1)S(1)}, u32[]{:S(2)}, u32[]{:S(2)}) collective-permute-start(bf16[4128,128]{1,0:T(8,128)(2,1)S(1)} %get-tuple-element.28), channel_id=1, source_target_pairs={{0,1},{1,0},{2,3},{3,2},{4,5},{5,4},{6,7},{7,6},{8,9},{9,8},{10,11... | collective-permute-start | bytes 3170312 | tf_op jit(solution)/shard_map/ppermute | solution.py:32
  115.2 2.6 %collective-permute-done.7.xs = bf16[4128,128]{1,0:T(8,128)(2,1)S(1)} collective-permute-done((bf16[4128,128]{1,0:T(8,128)(2,1)S(1)}, bf16[4128,128]{1,0:T(8,128)(2,1)S(1)}, u32[]{:S(2)}, u32[]{:S(2)}) %collective-permute-start.7) | collective-permute-done | bytes 1056800 | tf_op jit(solution)/shard_map/ppermute | solution.py:32
  118.1 1.9 %collective-permute-start.10 = (bf16[1056,128]{1,0:T(8,128)(2,1)S(1)}, bf16[1056,128]{1,0:T(8,128)(2,1)S(1)}, u32[]{:S(2)}, u32[]{:S(2)}) collective-permute-start(bf16[1056,128]{1,0:T(8,128)(2,1)S(1)} %get-tuple-element.35), channel_id=1, source_target_pairs={{0,16},{16,32},{32,48},{48,64},{64,80},{80,96},{96,112},{112,128},... | collective-permute-start | bytes 811016 | tf_op jit(solution)/shard_map/ppermute | solution.py:28
  120.0 3.9 %collective-permute-start.11 = (bf16[1056,128]{1,0:T(8,128)(2,1)S(1)}, bf16[1056,128]{1,0:T(8,128)(2,1)S(1)}, u32[]{:S(2)}, u32[]{:S(2)}) collective-permute-start(bf16[1056,128]{1,0:T(8,128)(2,1)S(1)} %get-tuple-element.36), channel_id=1, source_target_pairs={{0,240},{16,0},{32,16},{48,32},{64,48},{80,64},{96,80},{112,96},{1... | collective-permute-start | bytes 811016 | tf_op jit(solution)/shard_map/ppermute | solution.py:28
  123.9 4.0 %collective-permute-start.8 = (bf16[544,128]{1,0:T(8,128)(2,1)S(1)}, bf16[544,128]{1,0:T(8,128)(2,1)S(1)}, u32[]{:S(2)}, u32[]{:S(2)}) collective-permute-start(bf16[544,128]{1,0:T(8,128)(2,1)S(1)} %get-tuple-element.33), channel_id=1, source_target_pairs={{0,32},{16,48},{32,64},{48,80},{64,96},{80,112},{96,128},{112,144}... | collective-permute-start | bytes 417800 | tf_op jit(solution)/shard_map/ppermute | solution.py:28
  127.9 2.8 %collective-permute-start.9 = (bf16[544,128]{1,0:T(8,128)(2,1)S(1)}, bf16[544,128]{1,0:T(8,128)(2,1)S(1)}, u32[]{:S(2)}, u32[]{:S(2)}) collective-permute-start(bf16[544,128]{1,0:T(8,128)(2,1)S(1)} %get-tuple-element.34), channel_id=1, source_target_pairs={{0,224},{16,240},{32,0},{48,16},{64,32},{80,48},{96,64},{112,80},{... | collective-permute-start | bytes 417800 | tf_op jit(solution)/shard_map/ppermute | solution.py:28
  130.7 3.4 %collective-permute-done.8.ra = bf16[544,128]{1,0:T(8,128)(2,1)S(1)} collective-permute-done((bf16[544,128]{1,0:T(8,128)(2,1)S(1)}, bf16[544,128]{1,0:T(8,128)(2,1)S(1)}, u32[]{:S(2)}, u32[]{:S(2)}) %collective-permute-start.8) | collective-permute-done | bytes 139296 | tf_op jit(solution)/shard_map/ppermute | solution.py:28
  134.1 5.5 %collective-permute-done.9.rb = bf16[544,128]{1,0:T(8,128)(2,1)S(1)} collective-permute-done((bf16[544,128]{1,0:T(8,128)(2,1)S(1)}, bf16[544,128]{1,0:T(8,128)(2,1)S(1)}, u32[]{:S(2)}, u32[]{:S(2)}) %collective-permute-start.9) | collective-permute-done | bytes 139296 | tf_op jit(solution)/shard_map/ppermute | solution.py:28
  139.7 26.8 %all_to_all.21.parts = bf16[4,304,128]{2,1,0:T(8,128)(2,1)S(1)} all-to-all(bf16[4,304,128]{2,1,0:T(8,128)(2,1)S(1)} %join.1), channel_id=1, replica_groups=mesh['x'=2,'q'=4,'k'=4,'h'=2,'y'=4,'core'=2] {'q'}, dimensions={0} | all-to-all | bytes 622592 | tf_op jit(solution)/shard_map/all_to_all | solution.py:417
  166.6 0.7 total.1
  167.2 3.5 %all-to-all-start.3 = ((f32[16,24,128]{2,1,0:T(8,128)}), f32[16,24,128]{2,1,0:T(8,128)S(1)}, u32[]{:S(2)}, u32[]{:S(2)}) async-start(f32[16,24,128]{2,1,0:T(8,128)} %total.1), calls=%async_computation.3 | async-start | bytes 393216 | tf_op jit(solution)/shard_map/all_to_all | solution.py:421
  170.8 0.7 collective-permute-start.12
  171.5 7.6 %all-to-all-done.3.wall = f32[16,24,128]{2,1,0:T(8,128)S(1)} async-done(((f32[16,24,128]{2,1,0:T(8,128)}), f32[16,24,128]{2,1,0:T(8,128)S(1)}, u32[]{:S(2)}, u32[]{:S(2)}) %all-to-all-start.3) | async-done | bytes 196640 | tf_op jit(solution)/shard_map/all_to_all | solution.py:421
  179.1 0.7 unpack.1
  (21 shorter events, 0.6 us)
Async XLA Ops:
  0.6 4.5 %collective-permute-start = (bf16[256,128]{1,0:T(8,128)(2,1)}, bf16[256,128]{1,0:T(8,128)(2,1)S(1)}, u32[]{:S(2)}, u32[]{:S(2)}) collective-permute-start(bf16[256,128]{1,0:T(8,128)(2,1)} %bitcast.29), channel_id=1, source_target_pairs={{0,0},{1,256},{256,1},{257,257},{2,2},{3,258},{258,3},{259,259},{4... | collective-permute-start | bytes 196616 | tf_op jit(solution)/shard_map/ppermute | solution.py:36
  5.1 26.4 %collective-permute-start.1 = (bf16[4368,128]{1,0:T(8,128)(2,1)}, bf16[4368,128]{1,0:T(8,128)(2,1)S(1)}, u32[]{:S(2)}, u32[]{:S(2)}) collective-permute-start(bf16[4368,128]{1,0:T(8,128)(2,1)} %pack.1), channel_id=1, source_target_pairs={{0,0},{1,256},{256,1},{257,257},{2,2},{3,258},{258,3},{259,259},{4... | collective-permute-start | bytes 3354632 | tf_op jit(solution)/shard_map/ppermute | solution.py:36
  31.5 22.9 %collective-permute-start.3 = (bf16[4,256,128]{2,1,0:T(8,128)(2,1)S(1)}, bf16[4,256,128]{2,1,0:T(8,128)(2,1)S(1)}, u32[]{:S(2)}, u32[]{:S(2)}) collective-permute-start(bf16[4,256,128]{2,1,0:T(8,128)(2,1)S(1)} %bitcast.15), channel_id=1, source_target_pairs={{0,16},{16,32},{32,48},{48,64},{64,80},{80,96},{96,112},{112,128},... | collective-permute-start | bytes 786440 | tf_op jit(solution)/shard_map/ppermute | solution.py:28
  34.5 20.0 %collective-permute-start.2 = (bf16[4,256,128]{2,1,0:T(8,128)(2,1)S(1)}, bf16[4,256,128]{2,1,0:T(8,128)(2,1)S(1)}, u32[]{:S(2)}, u32[]{:S(2)}) collective-permute-start(bf16[4,256,128]{2,1,0:T(8,128)(2,1)S(1)} %bitcast.16), channel_id=1, source_target_pairs={{0,240},{16,0},{32,16},{48,32},{64,48},{80,64},{96,80},{112,96},{1... | collective-permute-start | bytes 786440 | tf_op jit(solution)/shard_map/ppermute | solution.py:28
  37.4 11.0 %collective-permute-start.5 = (bf16[2,256,128]{2,1,0:T(8,128)(2,1)S(1)}, bf16[2,256,128]{2,1,0:T(8,128)(2,1)S(1)}, u32[]{:S(2)}, u32[]{:S(2)}) collective-permute-start(bf16[2,256,128]{2,1,0:T(8,128)(2,1)S(1)} %get-tuple-element.42), channel_id=1, source_target_pairs={{0,32},{16,48},{32,64},{48,80},{64,96},{80,112},{96,128},{112,144}... | collective-permute-start | bytes 393224 | tf_op jit(solution)/shard_map/ppermute | solution.py:28
  43.6 10.9 %collective-permute-start.4 = (bf16[2,256,128]{2,1,0:T(8,128)(2,1)S(1)}, bf16[2,256,128]{2,1,0:T(8,128)(2,1)S(1)}, u32[]{:S(2)}, u32[]{:S(2)}) collective-permute-start(bf16[2,256,128]{2,1,0:T(8,128)(2,1)S(1)} %get-tuple-element.43), channel_id=1, source_target_pairs={{0,224},{16,240},{32,0},{48,16},{64,32},{80,48},{96,64},{112,80},{... | collective-permute-start | bytes 393224 | tf_op jit(solution)/shard_map/ppermute | solution.py:28
  54.5 4.6 %collective-permute-start.6 = (bf16[32,128,128]{2,1,0:T(8,128)(2,1)S(1)}, bf16[32,128,128]{2,1,0:T(8,128)(2,1)S(1)}, u32[]{:S(2)}, u32[]{:S(2)}) collective-permute-start(bf16[32,128,128]{2,1,0:T(8,128)(2,1)S(1)} %window.1.near), channel_id=1, source_target_pairs={{0,1},{1,0},{2,3},{3,2},{4,5},{5,4},{6,7},{7,6},{8,9},{9,8},{10,11... | collective-permute-start | bytes 3145736 | tf_op jit(solution)/shard_map/ppermute | solution.py:32
  61.8 8.0 %copy-start.2 = (bf16[128,172]{0,1:T(8,128)(2,1)S(1)}, bf16[128,172]{0,1:T(8,128)(2,1)}, u32[]{:S(2)}) copy-start(bf16[128,172]{0,1:T(8,128)(2,1)} %param.17) | copy-start | bytes 132100
  61.8 25.6 %copy-start = (bf16[128,128]{1,0:T(8,128)(2,1)S(1)}, bf16[128,128]{1,0:T(8,128)(2,1)}, u32[]{:S(2)}) copy-start(bf16[128,128]{1,0:T(8,128)(2,1)} %weight.1) | copy-start | bytes 98308
  61.8 25.6 %copy-start.1 = (f32[172]{0:T(256)S(1)}, f32[172]{0:T(256)}, u32[]{:S(2)}) copy-start(f32[172]{0:T(256)} %param.18) | copy-start | bytes 2068
  61.8 25.6 %all-to-all-start = ((bf16[16,256,128]{2,1,0:T(8,128)(2,1)}), bf16[16,256,128]{2,1,0:T(8,128)(2,1)S(1)}, u32[]{:S(2)}, u32[]{:S(2)}) async-start(bf16[16,256,128]{2,1,0:T(8,128)(2,1)} %bitcast.11), calls=%async_computation | async-start | bytes 2097152 | tf_op jit(solution)/shard_map/all_to_all | solution.py:368
  113.3 4.6 %collective-permute-start.7 = (bf16[4128,128]{1,0:T(8,128)(2,1)S(1)}, bf16[4128,128]{1,0:T(8,128)(2,1)S(1)}, u32[]{:S(2)}, u32[]{:S(2)}) collective-permute-start(bf16[4128,128]{1,0:T(8,128)(2,1)S(1)} %get-tuple-element.28), channel_id=1, source_target_pairs={{0,1},{1,0},{2,3},{3,2},{4,5},{5,4},{6,7},{7,6},{8,9},{9,8},{10,11... | collective-permute-start | bytes 3170312 | tf_op jit(solution)/shard_map/ppermute | solution.py:32
  118.1 21.5 %collective-permute-start.10 = (bf16[1056,128]{1,0:T(8,128)(2,1)S(1)}, bf16[1056,128]{1,0:T(8,128)(2,1)S(1)}, u32[]{:S(2)}, u32[]{:S(2)}) collective-permute-start(bf16[1056,128]{1,0:T(8,128)(2,1)S(1)} %get-tuple-element.35), channel_id=1, source_target_pairs={{0,16},{16,32},{32,48},{48,64},{64,80},{80,96},{96,112},{112,128},... | collective-permute-start | bytes 811016 | tf_op jit(solution)/shard_map/ppermute | solution.py:28
  120.0 19.6 %collective-permute-start.11 = (bf16[1056,128]{1,0:T(8,128)(2,1)S(1)}, bf16[1056,128]{1,0:T(8,128)(2,1)S(1)}, u32[]{:S(2)}, u32[]{:S(2)}) collective-permute-start(bf16[1056,128]{1,0:T(8,128)(2,1)S(1)} %get-tuple-element.36), channel_id=1, source_target_pairs={{0,240},{16,0},{32,16},{48,32},{64,48},{80,64},{96,80},{112,96},{1... | collective-permute-start | bytes 811016 | tf_op jit(solution)/shard_map/ppermute | solution.py:28
  123.9 10.1 %collective-permute-start.8 = (bf16[544,128]{1,0:T(8,128)(2,1)S(1)}, bf16[544,128]{1,0:T(8,128)(2,1)S(1)}, u32[]{:S(2)}, u32[]{:S(2)}) collective-permute-start(bf16[544,128]{1,0:T(8,128)(2,1)S(1)} %get-tuple-element.33), channel_id=1, source_target_pairs={{0,32},{16,48},{32,64},{48,80},{64,96},{80,112},{96,128},{112,144}... | collective-permute-start | bytes 417800 | tf_op jit(solution)/shard_map/ppermute | solution.py:28
  127.9 11.7 %collective-permute-start.9 = (bf16[544,128]{1,0:T(8,128)(2,1)S(1)}, bf16[544,128]{1,0:T(8,128)(2,1)S(1)}, u32[]{:S(2)}, u32[]{:S(2)}) collective-permute-start(bf16[544,128]{1,0:T(8,128)(2,1)S(1)} %get-tuple-element.34), channel_id=1, source_target_pairs={{0,224},{16,240},{32,0},{48,16},{64,32},{80,48},{96,64},{112,80},{... | collective-permute-start | bytes 417800 | tf_op jit(solution)/shard_map/ppermute | solution.py:28
  167.2 11.8 %all-to-all-start.3 = ((f32[16,24,128]{2,1,0:T(8,128)}), f32[16,24,128]{2,1,0:T(8,128)S(1)}, u32[]{:S(2)}, u32[]{:S(2)}) async-start(f32[16,24,128]{2,1,0:T(8,128)} %total.1), calls=%async_computation.3 | async-start | bytes 393216 | tf_op jit(solution)/shard_map/all_to_all | solution.py:421
  170.8 0.7 collective-permute-start.12

commit v7 on v6

--- a/solution.py
+++ b/solution.py
@@ -92,8 +92,9 @@
     o[28:32] = hb[...]
 
 
-def forward_kernel(ints, packed, near, across, o, xs, acc):
+def forward_kernel(ints, packed, near, across, o, small, xs, acc):
     slots = (packed.shape[0] - PROWS) // TILE - 2
+    small[...] = packed[slots * TILE : packed.shape[0]]
     xs[0:32] = near[...]
     xs[32:64] = across[...]
     acc[...] = jnp.zeros_like(acc)
@@ -162,18 +163,20 @@
     return lax.axis_index("core"), lax.axis_index("k")
 
 
-def dense_kernel(parts, weight, exit_weight, bias, small, sent, wb):
+def dense_kernel(parts, weight, exit_t, bias, small, sent, wb):
     nodes = parts.shape[1]
     total = f32(parts[0])
     for j in range(1, parts.shape[0]):
         total += f32(parts[j])
     agg = bf(total)
     w = weight[...]
-    ew = exit_weight[...]
+    et = exit_t[...]
     pre = jnp.dot(agg, w, preferred_element_type=jnp.float32)
     sig = 1.0 / (1.0 + jnp.exp(-pre))
     act = bf(pre * sig)
-    logits = jnp.dot(act, ew, preferred_element_type=jnp.float32) + bias[...]
+    logits = (
+        lax.dot_general(act, et, NT, preferred_element_type=jnp.float32) + bias[...]
+    )
     expd = jnp.exp(logits)
     probs = expd / jnp.sum(expd, axis=1, keepdims=True)
     ids = f32(lax.broadcasted_iota(jnp.int32, logits.shape, 1))
@@ -182,12 +185,12 @@
     mask = jnp.concatenate([columns[:, 5:6], columns[:, 6:7]], axis=0)
     onehot = f32(labels == ids)
     dlogits = bf(mask * (probs - onehot))
-    dact = f32(small[0:nodes]) + lax.dot_general(
-        dlogits, ew, NT, preferred_element_type=jnp.float32
+    dact = f32(small[0:nodes]) + jnp.dot(
+        dlogits, et, preferred_element_type=jnp.float32
     )
     dpre = bf(dact * sig * (1.0 + pre * (1.0 - sig)))
     dagg = bf(lax.dot_general(dpre, w, NT, preferred_element_type=jnp.float32))
-    classes = ew.shape[1]
+    classes = et.shape[0]
     wb[...] = jnp.zeros_like(wb)
     wb[0:TILE] = lax.dot_general(agg, dpre, TN, preferred_element_type=jnp.float32)
     wb[TILE : TILE + classes] = lax.dot_general(
@@ -356,11 +359,10 @@
 
     top = packed.shape[0] - nodes - PROWS
     ints = packed[top + nodes : top + nodes + 8].astype(jnp.int32)
-    small = packed[top:]
-    partial_value = call(
+    partial_value, small = call(
         forward_kernel,
         "forward_products",
-        out((2 * plane, TILE, hidden)),
+        (out((2 * plane, TILE, hidden)), out((nodes + PROWS, hidden))),
         (ints,),
         (packed, near, across),
         (pltpu.VMEM((64, TILE, hidden), jnp.bfloat16), acc(2 * plane + 1)),
@@ -373,7 +375,7 @@
         "dense",
         out((plane, nodes + WROWS, hidden)),
         (),
-        (parts, weight, exit_weight, exit_bias.reshape(1, classes), small),
+        (parts, weight, exit_weight.T, exit_bias.reshape(1, classes), small),
         (pltpu.VMEM((plane * WUSED + WROWS, hidden), jnp.float32),),
     )
     got = lax.all_to_all(sent, PLANE, 0, 0, tiled=True)

time: 181 us -> 178 us (0.983)
  blocking collectives: 74.1 us -> 98.1 us
  waiting for transfers between devices: 48.1 us -> 30.7 us
  starting transfers between devices: 45.9 us -> 37.9 us
    all_to_all x0 -> x1, blocking collectives: none -> 25.2 us  [local(): lax.all_to_all(partial_value.reshape(plane, nodes, hidden), PLANE, 0, 0,...]
    all_to_all x1 -> x0, waiting for transfers between devices: 17.5 us -> none  [local(): lax.all_to_all(partial_value.reshape(plane, nodes, hidden), PLANE, 0, 0,...]
    all_to_all x1 -> x0, starting transfers between devices: 7.98 us -> none  [local(): lax.all_to_all(partial_value.reshape(plane, nodes, hidden), PLANE, 0, 0,...]
  transfers between devices with their start and end apart: 15 -> 14, of which waited for: 8 -> 7; matrix products, arithmetic and copies ran while one was open for 0% -> 0% of each run, Pallas kernels for 1% -> 1%
where the time goes in v7:
time: 178 us; the launch traced here: 177 us
  blocking collectives  98.1 us (55%)
  starting transfers between devices  37.9 us (21%)
  waiting for transfers between devices  30.7 us (17%)
  Pallas kernels  8.97 us (5%)
    all_to_all x1, blocking collectives, local(): last = lax.all_to_all(joined, 'q', 0, 0, tiled=True)  26.8 us
    ppermute x8, starting transfers between devices, shift(): return lax.ppermute(v, RING, [(z, (z + d) % Z) for z in range(Z)])  26.4 us
    all_to_all x1, blocking collectives, local(): lax.all_to_all(partial_value.reshape(plane, nodes, hidden), PLANE, 0, 0,...  25.2 us
    all_gather x1, blocking collectives, local(): far = lax.all_gather(feats, 'q', axis=0)  24.6 us
    all_to_all x1, blocking collectives, local(): got = lax.all_to_all(sent, PLANE, 0, 0, tiled=True)  21.5 us
    ppermute x8, waiting for transfers between devices, shift(): return lax.ppermute(v, RING, [(z, (z + d) % Z) for z in range(Z)])  17.9 us
    all_to_all x1, waiting for transfers between devices, local(): wall = lax.all_to_all(wsum, PLANE, 0, 0, tiled=True)  7.58 us
    pallas_call x9, Pallas kernels, call(): pl.pallas_call(kernel, out_shape=outs, in_specs=[smem()] * len(scalars) +...  6.65 us
  transfers between devices with their start and end apart: 14, of which 7 were waited for; matrix products, arithmetic and copies ran while one was open for 0% of the time, Pallas kernels for 1%

profile of v7, /device:TPU:64, one launch (start us, length us, event | category | flops | bytes accessed | tf_op | source)
XLA Modules:
  0.0 177.2 jit_solution(13888192883319521029)
XLA Ops:
  0.6 1.5 collective-permute-start
  2.8 2.3 %pack.1 = bf16[4368,128]{1,0:T(8,128)(2,1)} custom-call(bf16[4096,128]{1,0:T(8,128)(2,1)} %bitcast.27, bf16[256,128]{1,0:T(8,128)(2,1)} %bitcast.28, s32[1,32]{1,0:T(1,128)} %bitcast.29, s32[1,32]{1,0:T(1,128)} %bitcast.30, s32[1,1]{1,0:T(1,128)S(6)} %copy.15.count, s32[1,256]{1,0:T(1,128)} %labels.1, s32[1,256]{1,0:T(1,128)} %mask.1), custom_call_target="tpu_custom_call" | custom-call | tf_op jit(solution)/shard_map/pack/pallas_call | solution.py:150
  5.1 1.9 %collective-permute-start.1 = (bf16[4368,128]{1,0:T(8,128)(2,1)}, bf16[4368,128]{1,0:T(8,128)(2,1)S(1)}, u32[]{:S(2)}, u32[]{:S(2)}) collective-permute-start(bf16[4368,128]{1,0:T(8,128)(2,1)} %pack.1), channel_id=1, source_target_pairs={{0,0},{1,256},{256,1},{257,257},{2,2},{3,258},{258,3},{259,259},{4... | collective-permute-start | bytes 3354632 | tf_op jit(solution)/shard_map/ppermute | solution.py:36
  7.0 24.6 %all-gather = bf16[1024,128]{1,0:T(8,128)(2,1)S(1)} all-gather(bf16[256,128]{1,0:T(8,128)(2,1)S(1)} %collective-permute-done), channel_id=2, replica_groups=mesh['x'=2,'q'=4,'k'=4,'h'=2,'y'=4,'core'=2] {'q'}, dimensions={0}, use_global_device_ids=true | all-gather | bytes 327680 | tf_op jit(solution)/shard_map/all_gather | solution.py:345
  31.6 2.9 %collective-permute-start.3 = (bf16[4,256,128]{2,1,0:T(8,128)(2,1)S(1)}, bf16[4,256,128]{2,1,0:T(8,128)(2,1)S(1)}, u32[]{:S(2)}, u32[]{:S(2)}) collective-permute-start(bf16[4,256,128]{2,1,0:T(8,128)(2,1)S(1)} %bitcast.16), channel_id=1, source_target_pairs={{0,16},{16,32},{32,48},{48,64},{64,80},{80,96},{96,112},{112,128},... | collective-permute-start | bytes 786440 | tf_op jit(solution)/shard_map/ppermute | solution.py:28
  34.5 2.9 %collective-permute-start.2 = (bf16[4,256,128]{2,1,0:T(8,128)(2,1)S(1)}, bf16[4,256,128]{2,1,0:T(8,128)(2,1)S(1)}, u32[]{:S(2)}, u32[]{:S(2)}) collective-permute-start(bf16[4,256,128]{2,1,0:T(8,128)(2,1)S(1)} %bitcast.17), channel_id=1, source_target_pairs={{0,240},{16,0},{32,16},{48,32},{64,48},{80,64},{96,80},{112,96},{1... | collective-permute-start | bytes 786440 | tf_op jit(solution)/shard_map/ppermute | solution.py:28
  37.5 6.1 %collective-permute-start.5 = (bf16[2,256,128]{2,1,0:T(8,128)(2,1)S(1)}, bf16[2,256,128]{2,1,0:T(8,128)(2,1)S(1)}, u32[]{:S(2)}, u32[]{:S(2)}) collective-permute-start(bf16[2,256,128]{2,1,0:T(8,128)(2,1)S(1)} %get-tuple-element.46), channel_id=1, source_target_pairs={{0,32},{16,48},{32,64},{48,80},{64,96},{80,112},{96,128},{112,144}... | collective-permute-start | bytes 393224 | tf_op jit(solution)/shard_map/ppermute | solution.py:28
  43.6 1.9 %collective-permute-start.4 = (bf16[2,256,128]{2,1,0:T(8,128)(2,1)S(1)}, bf16[2,256,128]{2,1,0:T(8,128)(2,1)S(1)}, u32[]{:S(2)}, u32[]{:S(2)}) collective-permute-start(bf16[2,256,128]{2,1,0:T(8,128)(2,1)S(1)} %get-tuple-element.47), channel_id=1, source_target_pairs={{0,224},{16,240},{32,0},{48,16},{64,32},{80,48},{96,64},{112,80},{... | collective-permute-start | bytes 393224 | tf_op jit(solution)/shard_map/ppermute | solution.py:28
  45.5 3.9 %collective-permute-done.5 = bf16[2,256,128]{2,1,0:T(8,128)(2,1)S(1)} collective-permute-done((bf16[2,256,128]{2,1,0:T(8,128)(2,1)S(1)}, bf16[2,256,128]{2,1,0:T(8,128)(2,1)S(1)}, u32[]{:S(2)}, u32[]{:S(2)}) %collective-permute-start.5) | collective-permute-done | bytes 131104 | tf_op jit(solution)/shard_map/ppermute | solution.py:28
  49.5 5.1 %collective-permute-done.4 = bf16[2,256,128]{2,1,0:T(8,128)(2,1)S(1)} collective-permute-done((bf16[2,256,128]{2,1,0:T(8,128)(2,1)S(1)}, bf16[2,256,128]{2,1,0:T(8,128)(2,1)S(1)}, u32[]{:S(2)}, u32[]{:S(2)}) %collective-permute-start.4) | collective-permute-done | bytes 131104 | tf_op jit(solution)/shard_map/ppermute | solution.py:28
  54.6 1.9 %collective-permute-start.6 = (bf16[32,128,128]{2,1,0:T(8,128)(2,1)S(1)}, bf16[32,128,128]{2,1,0:T(8,128)(2,1)S(1)}, u32[]{:S(2)}, u32[]{:S(2)}) collective-permute-start(bf16[32,128,128]{2,1,0:T(8,128)(2,1)S(1)} %window.1.near), channel_id=1, source_target_pairs={{0,1},{1,0},{2,3},{3,2},{4,5},{5,4},{6,7},{7,6},{8,9},{9,8},{10,11... | collective-permute-start | bytes 3145736 | tf_op jit(solution)/shard_map/ppermute | solution.py:32
  56.5 2.6 %collective-permute-done.6.across = bf16[32,128,128]{2,1,0:T(8,128)(2,1)S(1)} collective-permute-done((bf16[32,128,128]{2,1,0:T(8,128)(2,1)S(1)}, bf16[32,128,128]{2,1,0:T(8,128)(2,1)S(1)}, u32[]{:S(2)}, u32[]{:S(2)}) %collective-permute-start.6) | collective-permute-done | bytes 1048608 | tf_op jit(solution)/shard_map/ppermute | solution.py:32
  59.2 1.8 forward_products.1
  61.0 25.2 %all_to_all.20.parts = bf16[16,256,128]{2,1,0:T(8,128)(2,1)S(1)} all-to-all(bf16[16,256,128]{2,1,0:T(8,128)(2,1)S(1)} %bitcast.20), channel_id=1, replica_groups=mesh['x'=2,'q'=4,'k'=4,'h'=2,'y'=4,'core'=2] {'h','y','x'}, dimensions={0} | all-to-all | bytes 2097152 | tf_op jit(solution)/shard_map/all_to_all | solution.py:370
  86.1 0.8 dense.1
  87.0 21.5 %all_to_all.21.g = bf16[16,288,128]{2,1,0:T(8,128)(2,1)S(1)} all-to-all(bf16[16,288,128]{2,1,0:T(8,128)(2,1)S(1)} %dense.1), channel_id=1, replica_groups=mesh['x'=2,'q'=4,'k'=4,'h'=2,'y'=4,'core'=2] {'h','y','x'}, dimensions={0} | all-to-all | bytes 2359296 | tf_op jit(solution)/shard_map/all_to_all | solution.py:381
  108.5 2.2 %backward_products.1 = (bf16[4128,128]{1,0:T(8,128)(2,1)S(1)}, bf16[8,128,128]{2,1,0:T(8,128)(2,1)S(1)}, bf16[8,128,128]{2,1,0:T(8,128)(2,1)S(1)}, bf16[8,128,12...) custom-call(s32[8,128]{1,0:T(8,128)S(1)} %slice_convert_fusion.ints, ...), custom_call_target="tpu_custom_call" | custom-call | tf_op jit(solution)/shard_map/backward_products/pallas_call | solution.py:72
  110.7 1.9 %collective-permute-start.7 = (bf16[4128,128]{1,0:T(8,128)(2,1)S(1)}, bf16[4128,128]{1,0:T(8,128)(2,1)S(1)}, u32[]{:S(2)}, u32[]{:S(2)}) collective-permute-start(bf16[4128,128]{1,0:T(8,128)(2,1)S(1)} %get-tuple-element.32), channel_id=1, source_target_pairs={{0,1},{1,0},{2,3},{3,2},{4,5},{5,4},{6,7},{7,6},{8,9},{9,8},{10,11... | collective-permute-start | bytes 3170312 | tf_op jit(solution)/shard_map/ppermute | solution.py:32
  112.6 2.6 %collective-permute-done.7.xs = bf16[4128,128]{1,0:T(8,128)(2,1)S(1)} collective-permute-done((bf16[4128,128]{1,0:T(8,128)(2,1)S(1)}, bf16[4128,128]{1,0:T(8,128)(2,1)S(1)}, u32[]{:S(2)}, u32[]{:S(2)}) %collective-permute-start.7) | collective-permute-done | bytes 1056800 | tf_op jit(solution)/shard_map/ppermute | solution.py:32
  115.3 0.2 fold.1
  115.5 1.9 %collective-permute-start.10 = (bf16[1056,128]{1,0:T(8,128)(2,1)S(1)}, bf16[1056,128]{1,0:T(8,128)(2,1)S(1)}, u32[]{:S(2)}, u32[]{:S(2)}) collective-permute-start(bf16[1056,128]{1,0:T(8,128)(2,1)S(1)} %get-tuple-element.39), channel_id=1, source_target_pairs={{0,16},{16,32},{32,48},{48,64},{64,80},{80,96},{96,112},{112,128},... | collective-permute-start | bytes 811016 | tf_op jit(solution)/shard_map/ppermute | solution.py:28
  117.4 3.9 %collective-permute-start.11 = (bf16[1056,128]{1,0:T(8,128)(2,1)S(1)}, bf16[1056,128]{1,0:T(8,128)(2,1)S(1)}, u32[]{:S(2)}, u32[]{:S(2)}) collective-permute-start(bf16[1056,128]{1,0:T(8,128)(2,1)S(1)} %get-tuple-element.40), channel_id=1, source_target_pairs={{0,240},{16,0},{32,16},{48,32},{64,48},{80,64},{96,80},{112,96},{1... | collective-permute-start | bytes 811016 | tf_op jit(solution)/shard_map/ppermute | solution.py:28
  121.3 4.0 %collective-permute-start.8 = (bf16[544,128]{1,0:T(8,128)(2,1)S(1)}, bf16[544,128]{1,0:T(8,128)(2,1)S(1)}, u32[]{:S(2)}, u32[]{:S(2)}) collective-permute-start(bf16[544,128]{1,0:T(8,128)(2,1)S(1)} %get-tuple-element.37), channel_id=1, source_target_pairs={{0,32},{16,48},{32,64},{48,80},{64,96},{80,112},{96,128},{112,144}... | collective-permute-start | bytes 417800 | tf_op jit(solution)/shard_map/ppermute | solution.py:28
  125.3 2.8 %collective-permute-start.9 = (bf16[544,128]{1,0:T(8,128)(2,1)S(1)}, bf16[544,128]{1,0:T(8,128)(2,1)S(1)}, u32[]{:S(2)}, u32[]{:S(2)}) collective-permute-start(bf16[544,128]{1,0:T(8,128)(2,1)S(1)} %get-tuple-element.38), channel_id=1, source_target_pairs={{0,224},{16,240},{32,0},{48,16},{64,32},{80,48},{96,64},{112,80},{... | collective-permute-start | bytes 417800 | tf_op jit(solution)/shard_map/ppermute | solution.py:28
  128.1 3.4 %collective-permute-done.8.ra = bf16[544,128]{1,0:T(8,128)(2,1)S(1)} collective-permute-done((bf16[544,128]{1,0:T(8,128)(2,1)S(1)}, bf16[544,128]{1,0:T(8,128)(2,1)S(1)}, u32[]{:S(2)}, u32[]{:S(2)}) %collective-permute-start.8) | collective-permute-done | bytes 139296 | tf_op jit(solution)/shard_map/ppermute | solution.py:28
  131.5 5.5 %collective-permute-done.9.rb = bf16[544,128]{1,0:T(8,128)(2,1)S(1)} collective-permute-done((bf16[544,128]{1,0:T(8,128)(2,1)S(1)}, bf16[544,128]{1,0:T(8,128)(2,1)S(1)}, u32[]{:S(2)}, u32[]{:S(2)}) %collective-permute-start.9) | collective-permute-done | bytes 139296 | tf_op jit(solution)/shard_map/ppermute | solution.py:28
  137.1 26.8 %all_to_all.22.parts = bf16[4,304,128]{2,1,0:T(8,128)(2,1)S(1)} all-to-all(bf16[4,304,128]{2,1,0:T(8,128)(2,1)S(1)} %join.1), channel_id=1, replica_groups=mesh['x'=2,'q'=4,'k'=4,'h'=2,'y'=4,'core'=2] {'q'}, dimensions={0} | all-to-all | bytes 622592 | tf_op jit(solution)/shard_map/all_to_all | solution.py:419
  164.0 0.7 total.1
  164.7 3.5 %all-to-all-start.3 = ((f32[16,24,128]{2,1,0:T(8,128)}), f32[16,24,128]{2,1,0:T(8,128)S(1)}, u32[]{:S(2)}, u32[]{:S(2)}) async-start(f32[16,24,128]{2,1,0:T(8,128)} %total.1), calls=%async_computation.3 | async-start | bytes 393216 | tf_op jit(solution)/shard_map/all_to_all | solution.py:423
  168.2 0.7 collective-permute-start.12
  168.9 7.6 %all-to-all-done.3.wall = f32[16,24,128]{2,1,0:T(8,128)S(1)} async-done(((f32[16,24,128]{2,1,0:T(8,128)}), f32[16,24,128]{2,1,0:T(8,128)S(1)}, u32[]{:S(2)}, u32[]{:S(2)}) %all-to-all-start.3) | async-done | bytes 196640 | tf_op jit(solution)/shard_map/all_to_all | solution.py:423
  176.5 0.7 unpack.1
  (18 shorter events, 0.3 us)
Async XLA Ops:
  0.6 4.5 %collective-permute-start = (bf16[256,128]{1,0:T(8,128)(2,1)}, bf16[256,128]{1,0:T(8,128)(2,1)S(1)}, u32[]{:S(2)}, u32[]{:S(2)}) collective-permute-start(bf16[256,128]{1,0:T(8,128)(2,1)} %bitcast.32), channel_id=1, source_target_pairs={{0,0},{1,256},{256,1},{257,257},{2,2},{3,258},{258,3},{259,259},{4... | collective-permute-start | bytes 196616 | tf_op jit(solution)/shard_map/ppermute | solution.py:36
  5.1 26.5 %collective-permute-start.1 = (bf16[4368,128]{1,0:T(8,128)(2,1)}, bf16[4368,128]{1,0:T(8,128)(2,1)S(1)}, u32[]{:S(2)}, u32[]{:S(2)}) collective-permute-start(bf16[4368,128]{1,0:T(8,128)(2,1)} %pack.1), channel_id=1, source_target_pairs={{0,0},{1,256},{256,1},{257,257},{2,2},{3,258},{258,3},{259,259},{4... | collective-permute-start | bytes 3354632 | tf_op jit(solution)/shard_map/ppermute | solution.py:36
  31.6 22.9 %collective-permute-start.3 = (bf16[4,256,128]{2,1,0:T(8,128)(2,1)S(1)}, bf16[4,256,128]{2,1,0:T(8,128)(2,1)S(1)}, u32[]{:S(2)}, u32[]{:S(2)}) collective-permute-start(bf16[4,256,128]{2,1,0:T(8,128)(2,1)S(1)} %bitcast.16), channel_id=1, source_target_pairs={{0,16},{16,32},{32,48},{48,64},{64,80},{80,96},{96,112},{112,128},... | collective-permute-start | bytes 786440 | tf_op jit(solution)/shard_map/ppermute | solution.py:28
  34.5 20.0 %collective-permute-start.2 = (bf16[4,256,128]{2,1,0:T(8,128)(2,1)S(1)}, bf16[4,256,128]{2,1,0:T(8,128)(2,1)S(1)}, u32[]{:S(2)}, u32[]{:S(2)}) collective-permute-start(bf16[4,256,128]{2,1,0:T(8,128)(2,1)S(1)} %bitcast.17), channel_id=1, source_target_pairs={{0,240},{16,0},{32,16},{48,32},{64,48},{80,64},{96,80},{112,96},{1... | collective-permute-start | bytes 786440 | tf_op jit(solution)/shard_map/ppermute | solution.py:28
  37.5 12.0 %collective-permute-start.5 = (bf16[2,256,128]{2,1,0:T(8,128)(2,1)S(1)}, bf16[2,256,128]{2,1,0:T(8,128)(2,1)S(1)}, u32[]{:S(2)}, u32[]{:S(2)}) collective-permute-start(bf16[2,256,128]{2,1,0:T(8,128)(2,1)S(1)} %get-tuple-element.46), channel_id=1, source_target_pairs={{0,32},{16,48},{32,64},{48,80},{64,96},{80,112},{96,128},{112,144}... | collective-permute-start | bytes 393224 | tf_op jit(solution)/shard_map/ppermute | solution.py:28
  43.6 10.9 %collective-permute-start.4 = (bf16[2,256,128]{2,1,0:T(8,128)(2,1)S(1)}, bf16[2,256,128]{2,1,0:T(8,128)(2,1)S(1)}, u32[]{:S(2)}, u32[]{:S(2)}) collective-permute-start(bf16[2,256,128]{2,1,0:T(8,128)(2,1)S(1)} %get-tuple-element.47), channel_id=1, source_target_pairs={{0,224},{16,240},{32,0},{48,16},{64,32},{80,48},{96,64},{112,80},{... | collective-permute-start | bytes 393224 | tf_op jit(solution)/shard_map/ppermute | solution.py:28
  54.6 4.6 %collective-permute-start.6 = (bf16[32,128,128]{2,1,0:T(8,128)(2,1)S(1)}, bf16[32,128,128]{2,1,0:T(8,128)(2,1)S(1)}, u32[]{:S(2)}, u32[]{:S(2)}) collective-permute-start(bf16[32,128,128]{2,1,0:T(8,128)(2,1)S(1)} %window.1.near), channel_id=1, source_target_pairs={{0,1},{1,0},{2,3},{3,2},{4,5},{5,4},{6,7},{7,6},{8,9},{9,8},{10,11... | collective-permute-start | bytes 3145736 | tf_op jit(solution)/shard_map/ppermute | solution.py:32
  60.9 25.2 %copy-start = (bf16[128,172]{0,1:T(8,128)(2,1)S(1)}, bf16[128,172]{0,1:T(8,128)(2,1)}, u32[]{:S(2)}) copy-start(bf16[128,172]{0,1:T(8,128)(2,1)} %param.17) | copy-start | bytes 132100
  60.9 25.2 %copy-start.1 = (bf16[128,128]{1,0:T(8,128)(2,1)S(1)}, bf16[128,128]{1,0:T(8,128)(2,1)}, u32[]{:S(2)}) copy-start(bf16[128,128]{1,0:T(8,128)(2,1)} %weight.1) | copy-start | bytes 98308
  60.9 25.2 %copy-start.2 = (f32[172]{0:T(256)S(1)}, f32[172]{0:T(256)}, u32[]{:S(2)}) copy-start(f32[172]{0:T(256)} %param.18) | copy-start | bytes 2068
  110.7 4.6 %collective-permute-start.7 = (bf16[4128,128]{1,0:T(8,128)(2,1)S(1)}, bf16[4128,128]{1,0:T(8,128)(2,1)S(1)}, u32[]{:S(2)}, u32[]{:S(2)}) collective-permute-start(bf16[4128,128]{1,0:T(8,128)(2,1)S(1)} %get-tuple-element.32), channel_id=1, source_target_pairs={{0,1},{1,0},{2,3},{3,2},{4,5},{5,4},{6,7},{7,6},{8,9},{9,8},{10,11... | collective-permute-start | bytes 3170312 | tf_op jit(solution)/shard_map/ppermute | solution.py:32
  115.5 21.5 %collective-permute-start.10 = (bf16[1056,128]{1,0:T(8,128)(2,1)S(1)}, bf16[1056,128]{1,0:T(8,128)(2,1)S(1)}, u32[]{:S(2)}, u32[]{:S(2)}) collective-permute-start(bf16[1056,128]{1,0:T(8,128)(2,1)S(1)} %get-tuple-element.39), channel_id=1, source_target_pairs={{0,16},{16,32},{32,48},{48,64},{64,80},{80,96},{96,112},{112,128},... | collective-permute-start | bytes 811016 | tf_op jit(solution)/shard_map/ppermute | solution.py:28
  117.4 19.6 %collective-permute-start.11 = (bf16[1056,128]{1,0:T(8,128)(2,1)S(1)}, bf16[1056,128]{1,0:T(8,128)(2,1)S(1)}, u32[]{:S(2)}, u32[]{:S(2)}) collective-permute-start(bf16[1056,128]{1,0:T(8,128)(2,1)S(1)} %get-tuple-element.40), channel_id=1, source_target_pairs={{0,240},{16,0},{32,16},{48,32},{64,48},{80,64},{96,80},{112,96},{1... | collective-permute-start | bytes 811016 | tf_op jit(solution)/shard_map/ppermute | solution.py:28
  121.3 10.2 %collective-permute-start.8 = (bf16[544,128]{1,0:T(8,128)(2,1)S(1)}, bf16[544,128]{1,0:T(8,128)(2,1)S(1)}, u32[]{:S(2)}, u32[]{:S(2)}) collective-permute-start(bf16[544,128]{1,0:T(8,128)(2,1)S(1)} %get-tuple-element.37), channel_id=1, source_target_pairs={{0,32},{16,48},{32,64},{48,80},{64,96},{80,112},{96,128},{112,144}... | collective-permute-start | bytes 417800 | tf_op jit(solution)/shard_map/ppermute | solution.py:28
  125.3 11.7 %collective-permute-start.9 = (bf16[544,128]{1,0:T(8,128)(2,1)S(1)}, bf16[544,128]{1,0:T(8,128)(2,1)S(1)}, u32[]{:S(2)}, u32[]{:S(2)}) collective-permute-start(bf16[544,128]{1,0:T(8,128)(2,1)S(1)} %get-tuple-element.38), channel_id=1, source_target_pairs={{0,224},{16,240},{32,0},{48,16},{64,32},{80,48},{96,64},{112,80},{... | collective-permute-start | bytes 417800 | tf_op jit(solution)/shard_map/ppermute | solution.py:28
  164.7 11.8 %all-to-all-start.3 = ((f32[16,24,128]{2,1,0:T(8,128)}), f32[16,24,128]{2,1,0:T(8,128)S(1)}, u32[]{:S(2)}, u32[]{:S(2)}) async-start(f32[16,24,128]{2,1,0:T(8,128)} %total.1), calls=%async_computation.3 | async-start | bytes 393216 | tf_op jit(solution)/shard_map/all_to_all | solution.py:423
  168.2 0.7 collective-permute-start.12

commit v8 on v7

--- a/solution.py
+++ b/solution.py
@@ -280,6 +280,8 @@
     for j in range(1, FAR):
         other += f32(parts[(first + j) % FAR, both])
     total = total[0:WUSED] + other[WUSED : 2 * WUSED]
+    fill = jnp.zeros((WROWS - WUSED, TILE), jnp.float32)
+    total = bf(jnp.concatenate([total, fill], axis=0))
     for j in range(w.shape[0]):
         w[j] = total
 
@@ -295,7 +297,7 @@
 def unpack_kernel(scale, wall, grad, o, layer, exit_t, bias, wb):
     o[...] = grad[...]
     for j in range(wall.shape[0]):
-        wb[j * WUSED : (j + 1) * WUSED] = wall[j] * scale
+        wb[j * WUSED : (j + 1) * WUSED] = f32(wall[j])[0:WUSED] * scale
     classes = exit_t.shape[0]
     layer[...] = wb[0:TILE]
     exit_t[...] = wb[TILE : TILE + classes]
@@ -418,7 +420,7 @@
     )
     last = lax.all_to_all(joined, "q", 0, 0, tiled=True)
     wsum = call(
-        total_kernel, "total", out((plane, WUSED, hidden), jnp.float32), (), (last,)
+        total_kernel, "total", out((plane, WROWS, hidden)), (), (last,)
     )
     wall = lax.all_to_all(wsum, PLANE, 0, 0, tiled=True)
     grad_input = swap(call(finish_kernel, "finish", out((nodes, hidden)), (), (last,)))

time: 178 us -> 178 us (level)
  no operation moved by 1% of the time
where the time goes in v8:
time: 178 us; the launch traced here: 177 us
  blocking collectives  98.1 us (55%)
  starting transfers between devices  37.9 us (21%)
  waiting for transfers between devices  30.4 us (17%)
  Pallas kernels  8.95 us (5%)
    all_to_all x1, blocking collectives, local(): last = lax.all_to_all(joined, 'q', 0, 0, tiled=True)  26.9 us
    ppermute x8, starting transfers between devices, shift(): return lax.ppermute(v, RING, [(z, (z + d) % Z) for z in range(Z)])  26.4 us
    all_to_all x1, blocking collectives, local(): lax.all_to_all(partial_value.reshape(plane, nodes, hidden), PLANE, 0, 0,...  25.2 us
    all_gather x1, blocking collectives, local(): far = lax.all_gather(feats, 'q', axis=0)  24.6 us
    all_to_all x1, blocking collectives, local(): got = lax.all_to_all(sent, PLANE, 0, 0, tiled=True)  21.5 us
    ppermute x8, waiting for transfers between devices, shift(): return lax.ppermute(v, RING, [(z, (z + d) % Z) for z in range(Z)])  17.9 us
    all_to_all x1, waiting for transfers between devices, local(): wall = lax.all_to_all(wsum, PLANE, 0, 0, tiled=True)  7.22 us
    pallas_call x9, Pallas kernels, call(): pl.pallas_call(kernel, out_shape=outs, in_specs=[smem()] * len(scalars) +...  6.62 us
  transfers between devices with their start and end apart: 14, of which 7 were waited for; matrix products, arithmetic and copies ran while one was open for 0% of the time, Pallas kernels for 1%

profile of v8, /device:TPU:64, one launch (start us, length us, event | category | flops | bytes accessed | tf_op | source)
XLA Modules:
  0.0 176.8 jit_solution(15403214085833245245)
XLA Ops:
  0.6 1.5 collective-permute-start
  2.8 2.3 %pack.1 = bf16[4368,128]{1,0:T(8,128)(2,1)} custom-call(bf16[4096,128]{1,0:T(8,128)(2,1)} %bitcast.27, bf16[256,128]{1,0:T(8,128)(2,1)} %bitcast.28, s32[1,32]{1,0:T(1,128)} %bitcast.29, s32[1,32]{1,0:T(1,128)} %bitcast.30, s32[1,1]{1,0:T(1,128)S(6)} %copy.15.count, s32[1,256]{1,0:T(1,128)} %labels.1, s32[1,256]{1,0:T(1,128)} %mask.1), custom_call_target="tpu_custom_call" | custom-call | tf_op jit(solution)/shard_map/pack/pallas_call | solution.py:150
  5.1 1.9 %collective-permute-start.1 = (bf16[4368,128]{1,0:T(8,128)(2,1)}, bf16[4368,128]{1,0:T(8,128)(2,1)S(1)}, u32[]{:S(2)}, u32[]{:S(2)}) collective-permute-start(bf16[4368,128]{1,0:T(8,128)(2,1)} %pack.1), channel_id=1, source_target_pairs={{0,0},{1,256},{256,1},{257,257},{2,2},{3,258},{258,3},{259,259},{4... | collective-permute-start | bytes 3354632 | tf_op jit(solution)/shard_map/ppermute | solution.py:36
  7.0 24.6 %all-gather = bf16[1024,128]{1,0:T(8,128)(2,1)S(1)} all-gather(bf16[256,128]{1,0:T(8,128)(2,1)S(1)} %collective-permute-done), channel_id=2, replica_groups=mesh['x'=2,'q'=4,'k'=4,'h'=2,'y'=4,'core'=2] {'q'}, dimensions={0}, use_global_device_ids=true | all-gather | bytes 327680 | tf_op jit(solution)/shard_map/all_gather | solution.py:347
  31.6 2.9 %collective-permute-start.3 = (bf16[4,256,128]{2,1,0:T(8,128)(2,1)S(1)}, bf16[4,256,128]{2,1,0:T(8,128)(2,1)S(1)}, u32[]{:S(2)}, u32[]{:S(2)}) collective-permute-start(bf16[4,256,128]{2,1,0:T(8,128)(2,1)S(1)} %bitcast.16), channel_id=1, source_target_pairs={{0,16},{16,32},{32,48},{48,64},{64,80},{80,96},{96,112},{112,128},... | collective-permute-start | bytes 786440 | tf_op jit(solution)/shard_map/ppermute | solution.py:28
  34.5 2.9 %collective-permute-start.2 = (bf16[4,256,128]{2,1,0:T(8,128)(2,1)S(1)}, bf16[4,256,128]{2,1,0:T(8,128)(2,1)S(1)}, u32[]{:S(2)}, u32[]{:S(2)}) collective-permute-start(bf16[4,256,128]{2,1,0:T(8,128)(2,1)S(1)} %bitcast.17), channel_id=1, source_target_pairs={{0,240},{16,0},{32,16},{48,32},{64,48},{80,64},{96,80},{112,96},{1... | collective-permute-start | bytes 786440 | tf_op jit(solution)/shard_map/ppermute | solution.py:28
  37.5 6.1 %collective-permute-start.5 = (bf16[2,256,128]{2,1,0:T(8,128)(2,1)S(1)}, bf16[2,256,128]{2,1,0:T(8,128)(2,1)S(1)}, u32[]{:S(2)}, u32[]{:S(2)}) collective-permute-start(bf16[2,256,128]{2,1,0:T(8,128)(2,1)S(1)} %get-tuple-element.46), channel_id=1, source_target_pairs={{0,32},{16,48},{32,64},{48,80},{64,96},{80,112},{96,128},{112,144}... | collective-permute-start | bytes 393224 | tf_op jit(solution)/shard_map/ppermute | solution.py:28
  43.6 1.9 %collective-permute-start.4 = (bf16[2,256,128]{2,1,0:T(8,128)(2,1)S(1)}, bf16[2,256,128]{2,1,0:T(8,128)(2,1)S(1)}, u32[]{:S(2)}, u32[]{:S(2)}) collective-permute-start(bf16[2,256,128]{2,1,0:T(8,128)(2,1)S(1)} %get-tuple-element.47), channel_id=1, source_target_pairs={{0,224},{16,240},{32,0},{48,16},{64,32},{80,48},{96,64},{112,80},{... | collective-permute-start | bytes 393224 | tf_op jit(solution)/shard_map/ppermute | solution.py:28
  45.5 3.9 %collective-permute-done.5 = bf16[2,256,128]{2,1,0:T(8,128)(2,1)S(1)} collective-permute-done((bf16[2,256,128]{2,1,0:T(8,128)(2,1)S(1)}, bf16[2,256,128]{2,1,0:T(8,128)(2,1)S(1)}, u32[]{:S(2)}, u32[]{:S(2)}) %collective-permute-start.5) | collective-permute-done | bytes 131104 | tf_op jit(solution)/shard_map/ppermute | solution.py:28
  49.5 5.1 %collective-permute-done.4 = bf16[2,256,128]{2,1,0:T(8,128)(2,1)S(1)} collective-permute-done((bf16[2,256,128]{2,1,0:T(8,128)(2,1)S(1)}, bf16[2,256,128]{2,1,0:T(8,128)(2,1)S(1)}, u32[]{:S(2)}, u32[]{:S(2)}) %collective-permute-start.4) | collective-permute-done | bytes 131104 | tf_op jit(solution)/shard_map/ppermute | solution.py:28
  54.6 1.9 %collective-permute-start.6 = (bf16[32,128,128]{2,1,0:T(8,128)(2,1)S(1)}, bf16[32,128,128]{2,1,0:T(8,128)(2,1)S(1)}, u32[]{:S(2)}, u32[]{:S(2)}) collective-permute-start(bf16[32,128,128]{2,1,0:T(8,128)(2,1)S(1)} %window.1.near), channel_id=1, source_target_pairs={{0,1},{1,0},{2,3},{3,2},{4,5},{5,4},{6,7},{7,6},{8,9},{9,8},{10,11... | collective-permute-start | bytes 3145736 | tf_op jit(solution)/shard_map/ppermute | solution.py:32
  56.5 2.6 %collective-permute-done.6.across = bf16[32,128,128]{2,1,0:T(8,128)(2,1)S(1)} collective-permute-done((bf16[32,128,128]{2,1,0:T(8,128)(2,1)S(1)}, bf16[32,128,128]{2,1,0:T(8,128)(2,1)S(1)}, u32[]{:S(2)}, u32[]{:S(2)}) %collective-permute-start.6) | collective-permute-done | bytes 1048608 | tf_op jit(solution)/shard_map/ppermute | solution.py:32
  59.2 1.8 forward_products.1
  61.0 25.2 %all_to_all.20.parts = bf16[16,256,128]{2,1,0:T(8,128)(2,1)S(1)} all-to-all(bf16[16,256,128]{2,1,0:T(8,128)(2,1)S(1)} %bitcast.20), channel_id=1, replica_groups=mesh['x'=2,'q'=4,'k'=4,'h'=2,'y'=4,'core'=2] {'h','y','x'}, dimensions={0} | all-to-all | bytes 2097152 | tf_op jit(solution)/shard_map/all_to_all | solution.py:372
  86.1 0.8 dense.1
  87.0 21.5 %all_to_all.21.g = bf16[16,288,128]{2,1,0:T(8,128)(2,1)S(1)} all-to-all(bf16[16,288,128]{2,1,0:T(8,128)(2,1)S(1)} %dense.1), channel_id=1, replica_groups=mesh['x'=2,'q'=4,'k'=4,'h'=2,'y'=4,'core'=2] {'h','y','x'}, dimensions={0} | all-to-all | bytes 2359296 | tf_op jit(solution)/shard_map/all_to_all | solution.py:383
  108.5 2.2 %backward_products.1 = (bf16[4128,128]{1,0:T(8,128)(2,1)S(1)}, bf16[8,128,128]{2,1,0:T(8,128)(2,1)S(1)}, bf16[8,128,128]{2,1,0:T(8,128)(2,1)S(1)}, bf16[8,128,12...) custom-call(s32[8,128]{1,0:T(8,128)S(1)} %slice_convert_fusion.ints, ...), custom_call_target="tpu_custom_call" | custom-call | tf_op jit(solution)/shard_map/backward_products/pallas_call | solution.py:72
  110.7 1.9 %collective-permute-start.7 = (bf16[4128,128]{1,0:T(8,128)(2,1)S(1)}, bf16[4128,128]{1,0:T(8,128)(2,1)S(1)}, u32[]{:S(2)}, u32[]{:S(2)}) collective-permute-start(bf16[4128,128]{1,0:T(8,128)(2,1)S(1)} %get-tuple-element.32), channel_id=1, source_target_pairs={{0,1},{1,0},{2,3},{3,2},{4,5},{5,4},{6,7},{7,6},{8,9},{9,8},{10,11... | collective-permute-start | bytes 3170312 | tf_op jit(solution)/shard_map/ppermute | solution.py:32
  112.6 2.6 %collective-permute-done.7.xs = bf16[4128,128]{1,0:T(8,128)(2,1)S(1)} collective-permute-done((bf16[4128,128]{1,0:T(8,128)(2,1)S(1)}, bf16[4128,128]{1,0:T(8,128)(2,1)S(1)}, u32[]{:S(2)}, u32[]{:S(2)}) %collective-permute-start.7) | collective-permute-done | bytes 1056800 | tf_op jit(solution)/shard_map/ppermute | solution.py:32
  115.3 0.2 fold.1
  115.5 1.9 %collective-permute-start.10 = (bf16[1056,128]{1,0:T(8,128)(2,1)S(1)}, bf16[1056,128]{1,0:T(8,128)(2,1)S(1)}, u32[]{:S(2)}, u32[]{:S(2)}) collective-permute-start(bf16[1056,128]{1,0:T(8,128)(2,1)S(1)} %get-tuple-element.39), channel_id=1, source_target_pairs={{0,16},{16,32},{32,48},{48,64},{64,80},{80,96},{96,112},{112,128},... | collective-permute-start | bytes 811016 | tf_op jit(solution)/shard_map/ppermute | solution.py:28
  117.4 3.9 %collective-permute-start.11 = (bf16[1056,128]{1,0:T(8,128)(2,1)S(1)}, bf16[1056,128]{1,0:T(8,128)(2,1)S(1)}, u32[]{:S(2)}, u32[]{:S(2)}) collective-permute-start(bf16[1056,128]{1,0:T(8,128)(2,1)S(1)} %get-tuple-element.40), channel_id=1, source_target_pairs={{0,240},{16,0},{32,16},{48,32},{64,48},{80,64},{96,80},{112,96},{1... | collective-permute-start | bytes 811016 | tf_op jit(solution)/shard_map/ppermute | solution.py:28
  121.3 4.0 %collective-permute-start.8 = (bf16[544,128]{1,0:T(8,128)(2,1)S(1)}, bf16[544,128]{1,0:T(8,128)(2,1)S(1)}, u32[]{:S(2)}, u32[]{:S(2)}) collective-permute-start(bf16[544,128]{1,0:T(8,128)(2,1)S(1)} %get-tuple-element.37), channel_id=1, source_target_pairs={{0,32},{16,48},{32,64},{48,80},{64,96},{80,112},{96,128},{112,144}... | collective-permute-start | bytes 417800 | tf_op jit(solution)/shard_map/ppermute | solution.py:28
  125.3 2.8 %collective-permute-start.9 = (bf16[544,128]{1,0:T(8,128)(2,1)S(1)}, bf16[544,128]{1,0:T(8,128)(2,1)S(1)}, u32[]{:S(2)}, u32[]{:S(2)}) collective-permute-start(bf16[544,128]{1,0:T(8,128)(2,1)S(1)} %get-tuple-element.38), channel_id=1, source_target_pairs={{0,224},{16,240},{32,0},{48,16},{64,32},{80,48},{96,64},{112,80},{... | collective-permute-start | bytes 417800 | tf_op jit(solution)/shard_map/ppermute | solution.py:28
  128.1 3.4 %collective-permute-done.8.ra = bf16[544,128]{1,0:T(8,128)(2,1)S(1)} collective-permute-done((bf16[544,128]{1,0:T(8,128)(2,1)S(1)}, bf16[544,128]{1,0:T(8,128)(2,1)S(1)}, u32[]{:S(2)}, u32[]{:S(2)}) %collective-permute-start.8) | collective-permute-done | bytes 139296 | tf_op jit(solution)/shard_map/ppermute | solution.py:28
  131.5 5.5 %collective-permute-done.9.rb = bf16[544,128]{1,0:T(8,128)(2,1)S(1)} collective-permute-done((bf16[544,128]{1,0:T(8,128)(2,1)S(1)}, bf16[544,128]{1,0:T(8,128)(2,1)S(1)}, u32[]{:S(2)}, u32[]{:S(2)}) %collective-permute-start.9) | collective-permute-done | bytes 139296 | tf_op jit(solution)/shard_map/ppermute | solution.py:28
  137.1 26.9 %all_to_all.22.parts = bf16[4,304,128]{2,1,0:T(8,128)(2,1)S(1)} all-to-all(bf16[4,304,128]{2,1,0:T(8,128)(2,1)S(1)} %join.1), channel_id=1, replica_groups=mesh['x'=2,'q'=4,'k'=4,'h'=2,'y'=4,'core'=2] {'q'}, dimensions={0} | all-to-all | bytes 622592 | tf_op jit(solution)/shard_map/all_to_all | solution.py:421
  164.0 0.7 total.1
  164.6 3.5 %all-to-all-start.3 = ((bf16[16,32,128]{2,1,0:T(8,128)(2,1)}), bf16[16,32,128]{2,1,0:T(8,128)(2,1)S(1)}, u32[]{:S(2)}, u32[]{:S(2)}) async-start(bf16[16,32,128]{2,1,0:T(8,128)(2,1)} %total.1), calls=%async_computation.3 | async-start | bytes 262144 | tf_op jit(solution)/shard_map/all_to_all | solution.py:425
  168.2 0.7 collective-permute-start.12
  168.9 7.2 %all-to-all-done.3.wall = bf16[16,32,128]{2,1,0:T(8,128)(2,1)S(1)} async-done(((bf16[16,32,128]{2,1,0:T(8,128)(2,1)}), bf16[16,32,128]{2,1,0:T(8,128)(2,1)S(1)}, u32[]{:S(2)}, u32[]{:S(2)}) %all-to-all-start.3) | async-done | bytes 131104 | tf_op jit(solution)/shard_map/all_to_all | solution.py:425
  176.1 0.7 unpack.1
  (18 shorter events, 0.3 us)
Async XLA Ops:
  0.6 4.5 %collective-permute-start = (bf16[256,128]{1,0:T(8,128)(2,1)}, bf16[256,128]{1,0:T(8,128)(2,1)S(1)}, u32[]{:S(2)}, u32[]{:S(2)}) collective-permute-start(bf16[256,128]{1,0:T(8,128)(2,1)} %bitcast.32), channel_id=1, source_target_pairs={{0,0},{1,256},{256,1},{257,257},{2,2},{3,258},{258,3},{259,259},{4... | collective-permute-start | bytes 196616 | tf_op jit(solution)/shard_map/ppermute | solution.py:36
  5.1 26.5 %collective-permute-start.1 = (bf16[4368,128]{1,0:T(8,128)(2,1)}, bf16[4368,128]{1,0:T(8,128)(2,1)S(1)}, u32[]{:S(2)}, u32[]{:S(2)}) collective-permute-start(bf16[4368,128]{1,0:T(8,128)(2,1)} %pack.1), channel_id=1, source_target_pairs={{0,0},{1,256},{256,1},{257,257},{2,2},{3,258},{258,3},{259,259},{4... | collective-permute-start | bytes 3354632 | tf_op jit(solution)/shard_map/ppermute | solution.py:36
  31.6 22.9 %collective-permute-start.3 = (bf16[4,256,128]{2,1,0:T(8,128)(2,1)S(1)}, bf16[4,256,128]{2,1,0:T(8,128)(2,1)S(1)}, u32[]{:S(2)}, u32[]{:S(2)}) collective-permute-start(bf16[4,256,128]{2,1,0:T(8,128)(2,1)S(1)} %bitcast.16), channel_id=1, source_target_pairs={{0,16},{16,32},{32,48},{48,64},{64,80},{80,96},{96,112},{112,128},... | collective-permute-start | bytes 786440 | tf_op jit(solution)/shard_map/ppermute | solution.py:28
  34.5 20.0 %collective-permute-start.2 = (bf16[4,256,128]{2,1,0:T(8,128)(2,1)S(1)}, bf16[4,256,128]{2,1,0:T(8,128)(2,1)S(1)}, u32[]{:S(2)}, u32[]{:S(2)}) collective-permute-start(bf16[4,256,128]{2,1,0:T(8,128)(2,1)S(1)} %bitcast.17), channel_id=1, source_target_pairs={{0,240},{16,0},{32,16},{48,32},{64,48},{80,64},{96,80},{112,96},{1... | collective-permute-start | bytes 786440 | tf_op jit(solution)/shard_map/ppermute | solution.py:28
  37.5 12.0 %collective-permute-start.5 = (bf16[2,256,128]{2,1,0:T(8,128)(2,1)S(1)}, bf16[2,256,128]{2,1,0:T(8,128)(2,1)S(1)}, u32[]{:S(2)}, u32[]{:S(2)}) collective-permute-start(bf16[2,256,128]{2,1,0:T(8,128)(2,1)S(1)} %get-tuple-element.46), channel_id=1, source_target_pairs={{0,32},{16,48},{32,64},{48,80},{64,96},{80,112},{96,128},{112,144}... | collective-permute-start | bytes 393224 | tf_op jit(solution)/shard_map/ppermute | solution.py:28
  43.6 10.9 %collective-permute-start.4 = (bf16[2,256,128]{2,1,0:T(8,128)(2,1)S(1)}, bf16[2,256,128]{2,1,0:T(8,128)(2,1)S(1)}, u32[]{:S(2)}, u32[]{:S(2)}) collective-permute-start(bf16[2,256,128]{2,1,0:T(8,128)(2,1)S(1)} %get-tuple-element.47), channel_id=1, source_target_pairs={{0,224},{16,240},{32,0},{48,16},{64,32},{80,48},{96,64},{112,80},{... | collective-permute-start | bytes 393224 | tf_op jit(solution)/shard_map/ppermute | solution.py:28
  54.6 4.6 %collective-permute-start.6 = (bf16[32,128,128]{2,1,0:T(8,128)(2,1)S(1)}, bf16[32,128,128]{2,1,0:T(8,128)(2,1)S(1)}, u32[]{:S(2)}, u32[]{:S(2)}) collective-permute-start(bf16[32,128,128]{2,1,0:T(8,128)(2,1)S(1)} %window.1.near), channel_id=1, source_target_pairs={{0,1},{1,0},{2,3},{3,2},{4,5},{5,4},{6,7},{7,6},{8,9},{9,8},{10,11... | collective-permute-start | bytes 3145736 | tf_op jit(solution)/shard_map/ppermute | solution.py:32
  60.9 25.2 %copy-start = (bf16[128,172]{0,1:T(8,128)(2,1)S(1)}, bf16[128,172]{0,1:T(8,128)(2,1)}, u32[]{:S(2)}) copy-start(bf16[128,172]{0,1:T(8,128)(2,1)} %param.17) | copy-start | bytes 132100
  60.9 25.2 %copy-start.1 = (bf16[128,128]{1,0:T(8,128)(2,1)S(1)}, bf16[128,128]{1,0:T(8,128)(2,1)}, u32[]{:S(2)}) copy-start(bf16[128,128]{1,0:T(8,128)(2,1)} %weight.1) | copy-start | bytes 98308
  60.9 25.2 %copy-start.2 = (f32[172]{0:T(256)S(1)}, f32[172]{0:T(256)}, u32[]{:S(2)}) copy-start(f32[172]{0:T(256)} %param.18) | copy-start | bytes 2068
  110.7 4.6 %collective-permute-start.7 = (bf16[4128,128]{1,0:T(8,128)(2,1)S(1)}, bf16[4128,128]{1,0:T(8,128)(2,1)S(1)}, u32[]{:S(2)}, u32[]{:S(2)}) collective-permute-start(bf16[4128,128]{1,0:T(8,128)(2,1)S(1)} %get-tuple-element.32), channel_id=1, source_target_pairs={{0,1},{1,0},{2,3},{3,2},{4,5},{5,4},{6,7},{7,6},{8,9},{9,8},{10,11... | collective-permute-start | bytes 3170312 | tf_op jit(solution)/shard_map/ppermute | solution.py:32
  115.5 21.5 %collective-permute-start.10 = (bf16[1056,128]{1,0:T(8,128)(2,1)S(1)}, bf16[1056,128]{1,0:T(8,128)(2,1)S(1)}, u32[]{:S(2)}, u32[]{:S(2)}) collective-permute-start(bf16[1056,128]{1,0:T(8,128)(2,1)S(1)} %get-tuple-element.39), channel_id=1, source_target_pairs={{0,16},{16,32},{32,48},{48,64},{64,80},{80,96},{96,112},{112,128},... | collective-permute-start | bytes 811016 | tf_op jit(solution)/shard_map/ppermute | solution.py:28
  117.4 19.6 %collective-permute-start.11 = (bf16[1056,128]{1,0:T(8,128)(2,1)S(1)}, bf16[1056,128]{1,0:T(8,128)(2,1)S(1)}, u32[]{:S(2)}, u32[]{:S(2)}) collective-permute-start(bf16[1056,128]{1,0:T(8,128)(2,1)S(1)} %get-tuple-element.40), channel_id=1, source_target_pairs={{0,240},{16,0},{32,16},{48,32},{64,48},{80,64},{96,80},{112,96},{1... | collective-permute-start | bytes 811016 | tf_op jit(solution)/shard_map/ppermute | solution.py:28
  121.3 10.2 %collective-permute-start.8 = (bf16[544,128]{1,0:T(8,128)(2,1)S(1)}, bf16[544,128]{1,0:T(8,128)(2,1)S(1)}, u32[]{:S(2)}, u32[]{:S(2)}) collective-permute-start(bf16[544,128]{1,0:T(8,128)(2,1)S(1)} %get-tuple-element.37), channel_id=1, source_target_pairs={{0,32},{16,48},{32,64},{48,80},{64,96},{80,112},{96,128},{112,144}... | collective-permute-start | bytes 417800 | tf_op jit(solution)/shard_map/ppermute | solution.py:28
  125.3 11.7 %collective-permute-start.9 = (bf16[544,128]{1,0:T(8,128)(2,1)S(1)}, bf16[544,128]{1,0:T(8,128)(2,1)S(1)}, u32[]{:S(2)}, u32[]{:S(2)}) collective-permute-start(bf16[544,128]{1,0:T(8,128)(2,1)S(1)} %get-tuple-element.38), channel_id=1, source_target_pairs={{0,224},{16,240},{32,0},{48,16},{64,32},{80,48},{96,64},{112,80},{... | collective-permute-start | bytes 417800 | tf_op jit(solution)/shard_map/ppermute | solution.py:28
  164.6 11.5 %all-to-all-start.3 = ((bf16[16,32,128]{2,1,0:T(8,128)(2,1)}), bf16[16,32,128]{2,1,0:T(8,128)(2,1)S(1)}, u32[]{:S(2)}, u32[]{:S(2)}) async-start(bf16[16,32,128]{2,1,0:T(8,128)(2,1)} %total.1), calls=%async_computation.3 | async-start | bytes 262144 | tf_op jit(solution)/shard_map/all_to_all | solution.py:425
  168.2 0.7 collective-permute-start.12
